TPU v7x, 128 devices: a whole 4x4x4 slice. The times are simulated.
128 devices in a mesh: gx: 8 (over z, core), gy: 16 (over y, x).
Axes of the slice: x: 4, y: 4, z: 4, core: 2. Of those that a mesh axis runs over, the one named last changes fastest.
Arguments:
- displacement: float32 [3, 24, 384, 384], P(None, 'gx', 'gy'), may hold values from -1.6015 to 1.6015, as said below
- velocity: float32 [3, 24, 384, 384], P(None, 'gx', 'gy'), may hold values from -6 to 6
- energy: float32 [27, 8, 128, 128], P(None, 'gx', 'gy'), may hold values from 0.5 to 18
- mass_weight: float32 [216, 8, 128, 128], P(None, 'gx', 'gy'), may hold values from 0.002 to 0.02
- pinned_flags: int32 [3, 24, 384, 384], P(None, 'gx', 'gy'), may hold values 0 or 1
Outputs:
- acceleration: float32 [3, 24, 384, 384], P(None, 'gx', 'gy')
- velocity_new: float32 [3, 24, 384, 384], P(None, 'gx', 'gy')
- displacement_new: float32 [3, 24, 384, 384], P(None, 'gx', 'gy')
- energy_new: float32 [27, 8, 128, 128], P(None, 'gx', 'gy')
Inputs may be any that keep to these rules, and one draw needn't show every extreme that they name: Every entry of the displacement's derivative along local element coordinates stays below 0.11 in magnitude.
All inputs are finite; a program needn't handle non-finite values. No bound on the sum of `pinned_flags` on one device may be relied on, other than what follows from the above.
Results may differ from a plain program's by a relative error of at most 0.00018.
Values sent between devices are 32-bit elements; how exact they have to be, the bound alone decides.
No kernel may reach another device: no remote copies, remote signals or barrier semaphores. Data moves between devices by JAX's collectives and lax.ppermute only.
A program may use at most 128 MiB of HBM per device.

v0:
```python
from functools import partial
import math

import jax
import jax.numpy as jnp
import numpy as np
from jax import lax
from jax.sharding import PartitionSpec as P

Q = 6
ITERS = 3


HIGHEST = lax.Precision.HIGHEST
step_size = 0.05
viscosity = 0.3
gamma_less = 0.4


def shifted_2(shard, axis, by):
    devices = lax.axis_size(axis)
    return lax.ppermute(shard, axis, [(i, (i + by) % devices) for i in range(devices)])


def basis_tables():
    root_five = 1.0 / math.sqrt(5.0)
    lobatto = np.array([0.0, 0.5 - 0.5 * root_five, 0.5 + 0.5 * root_five, 1.0])
    legendre = np.array(
        [
            -0.932469514203152,
            -0.6612093864662645,
            -0.2386191860831909,
            0.2386191860831909,
            0.6612093864662645,
            0.932469514203152,
        ]
    )
    abscissa = 0.5 + 0.5 * legendre
    shape_values = np.ones((6, 4))
    shape_slopes = np.zeros((6, 4))
    for a in range(4):
        for b in range(4):
            if b != a:
                shape_values[:, a] = (
                    shape_values[:, a] * (abscissa - lobatto[b]) / (lobatto[a] - lobatto[b])
                )
        for c in range(4):
            if c != a:
                factor_term = np.ones(6) / (lobatto[a] - lobatto[c])
                for b in range(4):
                    if b != a and b != c:
                        factor_term = (
                            factor_term * (abscissa - lobatto[b]) / (lobatto[a] - lobatto[b])
                        )
                shape_slopes[:, a] = shape_slopes[:, a] + factor_term
    thermo_values = np.stack(
        [
            (1.0 - abscissa) * (1.0 - abscissa),
            2.0 * abscissa * (1.0 - abscissa),
            abscissa * abscissa,
        ],
        axis=1,
    )
    return (
        jnp.asarray(shape_values, jnp.float32),
        jnp.asarray(shape_slopes, jnp.float32),
        jnp.asarray(thermo_values, jnp.float32),
    )


def along_x(matrix, operand):
    return jnp.einsum("qa,cabgjk->cqbgjk", matrix, operand, precision=HIGHEST)


def along_y(matrix, operand):
    return jnp.einsum("qb,cabgjk->caqgjk", matrix, operand, precision=HIGHEST)


def along_z(matrix, operand):
    return jnp.einsum("qg,cabgjk->cabqjk", matrix, operand, precision=HIGHEST)


def split_nodes(operand, which_axis):
    num_cells = (operand.shape[which_axis] - 1) // 3
    outer_dims = operand.shape[:which_axis]
    inner_dims = operand.shape[which_axis + 1 :]
    head_part = lax.slice_in_dim(operand, 0, 3 * num_cells, axis=which_axis).reshape(
        outer_dims + (num_cells, 3) + inner_dims
    )
    head_part = jnp.moveaxis(head_part, which_axis + 1, which_axis)
    tail_part = lax.slice_in_dim(operand, 3, 3 * num_cells + 1, stride=3, axis=which_axis)
    return jnp.concatenate([head_part, jnp.expand_dims(tail_part, which_axis)], axis=which_axis)


def merge_nodes(operand, which_axis):
    num_cells = operand.shape[which_axis + 1]
    outer_dims = operand.shape[:which_axis]
    inner_dims = operand.shape[which_axis + 2 :]
    head_part = jnp.moveaxis(
        lax.slice_in_dim(operand, 0, 3, axis=which_axis), which_axis, which_axis + 1
    )
    head_part = head_part.reshape(outer_dims + (3 * num_cells,) + inner_dims)
    tail_part = jnp.moveaxis(
        lax.slice_in_dim(operand, 3, 4, axis=which_axis), which_axis, which_axis + 1
    )
    pad_tail = [(0, 0)] * tail_part.ndim
    pad_tail[which_axis + 1] = (0, 2)
    tail_part = jnp.pad(tail_part, pad_tail).reshape(outer_dims + (3 * num_cells,) + inner_dims)
    pad_head = [(0, 0)] * head_part.ndim
    pad_head[which_axis] = (0, 1)
    pad_shift = [(0, 0)] * head_part.ndim
    pad_shift[which_axis] = (3, 0)
    shifted = lax.slice_in_dim(jnp.pad(tail_part, pad_shift), 0, 3 * num_cells + 1, axis=which_axis)
    return jnp.pad(head_part, pad_head) + shifted


def slab_elements(slab_field):
    closed = jnp.concatenate([slab_field, slab_field[..., :1]], axis=-1)
    parts_y = split_nodes(closed, 2)
    parts_z = split_nodes(parts_y, 4)
    return jnp.moveaxis(parts_z, 4, 3)


def slab_assemble(element_field):
    parts_z = merge_nodes(jnp.moveaxis(element_field, 3, 4), 4)
    parts_y = merge_nodes(parts_z, 2)
    return jnp.concatenate([parts_y[..., :1] + parts_y[..., -1:], parts_y[..., 1:-1]], axis=-1)


def over_blocks(node_fields, cell_data, element_fn):
    num_cells = cell_data[0].shape[1]

    def one_block(block_index):
        node_start = 3 * block_index
        element_sets = tuple(
            (
                slab_elements(lax.dynamic_slice_in_dim(field_in, node_start, 4, axis=1))
                for field_in in node_fields
            )
        )
        cell_block = tuple(
            (
                lax.dynamic_index_in_dim(member, block_index, axis=1, keepdims=False)
                for member in cell_data
            )
        )
        contribution, outputs_extra = element_fn(element_sets, cell_block)
        return (slab_assemble(contribution), outputs_extra)

    node_pieces, extra_parts = lax.map(one_block, jnp.arange(num_cells, dtype=jnp.int32))
    assembled = merge_nodes(jnp.moveaxis(node_pieces, 0, 2), 1)
    return (assembled, tuple((jnp.moveaxis(member, 0, 1) for member in extra_parts)))


def thermo_interp(thermo_values, dofs):
    return along_x(thermo_values, along_y(thermo_values, along_z(thermo_values, dofs[None])))[0]


def thermo_project(thermo_values, at_quad):
    moved = thermo_values.T
    return along_x(moved, along_y(moved, along_z(moved, at_quad[None])))[0]


def force_block(element_sets, cell_block, basis_set):
    shape_values, shape_slopes, thermo_values = basis_set
    kinematic = element_sets[0]
    energy_block, weight_block = cell_block
    trailing_shape = energy_block.shape[1:]
    z_values = along_z(shape_values, kinematic)
    z_slopes = along_z(shape_slopes, kinematic)
    yz_values = along_y(shape_values, z_values)
    gradients = [
        along_x(shape_slopes, yz_values),
        along_x(shape_values, along_y(shape_slopes, z_values)),
        along_x(shape_values, along_y(shape_values, z_slopes)),
    ]
    jacobian = [[gradients[d][c] + (1.0 if c == d else 0.0) for d in range(3)] for c in range(3)]
    grad_vel = [[gradients[d][3 + c] for d in range(3)] for c in range(3)]
    cofactor = [
        [
            jacobian[(c + 1) % 3][(d + 1) % 3] * jacobian[(c + 2) % 3][(d + 2) % 3]
            - jacobian[(c + 1) % 3][(d + 2) % 3] * jacobian[(c + 2) % 3][(d + 1) % 3]
            for d in range(3)
        ]
        for c in range(3)
    ]
    determinant = (
        jacobian[0][0] * cofactor[0][0]
        + jacobian[0][1] * cofactor[0][1]
        + jacobian[0][2] * cofactor[0][2]
    )
    inverse_det = 1.0 / determinant
    spatial_grad = [
        [
            (
                grad_vel[c][0] * cofactor[e][0]
                + grad_vel[c][1] * cofactor[e][1]
                + grad_vel[c][2] * cofactor[e][2]
            )
            * inverse_det
            for e in range(3)
        ]
        for c in range(3)
    ]
    energy_quad = thermo_interp(thermo_values, energy_block.reshape((3, 3, 3) + trailing_shape))
    mass_quad = weight_block.reshape((Q, Q, Q) + trailing_shape)
    scale_quad = mass_quad * inverse_det
    stress_shape = [
        [
            viscosity * (spatial_grad[c][d] + spatial_grad[d][c])
            - (gamma_less * energy_quad if c == d else 0.0)
            for d in range(3)
        ]
        for c in range(3)
    ]
    flux = [
        [
            scale_quad
            * (
                stress_shape[c][0] * cofactor[0][f]
                + stress_shape[c][1] * cofactor[1][f]
                + stress_shape[c][2] * cofactor[2][f]
            )
            for f in range(3)
        ]
        for c in range(3)
    ]
    power_quad = jnp.zeros_like(mass_quad)
    for c in range(3):
        for f in range(3):
            power_quad = power_quad + flux[c][f] * grad_vel[c][f]
    flux_cols = [jnp.stack([flux[c][f] for c in range(3)]) for f in range(3)]
    moved = along_x(shape_slopes.T, along_y(shape_values.T, along_z(shape_values.T, flux_cols[0])))
    moved = moved + along_x(
        shape_values.T,
        along_y(shape_slopes.T, along_z(shape_values.T, flux_cols[1]))
        + along_y(shape_values.T, along_z(shape_slopes.T, flux_cols[2])),
    )
    energy_rhs = thermo_project(thermo_values, power_quad)
    lumped_mass = thermo_project(thermo_values, mass_quad)
    energy_next = energy_block + step_size * (energy_rhs / lumped_mass).reshape(energy_block.shape)
    return (-moved, (energy_next,))


def mass_block(element_sets, cell_block, basis_set):
    shape_values = basis_set[0]
    mass_quad = cell_block[0].reshape((Q, Q, Q) + cell_block[0].shape[1:])
    at_quad = (
        along_x(shape_values, along_y(shape_values, along_z(shape_values, element_sets[0])))
        * mass_quad
    )
    return (along_x(shape_values.T, along_y(shape_values.T, along_z(shape_values.T, at_quad))), ())


def extend_right(field_in):
    right_rim = shifted_2(field_in[:, :1], "gx", -1)
    wide_field = jnp.concatenate([field_in, right_rim], axis=1)
    top_rim = shifted_2(wide_field[:, :, :1], "gy", -1)
    return jnp.concatenate([wide_field, top_rim], axis=2)


def fold_back(field_in):
    upper_rim = shifted_2(field_in[:, :, -1:], "gy", 1)
    field_in = jnp.concatenate([field_in[:, :, :1] + upper_rim, field_in[:, :, 1:-1]], axis=2)
    side_rim = shifted_2(field_in[:, -1:], "gx", 1)
    return jnp.concatenate([field_in[:, :1] + side_rim, field_in[:, 1:-1]], axis=1)


def global_sum(value):
    return lax.psum(value, ("gx", "gy"))


def on_device(displacement, velocity, energy, mass_weight, pinned_flags):
    basis_set = basis_tables()
    free_mask = (1 - pinned_flags).astype(jnp.float32)
    kinematic = jnp.concatenate([displacement, velocity], axis=0)
    mass_apply = partial(mass_block, basis_set=basis_set)
    rows_x = displacement.shape[1]
    rows_y = displacement.shape[2]
    assembled, extra_parts = over_blocks(
        (extend_right(kinematic),), (energy, mass_weight), partial(force_block, basis_set=basis_set)
    )
    nodal_force = fold_back(assembled)
    owned = 1.0
    residual = free_mask * nodal_force
    energy_new = extra_parts[0]

    def local_inner(first, second):
        return jnp.sum(owned * (first * second))

    acceleration = jnp.zeros_like(residual)
    direction = residual
    norm_now = global_sum(local_inner(residual, residual))
    for iteration in range(ITERS):
        contribution = over_blocks((extend_right(direction),), (mass_weight,), mass_apply)[0]
        mass_image = free_mask * fold_back(contribution)
        step_length = norm_now / global_sum(local_inner(direction, mass_image))
        acceleration = acceleration + step_length * direction
        residual = residual - step_length * mass_image
        norm_next = global_sum(local_inner(residual, residual))
        direction = residual + norm_next / norm_now * direction
        norm_now = norm_next
    acceleration = acceleration[:, :rows_x, :rows_y]
    velocity_new = velocity + step_size * acceleration
    displacement_new = displacement + step_size * velocity_new
    return (acceleration, velocity_new, displacement_new, energy_new)


def solution(mesh):
    in_specs = (
        P(None, "gx", "gy", None),
        P(None, "gx", "gy", None),
        P(None, "gx", "gy", None),
        P(None, "gx", "gy", None),
        P(None, "gx", "gy", None),
    )
    out_specs = (
        P(None, "gx", "gy", None),
        P(None, "gx", "gy", None),
        P(None, "gx", "gy", None),
        P(None, "gx", "gy", None),
    )
    return jax.shard_map(
        on_device, mesh=mesh, in_specs=in_specs, out_specs=out_specs, check_vma=False
    )
```

profile of v0, /device:TPU:1, one launch (start us, length us, event | category | flops | bytes accessed | tf_op | source)
XLA Modules:
  0.0 1001.1 jit_solution(13770269630577380290)
XLA Ops:
  9.4 5.0 collective-permute-start.1
  21.4 12.5 %copy.282 = f32[6,4,4,8,384]{3,2,4,1,0:T(4,128)} copy(f32[6,4,4,8,384]{4,3,2,1,0:T(8,128)S(1)} %fusion.109) | data formatting | bytes 2359296 | tf_op jit(solution)/shard_map/while/body/eval_jaxpr/slice | solution.py:87
  33.9 18.3 %copy.283 = f32[6,4,4,8,128,3]{4,5,3,2,1,0:T(4,128)S(1)} copy(f32[6,4,4,8,128,3]{3,2,5,4,1,0:T(4,128)} %bitcast.311) | data formatting | bytes 2359296 | tf_op jit(solution)/shard_map/while/body/eval_jaxpr/reshape | solution.py:87
  52.2 15.2 %slice.434 = f32[6,4,4,8,128]{4,3,2,1,0:T(8,128)S(1)} slice(f32[6,4,4,8,385]{4,3,2,1,0:T(8,128)} %pad_maximum_fusion.3), slice={[0:6:1], [0:4:1], [0:4:1], [0:8:1], [3:385:3]} | slice | bytes 786432 | tf_op jit(solution)/shard_map/while/body/eval_jaxpr/slice | solution.py:91
  74.6 5.9 convolution_bitcast_fusion
  80.4 5.7 convolution_bitcast_fusion.1
  86.1 9.3 fusion.18
  95.4 5.7 fusion.36
  101.1 9.5 fusion.16
  110.6 9.5 fusion.20
  121.0 10.7 %copy_bitcast_fusion = (f32[6,6,6,6,8,128]{5,4,3,2,1,0:T(8,128)}, f32[6,6,6,6,8,128]{5,4,3,2,1,0:T(8,128)}) fusion(f32[6,6,6,8,128,6]{4,5,3,2,1,0:T(8,128)} %fusion.16, f32[6,6,6,8,128,6]{4,5,3,2,1,0:T(8,128)} %fusion.18), kind=kLoop, calls=%fused_computation.12 | loop fusion | bytes 21233664 | tf_op jit(solution)/shard_map/while/body/eval_jaxpr/qa,cabgjk->cqbgjk/transpose | solution.py:72
  131.7 5.6 bitcast_subtract_fusion.1
  139.7 4.8 multiply_multiply_fusion.1
  144.5 11.0 %add_bitcast_fusion = (f32[6,6,6,8,128]{4,3,2,1,0:T(8,128)}, f32[1,6,6,6,8,128]{5,4,3,2,1,0:T(8,128)}, f32[1,6,6,6,8,128]{5,4,3,2,1,0:T(8,128)}, f32[1,6,6,6,8,1...) fusion(f32[1,6,6,6,8,128]{5,4,3,2,1,0:T(8,128)S(1)} %get-tuple-, ...), kind=kLoop, calls=%fused_computation.143 | loop fusion | flops 25878528 | bytes 31850496 | tf_op jit(solution)/shard_map/reshape.83
  184.8 8.2 copy.305
  192.9 6.0 pad.142.clone
  198.9 10.8 %fusion = f32[3,4,4,8,385]{3,2,4,1,0:T(4,128)} fusion(f32[3,4,4,8,384]{3,2,4,1,0:T(4,128)} %bitcast.323, f32[3,4,4,8,384]{3,2,4,1,0:T(4,128)S(1)} %bitcast.319), kind=kLoop, calls=%fused_computation.4 | loop fusion | flops 147840 | bytes 1771008 | tf_op jit(solution)/shard_map/while/body/eval_jaxpr/add | solution.py:114
  209.7 7.9 slice_bitcast_fusion.3
  217.6 6.1 slice_bitcast_fusion.7
  223.7 9.2 copy.307
  236.0 5.9 collective-permute-done.2
  262.2 8.0 copy.314
  270.3 10.3 %copy.315 = f32[3,4,4,8,128,3]{4,5,3,2,1,0:T(4,128)} copy(f32[3,4,4,8,128,3]{3,2,5,4,1,0:T(4,128)} %bitcast.327) | data formatting | bytes 1179648 | tf_op jit(solution)/shard_map/while/body/eval_jaxpr/reshape | solution.py:87
  280.6 7.7 slice.477
  298.8 5.0 fusion.64
  312.6 7.4 pad.151.clone
  320.0 8.2 copy.322
  328.2 12.8 %fusion.1 = f32[3,4,4,8,385]{3,2,4,1,0:T(4,128)} fusion(f32[3,4,4,8,384]{3,2,4,1,0:T(4,128)} %bitcast.320, f32[3,4,4,8,384]{3,2,4,1,0:T(4,128)} %bitcast.324), kind=kLoop, calls=%fused_computation.5 | loop fusion | flops 147840 | bytes 1771008 | tf_op jit(solution)/shard_map/while/body/eval_jaxpr/add | solution.py:114
  341.0 7.9 slice_bitcast_fusion.2
  349.0 7.5 slice_bitcast_fusion.6
  356.5 10.0 copy.324
  368.5 6.5 copy.379
  377.0 6.1 collective-permute-done.6
  388.2 66.0 %all-reduce.36 = (f32[]{:T(128)}, f32[]{:T(128)}) all-reduce(f32[]{:T(128)} %get-tuple-element.88, f32[]{:T(128)} %get-tuple-element.87), channel_id=1, replica_groups=mesh['gx'=8,'gy'=16] {'gx','gy'}, use_global_device_ids=true, to_apply=%region_1.2 | all-reduce | flops 2 | bytes 16 | tf_op jit(solution)/shard_map/psum | solution.py:270
  457.2 62.5 %psum.44 = f32[]{:T(128)} all-reduce(f32[]{:T(128)} %get-tuple-element.114), channel_id=1, replica_groups=mesh['gx'=8,'gy'=16] {'gx','gy'}, use_global_device_ids=true, to_apply=%region_5.6 | all-reduce | flops 1 | bytes 8 | tf_op jit(solution)/shard_map/psum | solution.py:270
  536.6 8.0 copy.332
  544.6 10.3 %copy.333 = f32[3,4,4,8,128,3]{4,5,3,2,1,0:T(4,128)} copy(f32[3,4,4,8,128,3]{3,2,5,4,1,0:T(4,128)} %bitcast.328) | data formatting | bytes 1179648 | tf_op jit(solution)/shard_map/while/body/eval_jaxpr/reshape | solution.py:87
  554.9 8.5 slice.502
  569.4 4.7 bitcast_multiply_fusion.1
  574.1 5.1 fusion.67
  589.4 7.4 pad.160.clone
  596.9 8.2 copy.339
  605.0 12.8 %fusion.2 = f32[3,4,4,8,385]{3,2,4,1,0:T(4,128)} fusion(f32[3,4,4,8,384]{3,2,4,1,0:T(4,128)} %bitcast.321, f32[3,4,4,8,384]{3,2,4,1,0:T(4,128)} %bitcast.325), kind=kLoop, calls=%fused_computation.6 | loop fusion | flops 147840 | bytes 1771008 | tf_op jit(solution)/shard_map/while/body/eval_jaxpr/add | solution.py:114
  617.9 7.9 slice_bitcast_fusion.1
  625.8 7.5 slice_bitcast_fusion.5
  633.3 10.0 copy.341
  645.4 7.4 copy.382
  655.3 6.3 collective-permute-done.10
  665.9 65.0 %psum.45 = f32[]{:T(128)} all-reduce(f32[]{:T(128)} %get-tuple-element.112), channel_id=1, replica_groups=mesh['gx'=8,'gy'=16] {'gx','gy'}, use_global_device_ids=true, to_apply=%region_7.8 | all-reduce | flops 1 | bytes 8 | tf_op jit(solution)/shard_map/psum | solution.py:270
  735.6 62.5 %psum.46 = f32[]{:T(128)} all-reduce(f32[]{:T(128)} %multiply_reduce_fusion), channel_id=1, replica_groups=mesh['gx'=8,'gy'=16] {'gx','gy'}, use_global_device_ids=true, to_apply=%region_9.10 | all-reduce | flops 1 | bytes 8 | tf_op jit(solution)/shard_map/psum | solution.py:270
  813.1 8.0 copy.349
  821.2 10.3 %copy.350 = f32[3,4,4,8,128,3]{4,5,3,2,1,0:T(4,128)} copy(f32[3,4,4,8,128,3]{3,2,5,4,1,0:T(4,128)} %bitcast.329) | data formatting | bytes 1179648 | tf_op jit(solution)/shard_map/while/body/eval_jaxpr/reshape | solution.py:87
  831.5 7.9 slice.527
  845.2 4.7 bitcast_multiply_fusion
  849.9 4.8 fusion.70
  862.6 7.4 pad.169.clone
  870.1 7.0 copy.356
  877.1 12.9 %fusion.3 = f32[3,4,4,8,385]{3,2,4,1,0:T(4,128)} fusion(f32[3,4,4,8,384]{3,2,4,1,0:T(4,128)} %bitcast.322, f32[3,4,4,8,384]{3,2,4,1,0:T(4,128)} %bitcast.326), kind=kLoop, calls=%fused_computation.7 | loop fusion | flops 147840 | bytes 1771008 | tf_op jit(solution)/shard_map/while/body/eval_jaxpr/add | solution.py:114
  890.0 7.9 slice_bitcast_fusion
  897.9 7.5 slice_bitcast_fusion.4
  905.4 9.1 copy.358
  914.8 6.5 copy.385
  923.5 4.9 collective-permute-done.14
  933.3 65.1 %psum.47 = f32[]{:T(128)} all-reduce(f32[]{:T(128)} %fusion.140), channel_id=1, replica_groups=mesh['gx'=8,'gy'=16] {'gx','gy'}, use_global_device_ids=true, to_apply=%region_11.12 | all-reduce | flops 1 | bytes 8 | tf_op jit(solution)/shard_map/psum | solution.py:270
  (253 shorter events, 187.8 us)
Async XLA Ops:
  0.6 13.7 %copy-start.25 = (f32[6,3,1,1,1]{0,1,4,3,2:T(4,128)S(1)}, f32[6,3,1,1,1]{0,1,4,3,2:T(4,128)}, u32[]{:S(2)}) copy-start(f32[6,3,1,1,1]{0,1,4,3,2:T(4,128)} %constant.174) | copy-start | bytes 220
  2.7 6.7 collective-permute-start
  9.4 6.4 collective-permute-start.1
  33.9 33.5 %copy-start.18 = (f32[6,4,1,1,1,1]{0,1,5,4,3,2:T(4,128)S(1)}, f32[6,4,1,1,1,1]{0,1,5,4,3,2:T(4,128)}, u32[]{:S(2)}) copy-start(f32[6,4,1,1,1,1]{0,1,5,4,3,2:T(4,128)} %constant.172) | copy-start | bytes 292
  67.4 3.6 copy-start.27
  131.7 5.6 slice-start
  131.7 7.5 slice-start.2
  131.7 7.7 slice-start.1
  131.7 8.0 slice-start.3
  139.7 4.8 copy-start.1
  155.6 1.8 copy-start.10
  155.6 1.8 copy-start.11
  161.0 3.1 copy-start.7
  161.0 3.1 copy-start.8
  161.0 3.1 copy-start.9
  164.3 3.5 copy-start.4
  164.3 3.5 copy-start.5
  164.3 3.5 copy-start.6
  192.9 6.0 copy-start
  235.7 10.8 %copy-start.3 = (s32[3,3,24,384]{3,2,1,0:T(8,128)S(1)}, s32[3,3,24,384]{3,2,1,0:T(8,128)}, u32[]{:S(2)}) copy-start(s32[3,3,24,384]{3,2,1,0:T(8,128)} %param.12) | copy-start | bytes 995332
  235.8 18.2 %copy-start.2 = (f32[216,1,8,128]{3,2,1,0:T(8,128)S(1)}, f32[216,1,8,128]{3,2,1,0:T(8,128)}, u32[]{:S(2)}) copy-start(f32[216,1,8,128]{3,2,1,0:T(8,128)} %param.11) | copy-start | bytes 2654212
  235.8 6.0 collective-permute-start.2
  241.9 4.6 collective-permute-start.3
  246.6 5.5 collective-permute-start.4
  252.2 2.7 collective-permute-start.5
  254.9 0.9 copy-start.12
  375.0 1.1 copy-start.15
  376.8 6.3 collective-permute-start.6
  383.1 4.2 collective-permute-start.7
  387.4 66.8 %copy-start.22 = (f32[3,1,24,384]{3,2,1,0:T(8,128)}, f32[3,1,24,384]{3,2,1,0:T(8,128)S(1)}, u32[]{:S(2)}) copy-start(f32[3,1,24,384]{3,2,1,0:T(8,128)S(1)} %maximum_add_fusion.2) | copy-start | bytes 331780
  521.1 4.2 collective-permute-start.8
  525.3 3.2 collective-permute-start.9
  528.6 0.9 copy-start.13
  533.1 1.7 copy-start.17
  652.8 1.3 copy-start.16
  654.5 8.6 copy-start.26
  654.9 6.7 collective-permute-start.10
  661.7 3.5 collective-permute-start.11
  799.5 4.2 collective-permute-start.12
  803.7 3.9 collective-permute-start.13
  807.8 0.9 copy-start.14
  922.0 1.0 copy-start.21
  922.2 8.0 copy-start.24
  922.4 6.0 collective-permute-start.14
  923.4 9.2 copy-start.23
  923.4 76.3 %copy-start.19 = (f32[3,3,24,384]{3,2,1,0:T(8,128)S(1)}, f32[3,3,24,384]{3,2,1,0:T(8,128)}, u32[]{:S(2)}) copy-start(f32[3,3,24,384]{3,2,1,0:T(8,128)} %param.8) | copy-start | bytes 995332
  923.4 76.3 %copy-start.20 = (f32[3,3,24,384]{3,2,1,0:T(8,128)S(1)}, f32[3,3,24,384]{3,2,1,0:T(8,128)}, u32[]{:S(2)}) copy-start(f32[3,3,24,384]{3,2,1,0:T(8,128)} %param.9) | copy-start | bytes 995332
  928.4 3.5 collective-permute-start.15
where the time goes:
time: 1010 us; the launch traced here: 1000 us
  local copies, waits for them, and re-layouts  364 us (36%)
  blocking collectives  321 us (32%)
  matrix products  153 us (15%)
  other arithmetic  88.8 us (9%)
  waiting for transfers between devices  40 us (4%)
  starting transfers between devices  25.2 us (2%)
    psum x5, blocking collectives, global_sum(): return lax.psum(value, ('gx', 'gy'))  321 us
    transpose x16, local copies, waits for them, and re-layouts, merge_nodes(): jnp.moveaxis(lax.slice_in_dim(operand, 0, 3, axis=which_axis), which_axis...  104 us
    dot_general x14, matrix products, along_x(): return jnp.einsum('qa,cabgjk->cqbgjk', matrix, operand, precision=HIGHEST)  55.3 us
    dot_general x15, matrix products, along_y(): return jnp.einsum('qb,cabgjk->caqgjk', matrix, operand, precision=HIGHEST)  50.4 us
    reshape x8, local copies, waits for them, and re-layouts, split_nodes(): lax.slice_in_dim(operand, 0, 3 * num_cells, axis=which_axis)  50.1 us
    add x12, other arithmetic, merge_nodes(): return jnp.pad(head_part, pad_head) + shifted  50 us
    dot_general x14, matrix products, along_z(): return jnp.einsum('qg,cabgjk->cabqjk', matrix, operand, precision=HIGHEST)  47.1 us
    slice x8, local copies, waits for them, and re-layouts, split_nodes(): lax.slice_in_dim(operand, 3, 3 * num_cells + 1, stride=3, axis=which_axis)  46.5 us
  transfers between devices with their start and end apart: 16, of which 13 were waited for; matrix products, arithmetic and copies ran while one was open for 1% of the time, Pallas kernels for 0%

commit v1 on v0

v1 whole, which is shorter than its diff:
```python
import math

import jax
import jax.numpy as jnp
import numpy as np
from jax import lax
from jax.experimental import pallas as pl
from jax.experimental.pallas import tpu as pltpu
from jax.sharding import PartitionSpec as P

step_size = 0.05
viscosity = 0.3
gamma_less = 0.4
F32 = jnp.float32
VMEM_LIMIT = 48 * 1024 * 1024


def tables():
    root_five = 1.0 / math.sqrt(5.0)
    lobatto = np.array([0.0, 0.5 - 0.5 * root_five, 0.5 + 0.5 * root_five, 1.0])
    legendre = np.array(
        [
            -0.932469514203152,
            -0.6612093864662645,
            -0.2386191860831909,
            0.2386191860831909,
            0.6612093864662645,
            0.932469514203152,
        ]
    )
    t = 0.5 + 0.5 * legendre
    values = np.ones((6, 4))
    slopes = np.zeros((6, 4))
    for a in range(4):
        for b in range(4):
            if b != a:
                values[:, a] *= (t - lobatto[b]) / (lobatto[a] - lobatto[b])
        for c in range(4):
            if c != a:
                term = np.ones(6) / (lobatto[a] - lobatto[c])
                for b in range(4):
                    if b != a and b != c:
                        term = term * (t - lobatto[b]) / (lobatto[a] - lobatto[b])
                slopes[:, a] += term
    thermo = np.stack([(1.0 - t) * (1.0 - t), 2.0 * t * (1.0 - t), t * t], axis=1)
    return values, slopes, thermo


def even_odd(matrix):
    even = [[float((matrix[q, a] + matrix[q, 3 - a]) / 2) for a in range(2)] for q in range(3)]
    odd = [[float((matrix[q, a] - matrix[q, 3 - a]) / 2) for a in range(2)] for q in range(3)]
    return even, odd


VALUES, SLOPES, THERMO = tables()
BE, BO = even_odd(VALUES)
DE, DO = even_odd(SLOPES)
TE = [float((THERMO[q, 0] + THERMO[q, 2]) / 2) for q in range(3)]
TO = [float((THERMO[q, 0] - THERMO[q, 2]) / 2) for q in range(3)]
TM = [float(THERMO[q, 1]) for q in range(3)]


def butterfly(u):
    return [u[0] + u[3], u[1] + u[2], u[0] - u[3], u[1] - u[2]]


def unbutterfly(r):
    return [r[0] + r[2], r[1] + r[3], r[1] - r[3], r[0] - r[2]]


def interp_pair(h, q):
    even = BE[q][0] * h[0] + BE[q][1] * h[1]
    odd = BO[q][0] * h[2] + BO[q][1] * h[3]
    return even + odd, even - odd


def slope_pair(h, q):
    even = DE[q][0] * h[0] + DE[q][1] * h[1]
    odd = DO[q][0] * h[2] + DO[q][1] * h[3]
    return odd + even, odd - even


def along(pair_fn, h):
    out = [None] * 6
    for q in range(3):
        out[q], out[5 - q] = pair_fn(h, q)
    return out


def plus(total, term):
    return term if total is None else total + term


def interp_back(f, h=None, sign=1.0):
    h = [None] * 4 if h is None else list(h)
    for q in range(3):
        even, odd = f[q] + f[5 - q], f[q] - f[5 - q]
        for a in range(2):
            h[a] = plus(h[a], (sign * BE[q][a]) * even)
            h[2 + a] = plus(h[2 + a], (sign * BO[q][a]) * odd)
    return h


def slope_back(f, h=None, sign=1.0):
    h = [None] * 4 if h is None else list(h)
    for q in range(3):
        even, odd = f[q] + f[5 - q], f[q] - f[5 - q]
        for a in range(2):
            h[a] = plus(h[a], (sign * DE[q][a]) * odd)
            h[2 + a] = plus(h[2 + a], (sign * DO[q][a]) * even)
    return h


def thermo_along(u):
    even, odd, mid = u[0] + u[2], u[0] - u[2], u[1]
    out = [None] * 6
    for q in range(3):
        both, one = TE[q] * even + TM[q] * mid, TO[q] * odd
        out[q], out[5 - q] = both + one, both - one
    return out


def thermo_back(f):
    even = mid = odd = None
    for q in range(3):
        both, one = f[q] + f[5 - q], f[q] - f[5 - q]
        even = plus(even, TE[q] * both)
        mid = plus(mid, TM[q] * both)
        odd = plus(odd, TO[q] * one)
    return [even + odd, mid, even - odd]


def iotas(rows=8):
    shape = (rows, 128)
    return lax.broadcasted_iota(jnp.int32, shape, 0), lax.broadcasted_iota(jnp.int32, shape, 1)


def gather_lanes(x, index):
    return jnp.take_along_axis(x, index, axis=1, mode="promise_in_bounds")


def split_lanes(parts, rows=8):
    lane = iotas(rows)[1]
    out = []
    for g in range(3):
        place = 3 * lane + g
        index = place & 127
        moved = [gather_lanes(p, index) for p in parts]
        out.append(
            jnp.where(place < 128, moved[0], jnp.where(place < 256, moved[1], moved[2]))
        )
    return out


def join_lanes(parts):
    lane = iotas()[1]
    out = []
    for v in range(3):
        place = lane + 128 * v
        index = place // 3
        g = place - 3 * index
        moved = [gather_lanes(p, index) for p in parts]
        out.append(jnp.where(g == 0, moved[0], jnp.where(g == 1, moved[1], moved[2])))
    return out


def next_lane(x):
    return pltpu.roll(x, 127, 1)


def previous_lane(x):
    return pltpu.roll(x, 1, 1)


def pack_kernel(d_ref, v_ref, f_ref, x_ref, y_ref, c_ref):
    for n, ref in enumerate((d_ref, v_ref, f_ref)):
        for c in range(3):
            k = 3 * n + c
            face = ref[c, 0].astype(F32)
            x_ref[k] = face
            c_ref[k : k + 1, :] = face[0:1]
            for x in range(3):
                r = 9 * x + k
                y_ref[r : r + 1, :] = ref[c, x, 0:1, :].astype(F32)


def element_rows(load, place):
    for t in range(3):
        tiles = split_lanes([load(8 * t, 128 * v) for v in range(3)])
        for g in range(3):
            place[g, 8 * t : 8 * t + 8, :] = tiles[g]
    return [place[g, pl.ds(b, 8, stride=3), :] for b in range(3) for g in range(3)]


def prep_kernel(d_ref, v_ref, f_ref, u_ref, m_ref, place):
    def body(c, _):
        for x in range(3):
            for k, ref in enumerate((d_ref, v_ref, f_ref)):
                tiles = element_rows(
                    lambda s, l: ref[c, x, s : s + 8, l : l + 128].astype(F32), place.at[3 * x + k]
                )
                for n in range(9):
                    if k < 2:
                        u_ref[3 * k + c, x * 9 + n] = tiles[n]
                    else:
                        m_ref[x, c * 9 + n] = 1.0 - tiles[n]
        return 0

    lax.fori_loop(0, 3, body, 0)


def point(jac, vel, energy, mass):
    cof = [
        [
            jac[(c + 1) % 3][(d + 1) % 3] * jac[(c + 2) % 3][(d + 2) % 3]
            - jac[(c + 1) % 3][(d + 2) % 3] * jac[(c + 2) % 3][(d + 1) % 3]
            for d in range(3)
        ]
        for c in range(3)
    ]
    det = jac[0][0] * cof[0][0] + jac[0][1] * cof[0][1] + jac[0][2] * cof[0][2]
    inv = pl.reciprocal(det, approx=True)
    inv = inv * (2.0 - det * inv)
    inv = inv * (2.0 - det * inv)
    scale = mass * inv
    shear = (viscosity * scale) * inv
    press = scale * energy
    rate = [
        [vel[c][0] * cof[e][0] + vel[c][1] * cof[e][1] + vel[c][2] * cof[e][2] for e in range(3)]
        for c in range(3)
    ]
    stress = [[None] * 3 for _ in range(3)]
    power = None
    for c in range(3):
        stress[c][c] = shear * (rate[c][c] + rate[c][c]) - press
        power = plus(power, stress[c][c] * rate[c][c])
        for d in range(c + 1, 3):
            both = rate[c][d] + rate[d][c]
            stress[c][d] = stress[d][c] = shear * both
            power = power + stress[c][d] * both
    flux = [
        [
            stress[c][0] * cof[0][f] + stress[c][1] * cof[1][f] + stress[c][2] * cof[2][f]
            for f in range(3)
        ]
        for c in range(3)
    ]
    return flux, power


def spread_y(first, row):
    sub = iotas()[0]
    return jnp.where(sub == 7, row, pltpu.roll(first, 7, 0))


def store_parts(nodes_of, minus_ref, plus_ref, inner_ref, rim_ref):
    sub = iotas()[0]

    def body(c, _):
        for g in range(3):
            nodes = nodes_of(c, g)
            for x in range(4):
                over = nodes[x][3]
                nodes[x][0] = nodes[x][0] + jnp.where(sub == 0, 0.0, pltpu.roll(over, 1, 0))
                r = c * 3 + g
                if x in (0, 3):
                    ref = minus_ref if x == 0 else plus_ref
                    ref[pl.ds(216 + r, 1), :] = over[7:8]
                    for b in range(3):
                        ref[pl.ds(pl.multiple_of((c * 9 + b * 3 + g) * 8, 8), 8), :] = nodes[x][b]
                else:
                    rim_ref[x - 1, pl.ds(r, 1), :] = over[7:8]
                    for b in range(3):
                        inner_ref[x - 1, c * 9 + b * 3 + g] = nodes[x][b]
        return 0

    lax.fori_loop(0, 3, body, 0)


def force_kernel(
    u_ref, hx_ref, hy_ref, hc_ref, e_ref, w_ref,
    minus_ref, plus_ref, inner_ref, rim_ref, face_mask_ref, rim_mask_ref, energy_ref,
    hx_s, hy_s, q_s, zv_s, zs_s, w_s, ez_s, ey_s, xt_s, ya_s, yb_s, zn_s, px_s, py_s, place,
):
    rows = [
        jnp.concatenate(
            [hy_ref[:, 128 * v : 128 * v + 128], hc_ref[:, 128 * v : 128 * v + 128]], axis=0
        )
        for v in range(3)
    ]
    rows = [jnp.concatenate([r, jnp.zeros((4, 128), F32)], axis=0) for r in rows]
    for t in range(5):
        for g, tile in enumerate(split_lanes([r[8 * t : 8 * t + 8] for r in rows])):
            hy_s[g, 8 * t : 8 * t + 8, :] = tile
    for x in range(4):
        for c in range(3):
            for g in range(3):
                r = 9 * x + 6 + c
                rim_mask_ref[x, c * 3 + g : c * 3 + g + 1, :] = 1.0 - hy_s[g, r : r + 1, :]

    def face(j, _):
        for i in range(3):
            k = 3 * j + i
            tiles = element_rows(lambda s, l: hx_ref[k, s : s + 8, l : l + 128], place.at[i])
            for n in range(9):
                hx_s[k, n] = tiles[n]
        return 0

    lax.fori_loop(0, 3, face, 0)
    for c in range(3):
        for n in range(9):
            face_mask_ref[c * 9 + n] = 1.0 - hx_s[6 + c, n]

    def gather_nodes(c, _):
        for g in range(3):
            cols = []
            for x in range(4):
                if x < 3:
                    u = [u_ref[c, x * 9 + b * 3 + g] for b in range(3)]
                else:
                    u = [hx_s[c, b * 3 + g] for b in range(3)]
                row = hy_s[g, pl.ds(9 * x + c, 1), :]
                u.append(spread_y(u[0], row))
                cols.append(butterfly(u))
            for y in range(4):
                for x, t in enumerate(butterfly([cols[x][y] for x in range(4)])):
                    q_s[c, (x * 4 + y) * 3 + g] = t
        return 0

    lax.fori_loop(0, 6, gather_nodes, 0)

    def along_z(c, _):
        for n in range(16):
            u = [q_s[c, 3 * n + g] for g in range(3)]
            u.append(next_lane(u[0]))
            h = butterfly(u)
            for q, t in enumerate(along(interp_pair, h)):
                zv_s[q, c, n] = t
            for q, t in enumerate(along(slope_pair, h)):
                zs_s[q, c, n] = t
        return 0

    lax.fori_loop(0, 6, along_z, 0)
    for n in range(9):
        for q, t in enumerate(thermo_along([e_ref[3 * n + g] for g in range(3)])):
            ez_s[q, n] = t

    def plane(z, _):
        def along_y(c, _):
            for x in range(4):
                h = [zv_s[z, c, x * 4 + y] for y in range(4)]
                s = [zs_s[z, c, x * 4 + y] for y in range(4)]
                for q, t in enumerate(along(interp_pair, h)):
                    w_s[q, 0, c * 4 + x] = t
                for q, t in enumerate(along(slope_pair, h)):
                    w_s[q, 1, c * 4 + x] = t
                for q, t in enumerate(along(interp_pair, s)):
                    w_s[q, 2, c * 4 + x] = t
            return 0

        lax.fori_loop(0, 6, along_y, 0)
        for x in range(3):
            for q, t in enumerate(thermo_along([ez_s[z, 3 * x + y] for y in range(3)])):
                ey_s[q, x] = t

        def line(y, _):
            energy = thermo_along([gamma_less * ey_s[y, x] for x in range(3)])
            power = [None] * 6
            mass = [None] * 6
            back = [[[None] * 4 for _ in range(3)] for _ in range(3)]
            for q in range(3):
                grads = [[[None] * 3 for _ in range(6)] for _ in range(2)]
                for c in range(6):
                    for d in range(3):
                        h = [w_s[y, d, c * 4 + x] for x in range(4)]
                        pair = slope_pair(h, q) if d == 0 else interp_pair(h, q)
                        for side in range(2):
                            t = pair[side]
                            grads[side][c][d] = t + 1.0 if c == d else t
                flux = []
                for side in range(2):
                    p = q if side == 0 else 5 - q
                    mass[p] = w_ref[p * 36 + y * 6 + z]
                    f, power[p] = point(grads[side][:3], grads[side][3:], energy[p], mass[p])
                    flux.append(f)
                for c in range(3):
                    for f in range(3):
                        even = flux[0][c][f] + flux[1][c][f]
                        odd = flux[0][c][f] - flux[1][c][f]
                        h = back[c][f]
                        for a in range(2):
                            if f == 0:
                                h[a] = plus(h[a], DE[q][a] * odd)
                                h[2 + a] = plus(h[2 + a], DO[q][a] * even)
                            else:
                                h[a] = plus(h[a], BE[q][a] * even)
                                h[2 + a] = plus(h[2 + a], BO[q][a] * odd)
            for c in range(3):
                for f in range(3):
                    for x in range(4):
                        xt_s[y, f, c * 4 + x] = back[c][f][x]
            for x, t in enumerate(thermo_back(power)):
                px_s[y, x] = t
            for x, t in enumerate(thermo_back(mass)):
                px_s[y, 3 + x] = t
            return 0

        lax.fori_loop(0, 6, line, 0)

        def back_y(c, _):
            for x in range(4):
                f = [[xt_s[q, d, c * 4 + x] for q in range(6)] for d in range(3)]
                h = slope_back(f[1], interp_back(f[0]))
                s = interp_back(f[2])
                for y in range(4):
                    ya_s[z, c, x * 4 + y] = h[y]
                    yb_s[z, c, x * 4 + y] = s[y]
            return 0

        lax.fori_loop(0, 3, back_y, 0)
        for x in range(6):
            for y, t in enumerate(thermo_back([px_s[q, x] for q in range(6)])):
                py_s[z, 3 * x + y] = t
        return 0

    lax.fori_loop(0, 6, plane, 0)

    for n in range(9):
        work = thermo_back([py_s[q, n] for q in range(6)])
        lump = thermo_back([py_s[q, 9 + n] for q in range(6)])
        for g in range(3):
            energy_ref[3 * n + g] = e_ref[3 * n + g] + step_size * (work[g] / lump[g])

    def back_z(c, _):
        for n in range(16):
            h = interp_back([ya_s[q, c, n] for q in range(6)], sign=-1.0)
            h = slope_back([yb_s[q, c, n] for q in range(6)], h, sign=-1.0)
            u = unbutterfly(h)
            zn_s[c, n * 3] = u[0] + previous_lane(u[3])
            zn_s[c, n * 3 + 1] = u[1]
            zn_s[c, n * 3 + 2] = u[2]
        return 0

    lax.fori_loop(0, 3, back_z, 0)
    store_parts(lambda c, g: nodes_from(zn_s, c, g), minus_ref, plus_ref, inner_ref, rim_ref)


def nodes_from(zn_s, c, g):
    cols = [unbutterfly([zn_s[c, (x * 4 + y) * 3 + g] for y in range(4)]) for x in range(4)]
    rows = [unbutterfly([cols[x][b] for x in range(4)]) for b in range(4)]
    return [[rows[b][x] for b in range(4)] for x in range(4)]


def rows_kernel(minus_ref, plus_ref, inner_ref, rim_ref, got_low_ref, got_high_ref, down_ref, up_ref):
    for c in range(3):
        for g in range(3):
            r = c * 3 + g
            n = (c * 9 + g) * 8
            down_ref[r : r + 1, :] = minus_ref[n : n + 1, :] + got_low_ref[n : n + 1, :]
            down_ref[27 + r : 28 + r, :] = plus_ref[n : n + 1, :] + got_high_ref[n : n + 1, :]
            for x in range(2):
                down_ref[9 * (x + 1) + r : 9 * (x + 1) + r + 1, :] = inner_ref[x, c * 9 + g, 0:1, :]
    up_ref[0:9, :] = minus_ref[216:225, :] + got_low_ref[216:225, :]
    up_ref[27:36, :] = plus_ref[216:225, :] + got_high_ref[216:225, :]
    for x in range(2):
        up_ref[9 * (x + 1) : 9 * (x + 1) + 9, :] = rim_ref[x, 0:9, :]


def assemble(c, parts, mask_ref, face_mask_ref, rim_mask_ref, own_ref, q_s):
    minus_ref, plus_ref, inner_ref, rim_ref, low_ref, high_ref, from_down_ref, from_up_ref = parts
    sub = iotas()[0]
    for g in range(3):
        r = c * 3 + g
        cols = []
        for x in range(4):
            u = []
            for b in range(3):
                n = c * 9 + b * 3 + g
                tile = pl.ds(pl.multiple_of(n * 8, 8), 8)
                if x == 0:
                    t = minus_ref[tile, :] + low_ref[tile, :]
                elif x == 3:
                    t = plus_ref[tile, :] + high_ref[tile, :]
                else:
                    t = inner_ref[x - 1, n]
                if b == 0:
                    below = from_down_ref[pl.ds(9 * x + r, 1), :]
                    t = t + jnp.where(sub == 0, below, 0.0)
                t = t * (face_mask_ref[n] if x == 3 else mask_ref[x, n])
                u.append(t)
                if x < 3:
                    own_ref[x, n] = t
            edge = pl.ds(216 + r, 1)
            if x == 0:
                top = minus_ref[edge, :] + low_ref[edge, :]
            elif x == 3:
                top = plus_ref[edge, :] + high_ref[edge, :]
            else:
                top = rim_ref[x - 1, pl.ds(r, 1), :]
            top = (top + from_up_ref[pl.ds(9 * x + r, 1), :]) * rim_mask_ref[x, pl.ds(r, 1), :]
            u.append(spread_y(u[0], top))
            cols.append(butterfly(u))
        for y in range(4):
            for x, t in enumerate(butterfly([cols[x][y] for x in range(4)])):
                q_s[c, (x * 4 + y) * 3 + g] = t


def mass_along_z(c, q_s, zv_s):
    for n in range(16):
        u = [q_s[c, 3 * n + g] for g in range(3)]
        u.append(next_lane(u[0]))
        for q, t in enumerate(along(interp_pair, butterfly(u))):
            zv_s[q, c, n] = t


def apply_kernel(
    minus_ref, plus_ref, inner_ref, rim_ref, low_ref, high_ref, from_down_ref, from_up_ref,
    mask_ref, face_mask_ref, rim_mask_ref, w_ref,
    own_ref, out_minus_ref, out_plus_ref, out_inner_ref, out_rim_ref,
    q_s, zv_s, xt_s, ya_s, zn_s,
):
    parts = (
        minus_ref, plus_ref, inner_ref, rim_ref, low_ref, high_ref, from_down_ref, from_up_ref,
    )

    def first(c, _):
        assemble(c, parts, mask_ref, face_mask_ref, rim_mask_ref, own_ref, q_s)
        mass_along_z(c, q_s, zv_s)
        return 0

    lax.fori_loop(0, 3, first, 0)

    def plane(z, _):
        for c in range(3):
            lines = [along(interp_pair, [zv_s[z, c, x * 4 + y] for y in range(4)]) for x in range(4)]
            for y in range(6):
                h = [lines[x][y] for x in range(4)]
                at = along(interp_pair, h)
                at = [at[p] * w_ref[p * 36 + y * 6 + z] for p in range(6)]
                for x, t in enumerate(interp_back(at)):
                    xt_s[c, x, y] = t
            for x in range(4):
                for y, t in enumerate(interp_back([xt_s[c, x, q] for q in range(6)])):
                    ya_s[z, c, x * 4 + y] = t
        return 0

    lax.fori_loop(0, 6, plane, 0)

    def back_z(c, _):
        for n in range(16):
            u = unbutterfly(interp_back([ya_s[q, c, n] for q in range(6)]))
            zn_s[c, n * 3] = u[0] + previous_lane(u[3])
            zn_s[c, n * 3 + 1] = u[1]
            zn_s[c, n * 3 + 2] = u[2]
        return 0

    lax.fori_loop(0, 3, back_z, 0)
    store_parts(
        lambda c, g: nodes_from(zn_s, c, g), out_minus_ref, out_plus_ref, out_inner_ref, out_rim_ref
    )


def total(t):
    return jnp.sum(jnp.sum(t, axis=0, keepdims=True), axis=1, keepdims=True)


def moments_kernel(
    minus_ref, plus_ref, inner_ref, rim_ref, low_ref, high_ref, from_down_ref, from_up_ref,
    mask_ref, face_mask_ref, rim_mask_ref, w_ref, r_ref, v_ref,
    own_ref, sums_ref, q_s, zv_s,
):
    parts = (
        minus_ref, plus_ref, inner_ref, rim_ref, low_ref, high_ref, from_down_ref, from_up_ref,
    )

    def first(c, _):
        assemble(c, parts, mask_ref, face_mask_ref, rim_mask_ref, own_ref, q_s)
        mass_along_z(c, q_s, zv_s)
        return 0

    lax.fori_loop(0, 3, first, 0)
    zero = jnp.zeros((8, 128), F32)

    def dots(n, s):
        s = list(s)
        for x in range(3):
            r, v, w = r_ref[x, n], v_ref[x, n], own_ref[x, n]
            s = [
                s[0] + r * r, s[1] + r * v, s[2] + v * v, s[3] + v * w, s[4] + w * w,
            ]
        return tuple(s)

    sums = lax.fori_loop(0, 27, dots, (zero,) * 5)

    def plane(z, s):
        s = list(s)
        for c in range(3):
            lines = [along(interp_pair, [zv_s[z, c, x * 4 + y] for y in range(4)]) for x in range(4)]
            for y in range(6):
                at = along(interp_pair, [lines[x][y] for x in range(4)])
                for p in range(6):
                    s[c] = s[c] + (at[p] * at[p]) * w_ref[p * 36 + y * 6 + z]
        return tuple(s)

    last = lax.fori_loop(0, 6, plane, (zero,) * 3)
    sums = list(sums) + [last[0] + last[1] + last[2]]
    lane = iotas(1)[1]
    row = jnp.zeros((1, 128), F32)
    for k in range(6):
        row = row + jnp.where(lane == k, total(sums[k]), 0.0)
    sums_ref[...] = jnp.broadcast_to(row, (128, 128))


def coefficients(mu):
    unit = mu[1] / mu[0]
    m = [None] * 6
    scale = 1.0 / mu[0]
    for k in range(6):
        m[k] = mu[k] * scale
        scale = scale / unit
    a0 = m[0] / m[1]
    rr1 = a0 * a0 * m[2] - 2.0 * a0 * m[1] + m[0]
    b0 = rr1 / m[0]
    d1 = [1.0 + b0, -a0]
    a1 = rr1 / (d1[0] * d1[0] * m[1] + 2.0 * d1[0] * d1[1] * m[2] + d1[1] * d1[1] * m[3])
    p1 = -(a0 + a1 * d1[0])
    p2 = -a1 * d1[1]
    rr2 = (
        m[0] + p1 * p1 * m[2] + p2 * p2 * m[4]
        + 2.0 * (p1 * m[1] + p2 * m[2] + p1 * p2 * m[3])
    )
    b1 = rr2 / rr1
    q = [1.0 + b1 * d1[0], p1 + b1 * d1[1], p2]
    a2 = rr2 / (
        q[0] * q[0] * m[1] + q[1] * q[1] * m[3] + q[2] * q[2] * m[5]
        + 2.0 * (q[0] * q[1] * m[2] + q[0] * q[2] * m[3] + q[1] * q[2] * m[4])
    )
    x = [a0 + a1 * d1[0] + a2 * q[0], a1 * d1[1] + a2 * q[1], a2 * q[2]]
    return [x[0] / unit, x[1] / (unit * unit), x[2] / (unit * unit * unit)]


def final_kernel(sums_ref, r_ref, v_ref, w_ref, d_ref, vel_ref, a_out, v_out, d_out, place):
    lane = iotas(1)[1]
    row = jnp.sum(sums_ref[...], axis=0, keepdims=True)
    mu = [
        jnp.broadcast_to(jnp.sum(jnp.where(lane == k, row, 0.0), axis=1, keepdims=True), (8, 128))
        for k in range(6)
    ]
    k0, k1, k2 = coefficients(mu)

    def body(c, _):
        for x in range(3):
            for b in range(3):
                for g in range(3):
                    n = c * 9 + b * 3 + g
                    place[x, g, pl.ds(b, 8, stride=3), :] = (
                        k0 * r_ref[x, n] + k1 * v_ref[x, n] + k2 * w_ref[x, n]
                    )
            for s in range(3):
                rows = slice(8 * s, 8 * s + 8)
                for v, t in enumerate(join_lanes([place[x, g, rows, :] for g in range(3)])):
                    lanes = slice(128 * v, 128 * v + 128)
                    a_out[c, x, rows, lanes] = t
                    new = vel_ref[c, x, rows, lanes] + step_size * t
                    v_out[c, x, rows, lanes] = new
                    d_out[c, x, rows, lanes] = d_ref[c, x, rows, lanes] + step_size * new
        return 0

    lax.fori_loop(0, 3, body, 0)


def call(kernel, outs, scratch, name, flops=0):
    def run(*args):
        moved = sum(a.size * 4 for a in args) + sum(4 * math.prod(s) for s in outs)
        return pl.pallas_call(
            kernel,
            out_shape=[jax.ShapeDtypeStruct(s, F32) for s in outs],
            scratch_shapes=[pltpu.VMEM(s, F32) for s in scratch],
            compiler_params=pltpu.CompilerParams(vmem_limit_bytes=VMEM_LIMIT),
            cost_estimate=pl.CostEstimate(flops=flops, bytes_accessed=moved, transcendentals=0),
            name=name,
        )(*args)

    return run


T = (8, 128)
FACE = (232, 128)
PARTS = [FACE, FACE, (2, 27) + T, (2, 16, 128)]


def solution(mesh):
    gx, gy = mesh.shape["gx"], mesh.shape["gy"]

    def moved(value, by_x, by_y):
        pairs = [
            (i * gy + j, ((i + by_x) % gx) * gy + (j + by_y) % gy)
            for i in range(gx)
            for j in range(gy)
        ]
        return lax.ppermute(value, ("gx", "gy"), pairs)

    def complete(parts):
        minus, plus_face, inner, rim = parts
        low = moved(plus_face, 1, 0)
        high = moved(minus, -1, 0)
        down, up = call(rows_kernel, [(40, 128), (40, 128)], [], "rows")(
            minus, plus_face, inner, rim, low, high
        )
        from_up = moved(down, 0, -1)
        from_down = moved(up, 0, 1)
        return (minus, plus_face, inner, rim, low, high, from_down, from_up)

    def on_device(displacement, velocity, energy, mass_weight, pinned):
        weight = mass_weight.reshape((216,) + T)
        dofs = energy.reshape((27,) + T)
        face, row, corner = call(pack_kernel, [(9, 24, 384), (27, 384), (9, 384)], [], "pack")(
            displacement, velocity, pinned
        )
        hx = moved(face, -1, 0)
        hy = moved(row, 0, -1)
        hc = moved(corner, -1, -1)
        nodes, mask = call(prep_kernel, [(6, 27) + T, (3, 27) + T], [(9, 3, 24, 128)], "prep", flops=4000000)(
            displacement, velocity, pinned
        )
        out = call(
            force_kernel,
            PARTS + [(27,) + T, (4, 16, 128), (27,) + T],
            [
                (9, 9) + T, (3, 40, 128), (6, 48) + T, (6, 6, 16) + T, (6, 6, 16) + T,
                (6, 3, 24) + T, (6, 9) + T, (6, 3) + T, (6, 3, 12) + T, (6, 3, 16) + T,
                (6, 3, 16) + T, (3, 48) + T, (6, 6) + T, (6, 18) + T,
                (3, 3, 24, 128),
            ],
            "force",
            flops=90000 * 1024,
        )(nodes, hx, hy, hc, dofs, weight)
        parts, (face_mask, rim_mask, energy_new) = out[:4], out[4:]
        masks = (mask, face_mask, rim_mask)
        scratch = [
            (3, 48) + T, (6, 3, 16) + T, (3, 4, 6) + T, (6, 3, 16) + T, (3, 48) + T,
        ]
        apply = call(apply_kernel, [(3, 27) + T] + PARTS, scratch, "apply", flops=13000 * 1024)
        out = apply(*complete(parts), *masks, weight)
        r, parts = out[0], out[1:]
        out = apply(*complete(parts), *masks, weight)
        v, parts = out[0], out[1:]
        w, sums = call(
            moments_kernel, [(3, 27) + T, (128, 128)], scratch[:2], "moments", flops=8000 * 1024
        )(*complete(parts), *masks, weight, r, v)
        sums = sums.reshape(gx * gy, -1, 128)
        sums = lax.all_to_all(sums, ("gx", "gy"), 0, 0).reshape(-1, 128)
        shape = displacement.shape
        acceleration, velocity_new, displacement_new = call(
            final_kernel, [shape] * 3, [(3, 3, 24, 128)], "final", flops=1000 * 1024
        )(sums, r, v, w, displacement, velocity)
        return acceleration, velocity_new, displacement_new, energy_new.reshape(energy.shape)

    spec = P(None, "gx", "gy", None)
    return jax.shard_map(
        on_device, mesh=mesh, in_specs=(spec,) * 5, out_specs=(spec,) * 4, check_vma=False
    )
```

time: 1010 us -> 96.8 us (0.10)
  local copies, waits for them, and re-layouts: 364 us -> 3.01 us
  blocking collectives: 321 us -> 20.2 us
  matrix products: 153 us -> 0 us
  other arithmetic: 88.8 us -> 0 us
  waiting for transfers between devices: 40 us -> 9.54 us
  Pallas kernels: 0 us -> 25.1 us
  starting transfers between devices: 25.2 us -> 38.1 us
    psum x5 -> x0, blocking collectives: 321 us -> none  [global_sum(): return lax.psum(value, ('gx', 'gy'))]
    dot_general x43 -> x0, matrix products: 153 us -> none  [the longest x14 55.3 us: along_x(): return jnp.einsum('qa,cabgjk->cqbgjk', matrix, operand, precision=HIGHEST)]
    transpose x25 -> x0, local copies, waits for them, and re-layouts: 144 us -> none  [the longest x16 104 us: merge_nodes(): jnp.moveaxis(lax.slice_in_dim(operand, 0, 3, axis=which_axis), which_axis...]
    slice x40 -> x0, local copies, waits for them, and re-layouts: 92.6 us -> none  [the longest x8 46.5 us: split_nodes(): lax.slice_in_dim(operand, 3, 3 * num_cells + 1, stride=3, axis=which_axis)]
    reshape x20 -> x0, local copies, waits for them, and re-layouts: 55.5 us -> none  [the longest x8 50.1 us: split_nodes(): lax.slice_in_dim(operand, 0, 3 * num_cells, axis=which_axis)]
    add x27 -> x0, other arithmetic: 51.5 us -> none  [the longest x12 50 us: merge_nodes(): return jnp.pad(head_part, pad_head) + shifted]
    unnamed x73 -> x14, local copies, waits for them, and re-layouts: 39.7 us -> 3.01 us
    ppermute x16 -> x15, waiting for transfers between devices: 40 us -> 9.54 us  [moved(): return lax.ppermute(value, ('gx', 'gy'), pairs)]
  transfers between devices with their start and end apart: 16 -> 15, of which waited for: 13 -> 8; matrix products, arithmetic and copies ran while one was open for 1% -> 0% of each run, Pallas kernels for 0% -> 2%
where the time goes in v1:
time: 96.8 us; the launch traced here: 96.6 us
  starting transfers between devices  38.1 us (39%)
  Pallas kernels  25.1 us (26%)
  blocking collectives  20.2 us (21%)
  waiting for transfers between devices  9.54 us (10%)
  local copies, waits for them, and re-layouts  3.01 us (3%)
    ppermute x15, starting transfers between devices, moved(): return lax.ppermute(value, ('gx', 'gy'), pairs)  38.1 us
    pallas_call x10, Pallas kernels, run(): pl.pallas_call(kernel, out_shape=[jax.ShapeDtypeStruct(s, F32) for s in o...  25.1 us
    all_to_all x1, blocking collectives, on_device(): sums = lax.all_to_all(sums, ('gx', 'gy'), 0, 0).reshape(-1, 128)  20.2 us
    ppermute x15, waiting for transfers between devices, moved(): return lax.ppermute(value, ('gx', 'gy'), pairs)  9.54 us
    unnamed x14, local copies, waits for them, and re-layouts  3.01 us
  transfers between devices with their start and end apart: 15, of which 8 were waited for; matrix products, arithmetic and copies ran while one was open for 0% of the time, Pallas kernels for 2%

profile of v1, /device:TPU:1, one launch (start us, length us, event | category | flops | bytes accessed | tf_op | source)
XLA Modules:
  0.0 96.6 jit_solution(15936714730273316847)
XLA Ops:
  0.6 0.0 copy-start
  0.6 0.0 copy-start.1
  0.7 1.0 %copy-done.1 = f32[3,3,24,384]{3,2,1,0:T(8,128)S(1)} copy-done((f32[3,3,24,384]{3,2,1,0:T(8,128)S(1)}, f32[3,3,24,384]{3,2,1,0:T(8,128)}, u32[]{:S(2)}) %copy-start.1) | copy-done | bytes 331800
  1.7 0.0 copy-start.3
  1.7 1.0 %copy-done.3 = f32[3,3,24,384]{3,2,1,0:T(8,128)S(1)} copy-done((f32[3,3,24,384]{3,2,1,0:T(8,128)S(1)}, f32[3,3,24,384]{3,2,1,0:T(8,128)}, u32[]{:S(2)}) %copy-start.3) | copy-done | bytes 331800
  2.7 0.0 copy-start.5
  2.7 1.0 %copy-done.5 = s32[3,3,24,384]{3,2,1,0:T(8,128)S(1)} copy-done((s32[3,3,24,384]{3,2,1,0:T(8,128)S(1)}, s32[3,3,24,384]{3,2,1,0:T(8,128)}, u32[]{:S(2)}) %copy-start.5) | copy-done | bytes 331800
  3.7 1.4 %collective-permute-start = (f32[9,24,384]{2,1,0:T(8,128)S(1)}, f32[9,24,384]{2,1,0:T(8,128)S(1)}, u32[]{:S(2)}, u32[]{:S(2)}) collective-permute-start(f32[9,24,384]{2,1,0:T(8,128)S(1)} %get-tuple-element.38), channel_id=1, source_target_pairs={{0,112},{1,113},{2,114},{3,115},{4,116},{5,117},{6,118},{7,119},{8... | collective-permute-start | bytes 995336 | tf_op jit(solution)/shard_map/ppermute | solution.py:701
  5.1 5.0 %collective-permute-start.1 = (f32[27,384]{1,0:T(8,128)S(1)}, f32[27,384]{1,0:T(8,128)S(1)}, u32[]{:S(2)}, u32[]{:S(2)}) collective-permute-start(f32[27,384]{1,0:T(8,128)S(1)} %get-tuple-element.39), channel_id=1, source_target_pairs={{0,15},{1,0},{2,1},{3,2},{4,3},{5,4},{6,5},{7,6},{8,7},{9,8},{10,9... | collective-permute-start | bytes 124424 | tf_op jit(solution)/shard_map/ppermute | solution.py:701
  10.1 0.0 copy-start.6
  10.1 4.2 %collective-permute-start.2 = (f32[9,384]{1,0:T(8,128)S(1)}, f32[9,384]{1,0:T(8,128)S(1)}, u32[]{:S(2)}, u32[]{:S(2)}) collective-permute-start(f32[9,384]{1,0:T(8,128)S(1)} %get-tuple-element.40), channel_id=1, source_target_pairs={{0,127},{1,112},{2,113},{3,114},{4,115},{5,116},{6,117},{7,118},{8... | collective-permute-start | bytes 41480 | tf_op jit(solution)/shard_map/ppermute | solution.py:701
  14.3 1.9 %prep.1 = (f32[6,27,8,128]{3,2,1,0:T(8,128)S(1)}, f32[3,27,8,128]{3,2,1,0:T(8,128)S(1)}) custom-call(f32[3,3,24,384]{3,2,1,0:T(8,128)S(1)} %copy-done.1, f32[3,3,24,384]{3,2,1,0:T(8,128)S(1)} %copy-done.3, s32[3,3,24,384]{3,2,1,0:T(8,128)S(1)} %copy-done.5), custom_call_target="tpu_custom_call" | custom-call | flops 4000000 | bytes 1990656 | tf_op jit(solution)/shard_map/prep/pallas_call | solution.py:675
  16.2 0.0 collective-permute-done.2.hc_ref
  16.2 0.0 collective-permute-done.1.hy_ref
  16.2 0.0 collective-permute-done.hx_ref
  16.3 0.0 copy-done
  16.3 0.0 copy-done.6
  16.3 15.1 %force.1 = (f32[232,128]{1,0:T(8,128)S(1)}, f32[232,128]{1,0:T(8,128)S(1)}, f32[2,27,8,128]{3,2,1,0:T(8,128)S(1)}, f32[2,16,128]{2,1,0:T(8,128)S(1)}, f32[27,8,1...) custom-call(f32[6,27,8,128]{3,2,1,0:T(8,128)S(1)} %get-tuple-element.37.u_ref, ...), custom_call_target="tpu_custom_call" | custom-call | flops 92160000 | bytes 2775040 | tf_op jit(solution)/shard_map/force/pallas_call | solution.py:675
  31.4 0.9 collective-permute-start.4
  32.2 0.9 collective-permute-start.3
  33.1 2.5 %collective-permute-done.4.got_high_ref.high_ref = f32[232,128]{1,0:T(8,128)S(1)} collective-permute-done((f32[232,128]{1,0:T(8,128)S(1)}, f32[232,128]{1,0:T(8,128)S(1)}, u32[]{:S(2)}, u32[]{:S(2)}) %collective-permute-start.4) | collective-permute-done | bytes 118816 | tf_op jit(solution)/shard_map/ppermute | solution.py:701
  35.6 0.0 collective-permute-done.3.got_low_ref.low_ref
  35.6 1.0 %collective-permute-start.5 = (f32[40,128]{1,0:T(8,128)S(1)}, f32[40,128]{1,0:T(8,128)S(1)}, u32[]{:S(2)}, u32[]{:S(2)}) collective-permute-start(f32[40,128]{1,0:T(8,128)S(1)} %get-tuple-element.45), channel_id=1, source_target_pairs={{0,1},{1,2},{2,3},{3,4},{4,5},{5,6},{6,7},{7,8},{8,9},{9,10},{10,1... | collective-permute-start | bytes 61448 | tf_op jit(solution)/shard_map/ppermute | solution.py:701
  36.6 3.9 %collective-permute-start.6 = (f32[40,128]{1,0:T(8,128)S(1)}, f32[40,128]{1,0:T(8,128)S(1)}, u32[]{:S(2)}, u32[]{:S(2)}) collective-permute-start(f32[40,128]{1,0:T(8,128)S(1)} %get-tuple-element.46), channel_id=1, source_target_pairs={{0,15},{1,0},{2,1},{3,2},{4,3},{5,4},{6,5},{7,6},{8,7},{9,8},{10,9... | collective-permute-start | bytes 61448 | tf_op jit(solution)/shard_map/ppermute | solution.py:701
  40.5 1.2 %collective-permute-done.5.from_down_ref = f32[40,128]{1,0:T(8,128)S(1)} collective-permute-done((f32[40,128]{1,0:T(8,128)S(1)}, f32[40,128]{1,0:T(8,128)S(1)}, u32[]{:S(2)}, u32[]{:S(2)}) %collective-permute-start.5) | collective-permute-done | bytes 20512 | tf_op jit(solution)/shard_map/ppermute | solution.py:701
  41.7 0.0 collective-permute-done.6.from_up_ref
  41.7 2.2 %apply.2 = (f32[3,27,8,128]{3,2,1,0:T(8,128)S(1)}, f32[232,128]{1,0:T(8,128)S(1)}, f32[232,128]{1,0:T(8,128)S(1)}, f32[2,27,8,128]{3,2,1,0:T(8,128)S(1)}, f32[2,16,128]{2,1,0:T(8,128)S(1)}) custom-call(f32[232,128]{1,0:T(8,128)S(1)} %get-tuple-element.41.minus_ref, f32[232,128]{1,0:T(8,128)S(1)} %get-tuple-element.42.plus_ref, ...), custom_call_target="tpu_custom_call" | custom-call | flops 13312000 | bytes 2920448 | tf_op jit(solution)/shard_map/apply/pallas_call | solution.py:675
  43.9 5.8 %collective-permute-start.8 = (f32[232,128]{1,0:T(8,128)S(1)}, f32[232,128]{1,0:T(8,128)S(1)}, u32[]{:S(2)}, u32[]{:S(2)}) collective-permute-start(f32[232,128]{1,0:T(8,128)S(1)} %get-tuple-element.50.minus_ref), channel_id=1, source_target_pairs={{0,112},{1,113},{2,114},{3,115},{4,116},{5,117},{6,118},{7,119},{8... | collective-permute-start | bytes 356360 | tf_op jit(solution)/shard_map/ppermute | solution.py:701
  49.7 0.0 collective-permute-start.7
  49.7 1.0 %collective-permute-done.8.got_high_ref.high_ref = f32[232,128]{1,0:T(8,128)S(1)} collective-permute-done((f32[232,128]{1,0:T(8,128)S(1)}, f32[232,128]{1,0:T(8,128)S(1)}, u32[]{:S(2)}, u32[]{:S(2)}) %collective-permute-start.8) | collective-permute-done | bytes 118816 | tf_op jit(solution)/shard_map/ppermute | solution.py:701
  50.7 0.9 collective-permute-done.7.got_low_ref.low_ref
  51.6 0.1 collective-permute-start.9
  51.6 5.1 %collective-permute-start.10 = (f32[40,128]{1,0:T(8,128)S(1)}, f32[40,128]{1,0:T(8,128)S(1)}, u32[]{:S(2)}, u32[]{:S(2)}) collective-permute-start(f32[40,128]{1,0:T(8,128)S(1)} %get-tuple-element.55), channel_id=1, source_target_pairs={{0,15},{1,0},{2,1},{3,2},{4,3},{5,4},{6,5},{7,6},{8,7},{9,8},{10,9... | collective-permute-start | bytes 61448 | tf_op jit(solution)/shard_map/ppermute | solution.py:701
  56.8 1.1 %collective-permute-done.9.from_down_ref = f32[40,128]{1,0:T(8,128)S(1)} collective-permute-done((f32[40,128]{1,0:T(8,128)S(1)}, f32[40,128]{1,0:T(8,128)S(1)}, u32[]{:S(2)}, u32[]{:S(2)}) %collective-permute-start.9) | collective-permute-done | bytes 20512 | tf_op jit(solution)/shard_map/ppermute | solution.py:701
  57.9 0.0 collective-permute-done.10.from_up_ref
  57.9 2.2 %apply.3 = (f32[3,27,8,128]{3,2,1,0:T(8,128)S(1)}, f32[232,128]{1,0:T(8,128)S(1)}, f32[232,128]{1,0:T(8,128)S(1)}, f32[2,27,8,128]{3,2,1,0:T(8,128)S(1)}, f32[2,16,128]{2,1,0:T(8,128)S(1)}) custom-call(f32[232,128]{1,0:T(8,128)S(1)} %get-tuple-element.50.minus_ref, f32[232,128]{1,0:T(8,128)S(1)} %get-tuple-element.51.plus_ref, ...), custom_call_target="tpu_custom_call" | custom-call | flops 13312000 | bytes 2920448 | tf_op jit(solution)/shard_map/apply/pallas_call | solution.py:675
  60.1 4.5 %collective-permute-start.12 = (f32[232,128]{1,0:T(8,128)S(1)}, f32[232,128]{1,0:T(8,128)S(1)}, u32[]{:S(2)}, u32[]{:S(2)}) collective-permute-start(f32[232,128]{1,0:T(8,128)S(1)} %get-tuple-element.56.minus_ref), channel_id=1, source_target_pairs={{0,112},{1,113},{2,114},{3,115},{4,116},{5,117},{6,118},{7,119},{8... | collective-permute-start | bytes 356360 | tf_op jit(solution)/shard_map/ppermute | solution.py:701
  64.6 0.0 collective-permute-start.11
  64.6 1.3 %collective-permute-done.12.got_high_ref.high_ref = f32[232,128]{1,0:T(8,128)S(1)} collective-permute-done((f32[232,128]{1,0:T(8,128)S(1)}, f32[232,128]{1,0:T(8,128)S(1)}, u32[]{:S(2)}, u32[]{:S(2)}) %collective-permute-start.12) | collective-permute-done | bytes 118816 | tf_op jit(solution)/shard_map/ppermute | solution.py:701
  65.9 0.5 collective-permute-done.11.got_low_ref.low_ref
  66.5 0.1 collective-permute-start.13
  66.6 5.2 %collective-permute-start.14 = (f32[40,128]{1,0:T(8,128)S(1)}, f32[40,128]{1,0:T(8,128)S(1)}, u32[]{:S(2)}, u32[]{:S(2)}) collective-permute-start(f32[40,128]{1,0:T(8,128)S(1)} %get-tuple-element.61), channel_id=1, source_target_pairs={{0,15},{1,0},{2,1},{3,2},{4,3},{5,4},{6,5},{7,6},{8,7},{9,8},{10,9... | collective-permute-start | bytes 61448 | tf_op jit(solution)/shard_map/ppermute | solution.py:701
  71.8 1.1 %collective-permute-done.13.from_down_ref = f32[40,128]{1,0:T(8,128)S(1)} collective-permute-done((f32[40,128]{1,0:T(8,128)S(1)}, f32[40,128]{1,0:T(8,128)S(1)}, u32[]{:S(2)}, u32[]{:S(2)}) %collective-permute-start.13) | collective-permute-done | bytes 20512 | tf_op jit(solution)/shard_map/ppermute | solution.py:701
  72.9 0.0 collective-permute-done.14.from_up_ref
  72.9 0.0 copy-start.2
  72.9 0.0 copy-start.4
  72.9 1.6 %moments.1 = (f32[3,27,8,128]{3,2,1,0:T(8,128)S(1)}, f32[128,128]{1,0:T(8,128)S(1)}) custom-call(f32[232,128]{1,0:T(8,128)S(1)} %get-tuple-element.56.minus_ref, f32[232,128]{1,0:T(8,128)S(1)} %get-tuple-element.57.plus_ref, f32[2,27,8,128]{3,2,1,0:T(8,128)S(1)} %get-tuple-element.58.inner_ref, f32[2,16,128]{2,1,0:T(8,128)S(1)} %get-tuple-element.59.rim_ref, ...), custom_call_target="tpu_custom_call" | custom-call | flops 8192000 | bytes 3174400 | tf_op jit(solution)/shard_map/moments/pallas_call | solution.py:675
  74.5 20.2 %all_to_all.5 = f32[128,1,128]{2,1,0:T(1,128)S(1)} all-to-all(f32[128,1,128]{2,1,0:T(1,128)S(1)} %bitcast.15), channel_id=1, replica_groups=mesh['gx'=8,'gy'=16] {'gx','gy'}, dimensions={0} | all-to-all | bytes 131072 | tf_op jit(solution)/shard_map/all_to_all | solution.py:752
  94.7 0.0 copy-done.2
  94.7 0.0 copy-done.4
  94.7 1.9 %final.1 = (f32[3,3,24,384]{3,2,1,0:T(8,128)}, f32[3,3,24,384]{3,2,1,0:T(8,128)}, f32[3,3,24,384]{3,2,1,0:T(8,128)}) custom-call(f32[128,128]{1,0:T(8,128)S(1)} %bitcast.13, f32[3,27,8,128]{3,2,1,0:T(8,128)S(1)} %get-tuple-element.62.r_ref, f32[3,27,8,128]{3,2,1,0:T(8,128)S(1)} %get-tuple-element.63.v_ref, f32[3,27,8,128]{3,2,1,0:T(8,128)S(1)} %get-tuple-element.65.w_ref, ...), custom_call_target="tpu_custom_call" | custom-call | flops 1024000 | bytes 2719744 | tf_op jit(solution)/shard_map/final/pallas_call | solution.py:675
  (4 shorter events, 0.1 us)
Async XLA Ops:
  0.6 15.6 %copy-start = (f32[216,1,8,128]{3,2,1,0:T(8,128)S(1)}, f32[216,1,8,128]{3,2,1,0:T(8,128)}, u32[]{:S(2)}) copy-start(f32[216,1,8,128]{3,2,1,0:T(8,128)} %param.8) | copy-start | bytes 2654212
  0.6 1.1 %copy-start.1 = (f32[3,3,24,384]{3,2,1,0:T(8,128)S(1)}, f32[3,3,24,384]{3,2,1,0:T(8,128)}, u32[]{:S(2)}) copy-start(f32[3,3,24,384]{3,2,1,0:T(8,128)} %d_ref.5) | copy-start | bytes 995332
  1.7 1.0 %copy-start.3 = (f32[3,3,24,384]{3,2,1,0:T(8,128)S(1)}, f32[3,3,24,384]{3,2,1,0:T(8,128)}, u32[]{:S(2)}) copy-start(f32[3,3,24,384]{3,2,1,0:T(8,128)} %vel_ref.1) | copy-start | bytes 995332
  2.7 1.0 %copy-start.5 = (s32[3,3,24,384]{3,2,1,0:T(8,128)S(1)}, s32[3,3,24,384]{3,2,1,0:T(8,128)}, u32[]{:S(2)}) copy-start(s32[3,3,24,384]{3,2,1,0:T(8,128)} %f_ref.3) | copy-start | bytes 995332
  3.7 12.6 %collective-permute-start = (f32[9,24,384]{2,1,0:T(8,128)S(1)}, f32[9,24,384]{2,1,0:T(8,128)S(1)}, u32[]{:S(2)}, u32[]{:S(2)}) collective-permute-start(f32[9,24,384]{2,1,0:T(8,128)S(1)} %get-tuple-element.38), channel_id=1, source_target_pairs={{0,112},{1,113},{2,114},{3,115},{4,116},{5,117},{6,118},{7,119},{8... | collective-permute-start | bytes 995336 | tf_op jit(solution)/shard_map/ppermute | solution.py:701
  5.1 11.1 %collective-permute-start.1 = (f32[27,384]{1,0:T(8,128)S(1)}, f32[27,384]{1,0:T(8,128)S(1)}, u32[]{:S(2)}, u32[]{:S(2)}) collective-permute-start(f32[27,384]{1,0:T(8,128)S(1)} %get-tuple-element.39), channel_id=1, source_target_pairs={{0,15},{1,0},{2,1},{3,2},{4,3},{5,4},{6,5},{7,6},{8,7},{9,8},{10,9... | collective-permute-start | bytes 124424 | tf_op jit(solution)/shard_map/ppermute | solution.py:701
  10.1 6.1 %copy-start.6 = (f32[27,1,8,128]{3,2,1,0:T(8,128)S(1)}, f32[27,1,8,128]{3,2,1,0:T(8,128)}, u32[]{:S(2)}) copy-start(f32[27,1,8,128]{3,2,1,0:T(8,128)} %param.7) | copy-start | bytes 331780
  10.1 6.1 %collective-permute-start.2 = (f32[9,384]{1,0:T(8,128)S(1)}, f32[9,384]{1,0:T(8,128)S(1)}, u32[]{:S(2)}, u32[]{:S(2)}) collective-permute-start(f32[9,384]{1,0:T(8,128)S(1)} %get-tuple-element.40), channel_id=1, source_target_pairs={{0,127},{1,112},{2,113},{3,114},{4,115},{5,116},{6,117},{7,118},{8... | collective-permute-start | bytes 41480 | tf_op jit(solution)/shard_map/ppermute | solution.py:701
  31.4 4.3 %collective-permute-start.4 = (f32[232,128]{1,0:T(8,128)S(1)}, f32[232,128]{1,0:T(8,128)S(1)}, u32[]{:S(2)}, u32[]{:S(2)}) collective-permute-start(f32[232,128]{1,0:T(8,128)S(1)} %get-tuple-element.41.minus_ref), channel_id=1, source_target_pairs={{0,112},{1,113},{2,114},{3,115},{4,116},{5,117},{6,118},{7,119},{8... | collective-permute-start | bytes 356360 | tf_op jit(solution)/shard_map/ppermute | solution.py:701
  32.2 3.4 %collective-permute-start.3 = (f32[232,128]{1,0:T(8,128)S(1)}, f32[232,128]{1,0:T(8,128)S(1)}, u32[]{:S(2)}, u32[]{:S(2)}) collective-permute-start(f32[232,128]{1,0:T(8,128)S(1)} %get-tuple-element.42.plus_ref), channel_id=1, source_target_pairs={{0,16},{1,17},{2,18},{3,19},{4,20},{5,21},{6,22},{7,23},{8,24},{9,... | collective-permute-start | bytes 356360 | tf_op jit(solution)/shard_map/ppermute | solution.py:701
  35.6 6.0 %collective-permute-start.5 = (f32[40,128]{1,0:T(8,128)S(1)}, f32[40,128]{1,0:T(8,128)S(1)}, u32[]{:S(2)}, u32[]{:S(2)}) collective-permute-start(f32[40,128]{1,0:T(8,128)S(1)} %get-tuple-element.45), channel_id=1, source_target_pairs={{0,1},{1,2},{2,3},{3,4},{4,5},{5,6},{6,7},{7,8},{8,9},{9,10},{10,1... | collective-permute-start | bytes 61448 | tf_op jit(solution)/shard_map/ppermute | solution.py:701
  36.6 5.0 %collective-permute-start.6 = (f32[40,128]{1,0:T(8,128)S(1)}, f32[40,128]{1,0:T(8,128)S(1)}, u32[]{:S(2)}, u32[]{:S(2)}) collective-permute-start(f32[40,128]{1,0:T(8,128)S(1)} %get-tuple-element.46), channel_id=1, source_target_pairs={{0,15},{1,0},{2,1},{3,2},{4,3},{5,4},{6,5},{7,6},{8,7},{9,8},{10,9... | collective-permute-start | bytes 61448 | tf_op jit(solution)/shard_map/ppermute | solution.py:701
  43.9 6.8 %collective-permute-start.8 = (f32[232,128]{1,0:T(8,128)S(1)}, f32[232,128]{1,0:T(8,128)S(1)}, u32[]{:S(2)}, u32[]{:S(2)}) collective-permute-start(f32[232,128]{1,0:T(8,128)S(1)} %get-tuple-element.50.minus_ref), channel_id=1, source_target_pairs={{0,112},{1,113},{2,114},{3,115},{4,116},{5,117},{6,118},{7,119},{8... | collective-permute-start | bytes 356360 | tf_op jit(solution)/shard_map/ppermute | solution.py:701
  49.7 1.8 %collective-permute-start.7 = (f32[232,128]{1,0:T(8,128)S(1)}, f32[232,128]{1,0:T(8,128)S(1)}, u32[]{:S(2)}, u32[]{:S(2)}) collective-permute-start(f32[232,128]{1,0:T(8,128)S(1)} %get-tuple-element.51.plus_ref), channel_id=1, source_target_pairs={{0,16},{1,17},{2,18},{3,19},{4,20},{5,21},{6,22},{7,23},{8,24},{9,... | collective-permute-start | bytes 356360 | tf_op jit(solution)/shard_map/ppermute | solution.py:701
  51.6 6.3 %collective-permute-start.9 = (f32[40,128]{1,0:T(8,128)S(1)}, f32[40,128]{1,0:T(8,128)S(1)}, u32[]{:S(2)}, u32[]{:S(2)}) collective-permute-start(f32[40,128]{1,0:T(8,128)S(1)} %get-tuple-element.54), channel_id=1, source_target_pairs={{0,1},{1,2},{2,3},{3,4},{4,5},{5,6},{6,7},{7,8},{8,9},{9,10},{10,1... | collective-permute-start | bytes 61448 | tf_op jit(solution)/shard_map/ppermute | solution.py:701
  51.6 6.2 %collective-permute-start.10 = (f32[40,128]{1,0:T(8,128)S(1)}, f32[40,128]{1,0:T(8,128)S(1)}, u32[]{:S(2)}, u32[]{:S(2)}) collective-permute-start(f32[40,128]{1,0:T(8,128)S(1)} %get-tuple-element.55), channel_id=1, source_target_pairs={{0,15},{1,0},{2,1},{3,2},{4,3},{5,4},{6,5},{7,6},{8,7},{9,8},{10,9... | collective-permute-start | bytes 61448 | tf_op jit(solution)/shard_map/ppermute | solution.py:701
  60.1 5.8 %collective-permute-start.12 = (f32[232,128]{1,0:T(8,128)S(1)}, f32[232,128]{1,0:T(8,128)S(1)}, u32[]{:S(2)}, u32[]{:S(2)}) collective-permute-start(f32[232,128]{1,0:T(8,128)S(1)} %get-tuple-element.56.minus_ref), channel_id=1, source_target_pairs={{0,112},{1,113},{2,114},{3,115},{4,116},{5,117},{6,118},{7,119},{8... | collective-permute-start | bytes 356360 | tf_op jit(solution)/shard_map/ppermute | solution.py:701
  64.6 1.8 %collective-permute-start.11 = (f32[232,128]{1,0:T(8,128)S(1)}, f32[232,128]{1,0:T(8,128)S(1)}, u32[]{:S(2)}, u32[]{:S(2)}) collective-permute-start(f32[232,128]{1,0:T(8,128)S(1)} %get-tuple-element.57.plus_ref), channel_id=1, source_target_pairs={{0,16},{1,17},{2,18},{3,19},{4,20},{5,21},{6,22},{7,23},{8,24},{9,... | collective-permute-start | bytes 356360 | tf_op jit(solution)/shard_map/ppermute | solution.py:701
  66.5 6.4 %collective-permute-start.13 = (f32[40,128]{1,0:T(8,128)S(1)}, f32[40,128]{1,0:T(8,128)S(1)}, u32[]{:S(2)}, u32[]{:S(2)}) collective-permute-start(f32[40,128]{1,0:T(8,128)S(1)} %get-tuple-element.60), channel_id=1, source_target_pairs={{0,1},{1,2},{2,3},{3,4},{4,5},{5,6},{6,7},{7,8},{8,9},{9,10},{10,1... | collective-permute-start | bytes 61448 | tf_op jit(solution)/shard_map/ppermute | solution.py:701
  66.6 6.3 %collective-permute-start.14 = (f32[40,128]{1,0:T(8,128)S(1)}, f32[40,128]{1,0:T(8,128)S(1)}, u32[]{:S(2)}, u32[]{:S(2)}) collective-permute-start(f32[40,128]{1,0:T(8,128)S(1)} %get-tuple-element.61), channel_id=1, source_target_pairs={{0,15},{1,0},{2,1},{3,2},{4,3},{5,4},{6,5},{7,6},{8,7},{9,8},{10,9... | collective-permute-start | bytes 61448 | tf_op jit(solution)/shard_map/ppermute | solution.py:701
  72.9 21.8 %copy-start.2 = (f32[3,3,24,384]{3,2,1,0:T(8,128)S(1)}, f32[3,3,24,384]{3,2,1,0:T(8,128)}, u32[]{:S(2)}) copy-start(f32[3,3,24,384]{3,2,1,0:T(8,128)} %d_ref.5) | copy-start | bytes 995332
  72.9 21.8 %copy-start.4 = (f32[3,3,24,384]{3,2,1,0:T(8,128)S(1)}, f32[3,3,24,384]{3,2,1,0:T(8,128)}, u32[]{:S(2)}) copy-start(f32[3,3,24,384]{3,2,1,0:T(8,128)} %vel_ref.1) | copy-start | bytes 995332

commit v2 on v1

--- a/solution.py
+++ b/solution.py
@@ -12,7 +12,7 @@
 viscosity = 0.3
 gamma_less = 0.4
 F32 = jnp.float32
-VMEM_LIMIT = 48 * 1024 * 1024
+VMEM_LIMIT = 32 * 1024 * 1024
 
 
 def tables():
@@ -172,16 +172,26 @@
     return pltpu.roll(x, 1, 1)
 
 
-def pack_kernel(d_ref, v_ref, f_ref, x_ref, y_ref, c_ref):
+def pack_kernel(d_ref, v_ref, f_ref, x_ref, y_ref, c_ref, face, face_f, low, low_f, sems):
+    copies = []
     for n, ref in enumerate((d_ref, v_ref, f_ref)):
+        to_face, to_low = (face.at[n], low.at[n]) if n < 2 else (face_f, low_f)
+        copies.append(pltpu.make_async_copy(ref.at[:, 0], to_face, sems.at[2 * n]))
+        copies.append(pltpu.make_async_copy(ref.at[:, :, 0:8], to_low, sems.at[2 * n + 1]))
+    for copy in copies:
+        copy.start()
+    for copy in copies:
+        copy.wait()
+    for n in range(3):
         for c in range(3):
             k = 3 * n + c
-            face = ref[c, 0].astype(F32)
-            x_ref[k] = face
-            c_ref[k : k + 1, :] = face[0:1]
+            layer = (face[n, c] if n < 2 else face_f[c]).astype(F32)
+            x_ref[k] = layer
+            c_ref[k : k + 1, :] = layer[0:1]
             for x in range(3):
                 r = 9 * x + k
-                y_ref[r : r + 1, :] = ref[c, x, 0:1, :].astype(F32)
+                row = low[n, c, x, 0:1, :] if n < 2 else low_f[c, x, 0:1, :]
+                y_ref[r : r + 1, :] = row.astype(F32)
 
 
 def element_rows(load, place):
@@ -192,7 +202,7 @@
     return [place[g, pl.ds(b, 8, stride=3), :] for b in range(3) for g in range(3)]
 
 
-def prep_kernel(d_ref, v_ref, f_ref, u_ref, m_ref, place):
+def prep_kernel(d_ref, v_ref, f_ref, e_ref, w_ref, u_ref, m_ref, eq_ref, lump_ref, place, ez_s, ey_s):
     def body(c, _):
         for x in range(3):
             for k, ref in enumerate((d_ref, v_ref, f_ref)):
@@ -207,6 +217,47 @@
         return 0
 
     lax.fori_loop(0, 3, body, 0)
+    for n in range(9):
+        for q, t in enumerate(thermo_along([gamma_less * e_ref[3 * n + g] for g in range(3)])):
+            ez_s[q, n] = t
+
+    def plane(z, _):
+        for x in range(3):
+            for q, t in enumerate(thermo_along([ez_s[z, 3 * x + y] for y in range(3)])):
+                ey_s[q, x] = t
+        for y in range(6):
+            for q, t in enumerate(thermo_along([ey_s[y, x] for x in range(3)])):
+                eq_ref[q * 36 + y * 6 + z] = t
+        return 0
+
+    lax.fori_loop(0, 6, plane, 0)
+    project(w_ref, ez_s, ey_s, lump_ref)
+
+
+def project(at_ref, z_s, x_s, out_ref):
+    def plane(z, _):
+        for y in range(6):
+            for x, t in enumerate(thermo_back([at_ref[p * 36 + y * 6 + z] for p in range(6)])):
+                x_s[y, x] = t
+        for x in range(3):
+            for y, t in enumerate(thermo_back([x_s[q, x] for q in range(6)])):
+                z_s[z, 3 * x + y] = t
+        return 0
+
+    lax.fori_loop(0, 6, plane, 0)
+    for n in range(9):
+        for g, t in enumerate(thermo_back([z_s[q, n] for q in range(6)])):
+            out_ref[3 * n + g] = t
+
+
+def energy_kernel(power_ref, lump_ref, e_ref, out_ref, sum_s, z_s, x_s):
+    project(power_ref, z_s, x_s, sum_s)
+
+    def body(n, _):
+        out_ref[n] = e_ref[n] + step_size * (sum_s[n] / lump_ref[n])
+        return 0
+
+    lax.fori_loop(0, 27, body, 0)
 
 
 def point(jac, vel, energy, mass):
@@ -278,9 +329,9 @@
 
 
 def force_kernel(
-    u_ref, hx_ref, hy_ref, hc_ref, e_ref, w_ref,
-    minus_ref, plus_ref, inner_ref, rim_ref, face_mask_ref, rim_mask_ref, energy_ref,
-    hx_s, hy_s, q_s, zv_s, zs_s, w_s, ez_s, ey_s, xt_s, ya_s, yb_s, zn_s, px_s, py_s, place,
+    u_ref, hx_ref, hy_ref, hc_ref, eq_ref, w_ref,
+    minus_ref, plus_ref, inner_ref, rim_ref, face_mask_ref, rim_mask_ref, power_ref,
+    hx_s, hy_s, q_s, zv_s, zs_s, w_s, xt_s, ya_s, yb_s, zn_s, place,
 ):
     rows = [
         jnp.concatenate(
@@ -341,9 +392,6 @@
         return 0
 
     lax.fori_loop(0, 6, along_z, 0)
-    for n in range(9):
-        for q, t in enumerate(thermo_along([e_ref[3 * n + g] for g in range(3)])):
-            ez_s[q, n] = t
 
     def plane(z, _):
         def along_y(c, _):
@@ -359,14 +407,8 @@
             return 0
 
         lax.fori_loop(0, 6, along_y, 0)
-        for x in range(3):
-            for q, t in enumerate(thermo_along([ez_s[z, 3 * x + y] for y in range(3)])):
-                ey_s[q, x] = t
 
         def line(y, _):
-            energy = thermo_along([gamma_less * ey_s[y, x] for x in range(3)])
-            power = [None] * 6
-            mass = [None] * 6
             back = [[[None] * 4 for _ in range(3)] for _ in range(3)]
             for q in range(3):
                 grads = [[[None] * 3 for _ in range(6)] for _ in range(2)]
@@ -380,8 +422,8 @@
                 flux = []
                 for side in range(2):
                     p = q if side == 0 else 5 - q
-                    mass[p] = w_ref[p * 36 + y * 6 + z]
-                    f, power[p] = point(grads[side][:3], grads[side][3:], energy[p], mass[p])
+                    n = p * 36 + y * 6 + z
+                    f, power_ref[n] = point(grads[side][:3], grads[side][3:], eq_ref[n], w_ref[n])
                     flux.append(f)
                 for c in range(3):
                     for f in range(3):
@@ -399,10 +441,6 @@
                 for f in range(3):
                     for x in range(4):
                         xt_s[y, f, c * 4 + x] = back[c][f][x]
-            for x, t in enumerate(thermo_back(power)):
-                px_s[y, x] = t
-            for x, t in enumerate(thermo_back(mass)):
-                px_s[y, 3 + x] = t
             return 0
 
         lax.fori_loop(0, 6, line, 0)
@@ -418,18 +456,9 @@
             return 0
 
         lax.fori_loop(0, 3, back_y, 0)
-        for x in range(6):
-            for y, t in enumerate(thermo_back([px_s[q, x] for q in range(6)])):
-                py_s[z, 3 * x + y] = t
         return 0
 
     lax.fori_loop(0, 6, plane, 0)
-
-    for n in range(9):
-        work = thermo_back([py_s[q, n] for q in range(6)])
-        lump = thermo_back([py_s[q, 9 + n] for q in range(6)])
-        for g in range(3):
-            energy_ref[3 * n + g] = e_ref[3 * n + g] + step_size * (work[g] / lump[g])
 
     def back_z(c, _):
         for n in range(16):
@@ -608,7 +637,7 @@
     row = jnp.zeros((1, 128), F32)
     for k in range(6):
         row = row + jnp.where(lane == k, total(sums[k]), 0.0)
-    sums_ref[...] = jnp.broadcast_to(row, (128, 128))
+    sums_ref[...] = jnp.broadcast_to(row, sums_ref.shape)
 
 
 def coefficients(mu):
@@ -639,7 +668,9 @@
     return [x[0] / unit, x[1] / (unit * unit), x[2] / (unit * unit * unit)]
 
 
-def final_kernel(sums_ref, r_ref, v_ref, w_ref, d_ref, vel_ref, a_out, v_out, d_out, place):
+def final_kernel(
+    sums_ref, r_ref, v_ref, w_ref, d_ref, vel_ref, a_out, v_out, d_out, place, a_s, v_s, d_s, sems
+):
     lane = iotas(1)[1]
     row = jnp.sum(sums_ref[...], axis=0, keepdims=True)
     mu = [
@@ -647,6 +678,13 @@
         for k in range(6)
     ]
     k0, k1, k2 = coefficients(mu)
+
+    def copies(c):
+        pairs = ((a_s, a_out), (v_s, v_out), (d_s, d_out))
+        return [
+            pltpu.make_async_copy(src.at[c], dst.at[c], sems.at[c, i])
+            for i, (src, dst) in enumerate(pairs)
+        ]
 
     def body(c, _):
         for x in range(3):
@@ -660,25 +698,31 @@
                 rows = slice(8 * s, 8 * s + 8)
                 for v, t in enumerate(join_lanes([place[x, g, rows, :] for g in range(3)])):
                     lanes = slice(128 * v, 128 * v + 128)
-                    a_out[c, x, rows, lanes] = t
+                    a_s[c, x, rows, lanes] = t
                     new = vel_ref[c, x, rows, lanes] + step_size * t
-                    v_out[c, x, rows, lanes] = new
-                    d_out[c, x, rows, lanes] = d_ref[c, x, rows, lanes] + step_size * new
+                    v_s[c, x, rows, lanes] = new
+                    d_s[c, x, rows, lanes] = d_ref[c, x, rows, lanes] + step_size * new
+        for copy in copies(c):
+            copy.start()
         return 0
 
     lax.fori_loop(0, 3, body, 0)
-
-
-def call(kernel, outs, scratch, name, flops=0):
+    for c in range(3):
+        for copy in copies(c):
+            copy.wait()
+
+
+def call(kernel, outs, scratch, name, flops=0, **more):
     def run(*args):
         moved = sum(a.size * 4 for a in args) + sum(4 * math.prod(s) for s in outs)
         return pl.pallas_call(
             kernel,
             out_shape=[jax.ShapeDtypeStruct(s, F32) for s in outs],
-            scratch_shapes=[pltpu.VMEM(s, F32) for s in scratch],
+            scratch_shapes=[pltpu.VMEM(s, F32) if isinstance(s, tuple) else s for s in scratch],
             compiler_params=pltpu.CompilerParams(vmem_limit_bytes=VMEM_LIMIT),
             cost_estimate=pl.CostEstimate(flops=flops, bytes_accessed=moved, transcendentals=0),
             name=name,
+            **more,
         )(*args)
 
     return run
@@ -714,28 +758,43 @@
     def on_device(displacement, velocity, energy, mass_weight, pinned):
         weight = mass_weight.reshape((216,) + T)
         dofs = energy.reshape((27,) + T)
-        face, row, corner = call(pack_kernel, [(9, 24, 384), (27, 384), (9, 384)], [], "pack")(
-            displacement, velocity, pinned
-        )
+        flags = pinned.dtype
+        face, row, corner = call(
+            pack_kernel,
+            [(9, 24, 384), (27, 384), (9, 384)],
+            [
+                (2, 3, 24, 384), pltpu.VMEM((3, 24, 384), flags), (2, 3, 3, 8, 384),
+                pltpu.VMEM((3, 3, 8, 384), flags), pltpu.SemaphoreType.DMA((6,)),
+            ],
+            "pack",
+            in_specs=[pl.BlockSpec(memory_space=pltpu.HBM)] * 3,
+        )(displacement, velocity, pinned)
         hx = moved(face, -1, 0)
         hy = moved(row, 0, -1)
         hc = moved(corner, -1, -1)
-        nodes, mask = call(prep_kernel, [(6, 27) + T, (3, 27) + T], [(9, 3, 24, 128)], "prep", flops=4000000)(
-            displacement, velocity, pinned
-        )
+        nodes, mask, heat, lump = call(
+            prep_kernel,
+            [(6, 27) + T, (3, 27) + T, (216,) + T, (27,) + T],
+            [(9, 3, 24, 128), (6, 9) + T, (6, 3) + T],
+            "prep",
+            flops=4000 * 1024,
+        )(displacement, velocity, pinned, dofs, weight)
         out = call(
             force_kernel,
-            PARTS + [(27,) + T, (4, 16, 128), (27,) + T],
+            PARTS + [(27,) + T, (4, 16, 128), (216,) + T],
             [
                 (9, 9) + T, (3, 40, 128), (6, 48) + T, (6, 6, 16) + T, (6, 6, 16) + T,
-                (6, 3, 24) + T, (6, 9) + T, (6, 3) + T, (6, 3, 12) + T, (6, 3, 16) + T,
-                (6, 3, 16) + T, (3, 48) + T, (6, 6) + T, (6, 18) + T,
-                (3, 3, 24, 128),
+                (6, 3, 24) + T, (6, 3, 12) + T, (6, 3, 16) + T,
+                (6, 3, 16) + T, (3, 48) + T, (3, 3, 24, 128),
             ],
             "force",
             flops=90000 * 1024,
-        )(nodes, hx, hy, hc, dofs, weight)
-        parts, (face_mask, rim_mask, energy_new) = out[:4], out[4:]
+        )(nodes, hx, hy, hc, heat, weight)
+        parts, (face_mask, rim_mask, power) = out[:4], out[4:]
+        (energy_new,) = call(
+            energy_kernel, [(27,) + T], [(27,) + T, (6, 9) + T, (6, 3) + T], "energy",
+            flops=2000 * 1024,
+        )(power, lump, dofs)
         masks = (mask, face_mask, rim_mask)
         scratch = [
             (3, 48) + T, (6, 3, 16) + T, (3, 4, 6) + T, (6, 3, 16) + T, (3, 48) + T,
@@ -746,13 +805,18 @@
         out = apply(*complete(parts), *masks, weight)
         v, parts = out[0], out[1:]
         w, sums = call(
-            moments_kernel, [(3, 27) + T, (128, 128)], scratch[:2], "moments", flops=8000 * 1024
+            moments_kernel, [(3, 27) + T, (gx * gy, 128)], scratch[:2], "moments", flops=8000 * 1024
         )(*complete(parts), *masks, weight, r, v)
         sums = sums.reshape(gx * gy, -1, 128)
         sums = lax.all_to_all(sums, ("gx", "gy"), 0, 0).reshape(-1, 128)
         shape = displacement.shape
         acceleration, velocity_new, displacement_new = call(
-            final_kernel, [shape] * 3, [(3, 3, 24, 128)], "final", flops=1000 * 1024
+            final_kernel,
+            [shape] * 3,
+            [(3, 3, 24, 128), shape, shape, shape, pltpu.SemaphoreType.DMA((3, 3))],
+            "final",
+            flops=1000 * 1024,
+            out_specs=[pl.BlockSpec(memory_space=pltpu.HBM)] * 3,
         )(sums, r, v, w, displacement, velocity)
         return acceleration, velocity_new, displacement_new, energy_new.reshape(energy.shape)
 

time: 96.8 us -> 96.7 us (level)
  blocking collectives: 20.2 us -> 0 us
  starting transfers between devices: 38.1 us -> 48.4 us
  waiting for transfers between devices: 9.54 us -> 17.9 us
  Pallas kernels: 25.1 us -> 26.4 us
    all_to_all x1 -> x0, blocking collectives: 20.2 us -> none  [on_device(): sums = lax.all_to_all(sums, ('gx', 'gy'), 0, 0).reshape(-1, 128)]
    all_to_all x0 -> x1, starting transfers between devices: none -> 10.8 us  [on_device(): sums = lax.all_to_all(sums, ('gx', 'gy'), 0, 0).reshape(-1, 128)]
    all_to_all x0 -> x1, waiting for transfers between devices: none -> 8.33 us  [on_device(): sums = lax.all_to_all(sums, ('gx', 'gy'), 0, 0).reshape(-1, 128)]
    pallas_call x10 -> x11, Pallas kernels: 25.1 us -> 26.4 us  [run(): pl.pallas_call(kernel, out_shape=[jax.ShapeDtypeStruct(s, F32) for s in o...]
  transfers between devices with their start and end apart: 15 -> 16, of which waited for: 8 -> 9; matrix products, arithmetic and copies ran while one was open for 0% -> 0% of each run, Pallas kernels for 2% -> 4%
where the time goes in v2:
time: 96.7 us; the launch traced here: 96.5 us
  starting transfers between devices  48.4 us (50%)
  Pallas kernels  26.4 us (27%)
  waiting for transfers between devices  17.9 us (19%)
  local copies, waits for them, and re-layouts  3.01 us (3%)
    ppermute x15, starting transfers between devices, moved(): return lax.ppermute(value, ('gx', 'gy'), pairs)  37.6 us
    pallas_call x11, Pallas kernels, run(): pl.pallas_call(kernel, out_shape=[jax.ShapeDtypeStruct(s, F32) for s in o...  26.4 us
    all_to_all x1, starting transfers between devices, on_device(): sums = lax.all_to_all(sums, ('gx', 'gy'), 0, 0).reshape(-1, 128)  10.8 us
    ppermute x15, waiting for transfers between devices, moved(): return lax.ppermute(value, ('gx', 'gy'), pairs)  9.54 us
    all_to_all x1, waiting for transfers between devices, on_device(): sums = lax.all_to_all(sums, ('gx', 'gy'), 0, 0).reshape(-1, 128)  8.33 us
    unnamed x14, local copies, waits for them, and re-layouts  3.01 us
  transfers between devices with their start and end apart: 16, of which 9 were waited for; matrix products, arithmetic and copies ran while one was open for 0% of the time, Pallas kernels for 4%

profile of v2, /device:TPU:1, one launch (start us, length us, event | category | flops | bytes accessed | tf_op | source)
XLA Modules:
  0.0 96.5 jit_solution(15205719583137605046)
XLA Ops:
  0.6 0.0 copy-start
  0.6 0.0 copy-start.1
  0.7 1.0 %copy-done.1 = f32[3,3,24,384]{3,2,1,0:T(8,128)S(1)} copy-done((f32[3,3,24,384]{3,2,1,0:T(8,128)S(1)}, f32[3,3,24,384]{3,2,1,0:T(8,128)}, u32[]{:S(2)}) %copy-start.1) | copy-done | bytes 331800
  1.7 0.0 copy-start.3
  1.7 1.0 %copy-done.3 = f32[3,3,24,384]{3,2,1,0:T(8,128)S(1)} copy-done((f32[3,3,24,384]{3,2,1,0:T(8,128)S(1)}, f32[3,3,24,384]{3,2,1,0:T(8,128)}, u32[]{:S(2)}) %copy-start.3) | copy-done | bytes 331800
  2.7 0.0 copy-start.5
  2.7 1.0 %copy-done.5 = s32[3,3,24,384]{3,2,1,0:T(8,128)S(1)} copy-done((s32[3,3,24,384]{3,2,1,0:T(8,128)S(1)}, s32[3,3,24,384]{3,2,1,0:T(8,128)}, u32[]{:S(2)}) %copy-start.5) | copy-done | bytes 331800
  3.6 0.0 copy-start.6
  3.6 0.3 pack.1
  3.9 1.4 %collective-permute-start = (f32[9,24,384]{2,1,0:T(8,128)S(1)}, f32[9,24,384]{2,1,0:T(8,128)S(1)}, u32[]{:S(2)}, u32[]{:S(2)}) collective-permute-start(f32[9,24,384]{2,1,0:T(8,128)S(1)} %get-tuple-element.40), channel_id=1, source_target_pairs={{0,112},{1,113},{2,114},{3,115},{4,116},{5,117},{6,118},{7,119},{8... | collective-permute-start | bytes 995336 | tf_op jit(solution)/shard_map/ppermute | solution.py:745
  5.4 5.0 %collective-permute-start.1 = (f32[27,384]{1,0:T(8,128)S(1)}, f32[27,384]{1,0:T(8,128)S(1)}, u32[]{:S(2)}, u32[]{:S(2)}) collective-permute-start(f32[27,384]{1,0:T(8,128)S(1)} %get-tuple-element.41), channel_id=1, source_target_pairs={{0,15},{1,0},{2,1},{3,2},{4,3},{5,4},{6,5},{7,6},{8,7},{9,8},{10,9... | collective-permute-start | bytes 124424 | tf_op jit(solution)/shard_map/ppermute | solution.py:745
  10.4 4.2 %collective-permute-start.2 = (f32[9,384]{1,0:T(8,128)S(1)}, f32[9,384]{1,0:T(8,128)S(1)}, u32[]{:S(2)}, u32[]{:S(2)}) collective-permute-start(f32[9,384]{1,0:T(8,128)S(1)} %get-tuple-element.42), channel_id=1, source_target_pairs={{0,127},{1,112},{2,113},{3,114},{4,115},{5,116},{6,117},{7,118},{8... | collective-permute-start | bytes 41480 | tf_op jit(solution)/shard_map/ppermute | solution.py:745
  14.6 0.0 copy-done
  14.6 0.0 copy-done.6
  14.6 2.3 %prep.1 = (f32[6,27,8,128]{3,2,1,0:T(8,128)S(1)}, f32[3,27,8,128]{3,2,1,0:T(8,128)S(1)}, f32[216,8,128]{2,1,0:T(8,128)S(1)}, f32[27,8,128]{2,1,0:T(8,128)S(1)}) custom-call(f32[3,3,24,384]{3,2,1,0:T(8,128)S(1)} %copy-done.1, f32[3,3,24,384]{3,2,1,0:T(8,128)S(1)} %copy-done.3, s32[3,3,24,384]{3,2,1,0:T(8,128)S(1)} %copy-done.5, f32[27,8,128]{2,1,0:T(8,128)S(1)} %bitcast.14, ...), custom_call_target="tpu_custom_call" | custom-call | flops 4096000 | bytes 3981312 | tf_op jit(solution)/shard_map/prep/pallas_call | solution.py:718
  16.9 0.0 collective-permute-done.2.hc_ref
  16.9 0.0 collective-permute-done.1.hy_ref
  16.9 0.0 collective-permute-done.hx_ref
  16.9 14.1 %force.1 = (f32[232,128]{1,0:T(8,128)S(1)}, f32[232,128]{1,0:T(8,128)S(1)}, f32[2,27,8,128]{3,2,1,0:T(8,128)S(1)}, f32[2,16,128]{2,1,0:T(8,128)S(1)}, f32[27,8,1...) custom-call(f32[6,27,8,128]{3,2,1,0:T(8,128)S(1)} %get-tuple-element.39.u_ref, ...), custom_call_target="tpu_custom_call" | custom-call | flops 92160000 | bytes 4323328 | tf_op jit(solution)/shard_map/force/pallas_call | solution.py:718
  31.1 0.5 collective-permute-start.4
  31.5 1.3 %collective-permute-start.3 = (f32[232,128]{1,0:T(8,128)S(1)}, f32[232,128]{1,0:T(8,128)S(1)}, u32[]{:S(2)}, u32[]{:S(2)}) collective-permute-start(f32[232,128]{1,0:T(8,128)S(1)} %get-tuple-element.45.plus_ref), channel_id=1, source_target_pairs={{0,16},{1,17},{2,18},{3,19},{4,20},{5,21},{6,22},{7,23},{8,24},{9,... | collective-permute-start | bytes 356360 | tf_op jit(solution)/shard_map/ppermute | solution.py:745
  32.9 2.5 %collective-permute-done.4.got_high_ref.high_ref = f32[232,128]{1,0:T(8,128)S(1)} collective-permute-done((f32[232,128]{1,0:T(8,128)S(1)}, f32[232,128]{1,0:T(8,128)S(1)}, u32[]{:S(2)}, u32[]{:S(2)}) %collective-permute-start.4) | collective-permute-done | bytes 118816 | tf_op jit(solution)/shard_map/ppermute | solution.py:745
  35.4 0.0 collective-permute-done.3.got_low_ref.low_ref
  35.4 1.0 %collective-permute-start.5 = (f32[40,128]{1,0:T(8,128)S(1)}, f32[40,128]{1,0:T(8,128)S(1)}, u32[]{:S(2)}, u32[]{:S(2)}) collective-permute-start(f32[40,128]{1,0:T(8,128)S(1)} %get-tuple-element.48), channel_id=1, source_target_pairs={{0,1},{1,2},{2,3},{3,4},{4,5},{5,6},{6,7},{7,8},{8,9},{9,10},{10,1... | collective-permute-start | bytes 61448 | tf_op jit(solution)/shard_map/ppermute | solution.py:745
  36.4 3.9 %collective-permute-start.6 = (f32[40,128]{1,0:T(8,128)S(1)}, f32[40,128]{1,0:T(8,128)S(1)}, u32[]{:S(2)}, u32[]{:S(2)}) collective-permute-start(f32[40,128]{1,0:T(8,128)S(1)} %get-tuple-element.49), channel_id=1, source_target_pairs={{0,15},{1,0},{2,1},{3,2},{4,3},{5,4},{6,5},{7,6},{8,7},{9,8},{10,9... | collective-permute-start | bytes 61448 | tf_op jit(solution)/shard_map/ppermute | solution.py:745
  40.3 1.2 %collective-permute-done.5.from_down_ref = f32[40,128]{1,0:T(8,128)S(1)} collective-permute-done((f32[40,128]{1,0:T(8,128)S(1)}, f32[40,128]{1,0:T(8,128)S(1)}, u32[]{:S(2)}, u32[]{:S(2)}) %collective-permute-start.5) | collective-permute-done | bytes 20512 | tf_op jit(solution)/shard_map/ppermute | solution.py:745
  41.4 0.0 collective-permute-done.6.from_up_ref
  41.4 2.2 %apply.2 = (f32[3,27,8,128]{3,2,1,0:T(8,128)S(1)}, f32[232,128]{1,0:T(8,128)S(1)}, f32[232,128]{1,0:T(8,128)S(1)}, f32[2,27,8,128]{3,2,1,0:T(8,128)S(1)}, f32[2,16,128]{2,1,0:T(8,128)S(1)}) custom-call(f32[232,128]{1,0:T(8,128)S(1)} %get-tuple-element.44.minus_ref, f32[232,128]{1,0:T(8,128)S(1)} %get-tuple-element.45.plus_ref, ...), custom_call_target="tpu_custom_call" | custom-call | flops 13312000 | bytes 2920448 | tf_op jit(solution)/shard_map/apply/pallas_call | solution.py:718
  43.7 5.3 %collective-permute-start.8 = (f32[232,128]{1,0:T(8,128)S(1)}, f32[232,128]{1,0:T(8,128)S(1)}, u32[]{:S(2)}, u32[]{:S(2)}) collective-permute-start(f32[232,128]{1,0:T(8,128)S(1)} %get-tuple-element.53.minus_ref), channel_id=1, source_target_pairs={{0,112},{1,113},{2,114},{3,115},{4,116},{5,117},{6,118},{7,119},{8... | collective-permute-start | bytes 356360 | tf_op jit(solution)/shard_map/ppermute | solution.py:745
  49.0 0.0 collective-permute-start.7
  49.0 1.0 %collective-permute-done.8.got_high_ref.high_ref = f32[232,128]{1,0:T(8,128)S(1)} collective-permute-done((f32[232,128]{1,0:T(8,128)S(1)}, f32[232,128]{1,0:T(8,128)S(1)}, u32[]{:S(2)}, u32[]{:S(2)}) %collective-permute-start.8) | collective-permute-done | bytes 118816 | tf_op jit(solution)/shard_map/ppermute | solution.py:745
  50.0 0.9 collective-permute-done.7.got_low_ref.low_ref
  50.8 0.1 collective-permute-start.9
  50.9 5.1 %collective-permute-start.10 = (f32[40,128]{1,0:T(8,128)S(1)}, f32[40,128]{1,0:T(8,128)S(1)}, u32[]{:S(2)}, u32[]{:S(2)}) collective-permute-start(f32[40,128]{1,0:T(8,128)S(1)} %get-tuple-element.58), channel_id=1, source_target_pairs={{0,15},{1,0},{2,1},{3,2},{4,3},{5,4},{6,5},{7,6},{8,7},{9,8},{10,9... | collective-permute-start | bytes 61448 | tf_op jit(solution)/shard_map/ppermute | solution.py:745
  56.1 1.1 %collective-permute-done.9.from_down_ref = f32[40,128]{1,0:T(8,128)S(1)} collective-permute-done((f32[40,128]{1,0:T(8,128)S(1)}, f32[40,128]{1,0:T(8,128)S(1)}, u32[]{:S(2)}, u32[]{:S(2)}) %collective-permute-start.9) | collective-permute-done | bytes 20512 | tf_op jit(solution)/shard_map/ppermute | solution.py:745
  57.1 0.0 collective-permute-done.10.from_up_ref
  57.2 2.2 %apply.3 = (f32[3,27,8,128]{3,2,1,0:T(8,128)S(1)}, f32[232,128]{1,0:T(8,128)S(1)}, f32[232,128]{1,0:T(8,128)S(1)}, f32[2,27,8,128]{3,2,1,0:T(8,128)S(1)}, f32[2,16,128]{2,1,0:T(8,128)S(1)}) custom-call(f32[232,128]{1,0:T(8,128)S(1)} %get-tuple-element.53.minus_ref, f32[232,128]{1,0:T(8,128)S(1)} %get-tuple-element.54.plus_ref, ...), custom_call_target="tpu_custom_call" | custom-call | flops 13312000 | bytes 2920448 | tf_op jit(solution)/shard_map/apply/pallas_call | solution.py:718
  59.4 4.5 %collective-permute-start.12 = (f32[232,128]{1,0:T(8,128)S(1)}, f32[232,128]{1,0:T(8,128)S(1)}, u32[]{:S(2)}, u32[]{:S(2)}) collective-permute-start(f32[232,128]{1,0:T(8,128)S(1)} %get-tuple-element.59.minus_ref), channel_id=1, source_target_pairs={{0,112},{1,113},{2,114},{3,115},{4,116},{5,117},{6,118},{7,119},{8... | collective-permute-start | bytes 356360 | tf_op jit(solution)/shard_map/ppermute | solution.py:745
  63.9 0.0 collective-permute-start.11
  63.9 1.3 %collective-permute-done.12.got_high_ref.high_ref = f32[232,128]{1,0:T(8,128)S(1)} collective-permute-done((f32[232,128]{1,0:T(8,128)S(1)}, f32[232,128]{1,0:T(8,128)S(1)}, u32[]{:S(2)}, u32[]{:S(2)}) %collective-permute-start.12) | collective-permute-done | bytes 118816 | tf_op jit(solution)/shard_map/ppermute | solution.py:745
  65.2 0.5 collective-permute-done.11.got_low_ref.low_ref
  65.8 0.1 collective-permute-start.13
  65.9 5.2 %collective-permute-start.14 = (f32[40,128]{1,0:T(8,128)S(1)}, f32[40,128]{1,0:T(8,128)S(1)}, u32[]{:S(2)}, u32[]{:S(2)}) collective-permute-start(f32[40,128]{1,0:T(8,128)S(1)} %get-tuple-element.64), channel_id=1, source_target_pairs={{0,15},{1,0},{2,1},{3,2},{4,3},{5,4},{6,5},{7,6},{8,7},{9,8},{10,9... | collective-permute-start | bytes 61448 | tf_op jit(solution)/shard_map/ppermute | solution.py:745
  71.1 1.1 %collective-permute-done.13.from_down_ref = f32[40,128]{1,0:T(8,128)S(1)} collective-permute-done((f32[40,128]{1,0:T(8,128)S(1)}, f32[40,128]{1,0:T(8,128)S(1)}, u32[]{:S(2)}, u32[]{:S(2)}) %collective-permute-start.13) | collective-permute-done | bytes 20512 | tf_op jit(solution)/shard_map/ppermute | solution.py:745
  72.2 0.0 collective-permute-done.14.from_up_ref
  72.2 2.3 %moments.1 = (f32[3,27,8,128]{3,2,1,0:T(8,128)S(1)}, f32[128,128]{1,0:T(8,128)}) custom-call(f32[232,128]{1,0:T(8,128)S(1)} %get-tuple-element.59.minus_ref, f32[232,128]{1,0:T(8,128)S(1)} %get-tuple-element.60.plus_ref, f32[2,27,8,128]{3,2,1,0:T(8,128)S(1)} %get-tuple-element.61.inner_ref, f32[2,16,128]{2,1,0:T(8,128)S(1)} %get-tuple-element.62.rim_ref, ...), custom_call_target="tpu_custom_call" | custom-call | flops 8192000 | bytes 3174400 | tf_op jit(solution)/shard_map/moments/pallas_call | solution.py:718
  74.4 10.8 %all-to-all-start = ((f32[128,1,128]{2,1,0:T(1,128)}), f32[128,1,128]{2,1,0:T(1,128)S(1)}, u32[]{:S(2)}, u32[]{:S(2)}) async-start(f32[128,1,128]{2,1,0:T(1,128)} %bitcast.3), calls=%async_computation | async-start | bytes 131072 | tf_op jit(solution)/shard_map/all_to_all | solution.py:811
  85.3 0.0 copy-start.2
  85.3 0.0 copy-start.4
  85.3 1.2 %energy.1 = f32[27,8,128]{2,1,0:T(8,128)} custom-call(f32[216,8,128]{2,1,0:T(8,128)S(1)} %get-tuple-element.72.power_ref, f32[27,8,128]{2,1,0:T(8,128)S(1)} %get-tuple-element.73.lump_ref, f32[27,8,128]{2,1,0:T(8,128)S(1)} %bitcast.15), custom_call_target="tpu_custom_call" | custom-call | flops 2048000 | bytes 1216512 | tf_op jit(solution)/shard_map/energy/pallas_call | solution.py:718
  86.4 8.3 %all-to-all-done = f32[128,1,128]{2,1,0:T(1,128)S(1)} async-done(((f32[128,1,128]{2,1,0:T(1,128)}), f32[128,1,128]{2,1,0:T(1,128)S(1)}, u32[]{:S(2)}, u32[]{:S(2)}) %all-to-all-start) | async-done | bytes 65568 | tf_op jit(solution)/shard_map/all_to_all | solution.py:811
  94.8 0.0 copy-done.2
  94.8 0.0 copy-done.4
  94.8 1.8 %final.1 = (f32[3,3,24,384]{3,2,1,0:T(8,128)}, f32[3,3,24,384]{3,2,1,0:T(8,128)}, f32[3,3,24,384]{3,2,1,0:T(8,128)}) custom-call(f32[128,128]{1,0:T(8,128)S(1)} %bitcast.16, f32[3,27,8,128]{3,2,1,0:T(8,128)S(1)} %get-tuple-element.65.r_ref, f32[3,27,8,128]{3,2,1,0:T(8,128)S(1)} %get-tuple-element.66.v_ref, f32[3,27,8,128]{3,2,1,0:T(8,128)S(1)} %get-tuple-element.68.w_ref, ...), custom_call_target="tpu_custom_call" | custom-call | flops 1024000 | bytes 2719744 | tf_op jit(solution)/shard_map/final/pallas_call | solution.py:718
  (3 shorter events, 0.1 us)
Async XLA Ops:
  0.6 13.9 %copy-start = (f32[216,1,8,128]{3,2,1,0:T(8,128)S(1)}, f32[216,1,8,128]{3,2,1,0:T(8,128)}, u32[]{:S(2)}) copy-start(f32[216,1,8,128]{3,2,1,0:T(8,128)} %param.8) | copy-start | bytes 2654212
  0.6 1.1 %copy-start.1 = (f32[3,3,24,384]{3,2,1,0:T(8,128)S(1)}, f32[3,3,24,384]{3,2,1,0:T(8,128)}, u32[]{:S(2)}) copy-start(f32[3,3,24,384]{3,2,1,0:T(8,128)} %d_ref.5) | copy-start | bytes 995332
  1.7 1.0 %copy-start.3 = (f32[3,3,24,384]{3,2,1,0:T(8,128)S(1)}, f32[3,3,24,384]{3,2,1,0:T(8,128)}, u32[]{:S(2)}) copy-start(f32[3,3,24,384]{3,2,1,0:T(8,128)} %vel_ref.1) | copy-start | bytes 995332
  2.7 1.0 %copy-start.5 = (s32[3,3,24,384]{3,2,1,0:T(8,128)S(1)}, s32[3,3,24,384]{3,2,1,0:T(8,128)}, u32[]{:S(2)}) copy-start(s32[3,3,24,384]{3,2,1,0:T(8,128)} %f_ref.3) | copy-start | bytes 995332
  3.6 10.9 %copy-start.6 = (f32[27,1,8,128]{3,2,1,0:T(8,128)S(1)}, f32[27,1,8,128]{3,2,1,0:T(8,128)}, u32[]{:S(2)}) copy-start(f32[27,1,8,128]{3,2,1,0:T(8,128)} %param.7) | copy-start | bytes 331780
  3.9 13.0 %collective-permute-start = (f32[9,24,384]{2,1,0:T(8,128)S(1)}, f32[9,24,384]{2,1,0:T(8,128)S(1)}, u32[]{:S(2)}, u32[]{:S(2)}) collective-permute-start(f32[9,24,384]{2,1,0:T(8,128)S(1)} %get-tuple-element.40), channel_id=1, source_target_pairs={{0,112},{1,113},{2,114},{3,115},{4,116},{5,117},{6,118},{7,119},{8... | collective-permute-start | bytes 995336 | tf_op jit(solution)/shard_map/ppermute | solution.py:745
  5.4 11.6 %collective-permute-start.1 = (f32[27,384]{1,0:T(8,128)S(1)}, f32[27,384]{1,0:T(8,128)S(1)}, u32[]{:S(2)}, u32[]{:S(2)}) collective-permute-start(f32[27,384]{1,0:T(8,128)S(1)} %get-tuple-element.41), channel_id=1, source_target_pairs={{0,15},{1,0},{2,1},{3,2},{4,3},{5,4},{6,5},{7,6},{8,7},{9,8},{10,9... | collective-permute-start | bytes 124424 | tf_op jit(solution)/shard_map/ppermute | solution.py:745
  10.4 6.5 %collective-permute-start.2 = (f32[9,384]{1,0:T(8,128)S(1)}, f32[9,384]{1,0:T(8,128)S(1)}, u32[]{:S(2)}, u32[]{:S(2)}) collective-permute-start(f32[9,384]{1,0:T(8,128)S(1)} %get-tuple-element.42), channel_id=1, source_target_pairs={{0,127},{1,112},{2,113},{3,114},{4,115},{5,116},{6,117},{7,118},{8... | collective-permute-start | bytes 41480 | tf_op jit(solution)/shard_map/ppermute | solution.py:745
  31.1 4.3 %collective-permute-start.4 = (f32[232,128]{1,0:T(8,128)S(1)}, f32[232,128]{1,0:T(8,128)S(1)}, u32[]{:S(2)}, u32[]{:S(2)}) collective-permute-start(f32[232,128]{1,0:T(8,128)S(1)} %get-tuple-element.44.minus_ref), channel_id=1, source_target_pairs={{0,112},{1,113},{2,114},{3,115},{4,116},{5,117},{6,118},{7,119},{8... | collective-permute-start | bytes 356360 | tf_op jit(solution)/shard_map/ppermute | solution.py:745
  31.5 3.8 %collective-permute-start.3 = (f32[232,128]{1,0:T(8,128)S(1)}, f32[232,128]{1,0:T(8,128)S(1)}, u32[]{:S(2)}, u32[]{:S(2)}) collective-permute-start(f32[232,128]{1,0:T(8,128)S(1)} %get-tuple-element.45.plus_ref), channel_id=1, source_target_pairs={{0,16},{1,17},{2,18},{3,19},{4,20},{5,21},{6,22},{7,23},{8,24},{9,... | collective-permute-start | bytes 356360 | tf_op jit(solution)/shard_map/ppermute | solution.py:745
  35.4 6.0 %collective-permute-start.5 = (f32[40,128]{1,0:T(8,128)S(1)}, f32[40,128]{1,0:T(8,128)S(1)}, u32[]{:S(2)}, u32[]{:S(2)}) collective-permute-start(f32[40,128]{1,0:T(8,128)S(1)} %get-tuple-element.48), channel_id=1, source_target_pairs={{0,1},{1,2},{2,3},{3,4},{4,5},{5,6},{6,7},{7,8},{8,9},{9,10},{10,1... | collective-permute-start | bytes 61448 | tf_op jit(solution)/shard_map/ppermute | solution.py:745
  36.4 5.0 %collective-permute-start.6 = (f32[40,128]{1,0:T(8,128)S(1)}, f32[40,128]{1,0:T(8,128)S(1)}, u32[]{:S(2)}, u32[]{:S(2)}) collective-permute-start(f32[40,128]{1,0:T(8,128)S(1)} %get-tuple-element.49), channel_id=1, source_target_pairs={{0,15},{1,0},{2,1},{3,2},{4,3},{5,4},{6,5},{7,6},{8,7},{9,8},{10,9... | collective-permute-start | bytes 61448 | tf_op jit(solution)/shard_map/ppermute | solution.py:745
  43.7 6.3 %collective-permute-start.8 = (f32[232,128]{1,0:T(8,128)S(1)}, f32[232,128]{1,0:T(8,128)S(1)}, u32[]{:S(2)}, u32[]{:S(2)}) collective-permute-start(f32[232,128]{1,0:T(8,128)S(1)} %get-tuple-element.53.minus_ref), channel_id=1, source_target_pairs={{0,112},{1,113},{2,114},{3,115},{4,116},{5,117},{6,118},{7,119},{8... | collective-permute-start | bytes 356360 | tf_op jit(solution)/shard_map/ppermute | solution.py:745
  49.0 1.8 %collective-permute-start.7 = (f32[232,128]{1,0:T(8,128)S(1)}, f32[232,128]{1,0:T(8,128)S(1)}, u32[]{:S(2)}, u32[]{:S(2)}) collective-permute-start(f32[232,128]{1,0:T(8,128)S(1)} %get-tuple-element.54.plus_ref), channel_id=1, source_target_pairs={{0,16},{1,17},{2,18},{3,19},{4,20},{5,21},{6,22},{7,23},{8,24},{9,... | collective-permute-start | bytes 356360 | tf_op jit(solution)/shard_map/ppermute | solution.py:745
  50.8 6.3 %collective-permute-start.9 = (f32[40,128]{1,0:T(8,128)S(1)}, f32[40,128]{1,0:T(8,128)S(1)}, u32[]{:S(2)}, u32[]{:S(2)}) collective-permute-start(f32[40,128]{1,0:T(8,128)S(1)} %get-tuple-element.57), channel_id=1, source_target_pairs={{0,1},{1,2},{2,3},{3,4},{4,5},{5,6},{6,7},{7,8},{8,9},{9,10},{10,1... | collective-permute-start | bytes 61448 | tf_op jit(solution)/shard_map/ppermute | solution.py:745
  50.9 6.2 %collective-permute-start.10 = (f32[40,128]{1,0:T(8,128)S(1)}, f32[40,128]{1,0:T(8,128)S(1)}, u32[]{:S(2)}, u32[]{:S(2)}) collective-permute-start(f32[40,128]{1,0:T(8,128)S(1)} %get-tuple-element.58), channel_id=1, source_target_pairs={{0,15},{1,0},{2,1},{3,2},{4,3},{5,4},{6,5},{7,6},{8,7},{9,8},{10,9... | collective-permute-start | bytes 61448 | tf_op jit(solution)/shard_map/ppermute | solution.py:745
  59.4 5.8 %collective-permute-start.12 = (f32[232,128]{1,0:T(8,128)S(1)}, f32[232,128]{1,0:T(8,128)S(1)}, u32[]{:S(2)}, u32[]{:S(2)}) collective-permute-start(f32[232,128]{1,0:T(8,128)S(1)} %get-tuple-element.59.minus_ref), channel_id=1, source_target_pairs={{0,112},{1,113},{2,114},{3,115},{4,116},{5,117},{6,118},{7,119},{8... | collective-permute-start | bytes 356360 | tf_op jit(solution)/shard_map/ppermute | solution.py:745
  63.9 1.8 %collective-permute-start.11 = (f32[232,128]{1,0:T(8,128)S(1)}, f32[232,128]{1,0:T(8,128)S(1)}, u32[]{:S(2)}, u32[]{:S(2)}) collective-permute-start(f32[232,128]{1,0:T(8,128)S(1)} %get-tuple-element.60.plus_ref), channel_id=1, source_target_pairs={{0,16},{1,17},{2,18},{3,19},{4,20},{5,21},{6,22},{7,23},{8,24},{9,... | collective-permute-start | bytes 356360 | tf_op jit(solution)/shard_map/ppermute | solution.py:745
  65.8 6.4 %collective-permute-start.13 = (f32[40,128]{1,0:T(8,128)S(1)}, f32[40,128]{1,0:T(8,128)S(1)}, u32[]{:S(2)}, u32[]{:S(2)}) collective-permute-start(f32[40,128]{1,0:T(8,128)S(1)} %get-tuple-element.63), channel_id=1, source_target_pairs={{0,1},{1,2},{2,3},{3,4},{4,5},{5,6},{6,7},{7,8},{8,9},{9,10},{10,1... | collective-permute-start | bytes 61448 | tf_op jit(solution)/shard_map/ppermute | solution.py:745
  65.9 6.3 %collective-permute-start.14 = (f32[40,128]{1,0:T(8,128)S(1)}, f32[40,128]{1,0:T(8,128)S(1)}, u32[]{:S(2)}, u32[]{:S(2)}) collective-permute-start(f32[40,128]{1,0:T(8,128)S(1)} %get-tuple-element.64), channel_id=1, source_target_pairs={{0,15},{1,0},{2,1},{3,2},{4,3},{5,4},{6,5},{7,6},{8,7},{9,8},{10,9... | collective-permute-start | bytes 61448 | tf_op jit(solution)/shard_map/ppermute | solution.py:745
  74.4 20.3 %all-to-all-start = ((f32[128,1,128]{2,1,0:T(1,128)}), f32[128,1,128]{2,1,0:T(1,128)S(1)}, u32[]{:S(2)}, u32[]{:S(2)}) async-start(f32[128,1,128]{2,1,0:T(1,128)} %bitcast.3), calls=%async_computation | async-start | bytes 131072 | tf_op jit(solution)/shard_map/all_to_all | solution.py:811
  85.3 9.5 %copy-start.2 = (f32[3,3,24,384]{3,2,1,0:T(8,128)S(1)}, f32[3,3,24,384]{3,2,1,0:T(8,128)}, u32[]{:S(2)}) copy-start(f32[3,3,24,384]{3,2,1,0:T(8,128)} %d_ref.5) | copy-start | bytes 995332
  85.3 9.5 %copy-start.4 = (f32[3,3,24,384]{3,2,1,0:T(8,128)S(1)}, f32[3,3,24,384]{3,2,1,0:T(8,128)}, u32[]{:S(2)}) copy-start(f32[3,3,24,384]{3,2,1,0:T(8,128)} %vel_ref.1) | copy-start | bytes 995332

commit v3 on v2

--- a/solution.py
+++ b/solution.py
@@ -250,7 +250,7 @@
             out_ref[3 * n + g] = t
 
 
-def energy_kernel(power_ref, lump_ref, e_ref, out_ref, sum_s, z_s, x_s):
+def energy_kernel(power_ref, lump_ref, e_ref, out_ref, token_ref, sum_s, z_s, x_s):
     project(power_ref, z_s, x_s, sum_s)
 
     def body(n, _):
@@ -258,6 +258,7 @@
         return 0
 
     lax.fori_loop(0, 27, body, 0)
+    token_ref[...] = sum_s[0]
 
 
 def point(jac, vel, energy, mass):
@@ -480,7 +481,8 @@
     return [[rows[b][x] for b in range(4)] for x in range(4)]
 
 
-def rows_kernel(minus_ref, plus_ref, inner_ref, rim_ref, got_low_ref, got_high_ref, down_ref, up_ref):
+def rows_kernel(minus_ref, plus_ref, inner_ref, rim_ref, got_low_ref, got_high_ref, *rest):
+    down_ref, up_ref = rest[-2:]
     for c in range(3):
         for g in range(3):
             r = c * 3 + g
@@ -712,14 +714,14 @@
             copy.wait()
 
 
-def call(kernel, outs, scratch, name, flops=0, **more):
+def call(kernel, outs, scratch, name, flops=0, limit=VMEM_LIMIT, **more):
     def run(*args):
         moved = sum(a.size * 4 for a in args) + sum(4 * math.prod(s) for s in outs)
         return pl.pallas_call(
             kernel,
             out_shape=[jax.ShapeDtypeStruct(s, F32) for s in outs],
             scratch_shapes=[pltpu.VMEM(s, F32) if isinstance(s, tuple) else s for s in scratch],
-            compiler_params=pltpu.CompilerParams(vmem_limit_bytes=VMEM_LIMIT),
+            compiler_params=pltpu.CompilerParams(vmem_limit_bytes=limit),
             cost_estimate=pl.CostEstimate(flops=flops, bytes_accessed=moved, transcendentals=0),
             name=name,
             **more,
@@ -744,12 +746,14 @@
         ]
         return lax.ppermute(value, ("gx", "gy"), pairs)
 
-    def complete(parts):
+    def complete(parts, *done):
         minus, plus_face, inner, rim = parts
         low = moved(plus_face, 1, 0)
         high = moved(minus, -1, 0)
-        down, up = call(rows_kernel, [(40, 128), (40, 128)], [], "rows")(
-            minus, plus_face, inner, rim, low, high
+        specs = [pl.BlockSpec(memory_space=pltpu.VMEM)] * 6
+        specs += [pl.BlockSpec(memory_space=pltpu.VMEM)] * len(done)
+        down, up = call(rows_kernel, [(40, 128), (40, 128)], [], "rows", in_specs=specs)(
+            minus, plus_face, inner, rim, low, high, *done
         )
         from_up = moved(down, 0, -1)
         from_down = moved(up, 0, 1)
@@ -767,6 +771,7 @@
                 pltpu.VMEM((3, 3, 8, 384), flags), pltpu.SemaphoreType.DMA((6,)),
             ],
             "pack",
+            limit=62 * 1024 * 1024,
             in_specs=[pl.BlockSpec(memory_space=pltpu.HBM)] * 3,
         )(displacement, velocity, pinned)
         hx = moved(face, -1, 0)
@@ -791,8 +796,8 @@
             flops=90000 * 1024,
         )(nodes, hx, hy, hc, heat, weight)
         parts, (face_mask, rim_mask, power) = out[:4], out[4:]
-        (energy_new,) = call(
-            energy_kernel, [(27,) + T], [(27,) + T, (6, 9) + T, (6, 3) + T], "energy",
+        energy_new, token = call(
+            energy_kernel, [(27,) + T, T], [(27,) + T, (6, 9) + T, (6, 3) + T], "energy",
             flops=2000 * 1024,
         )(power, lump, dofs)
         masks = (mask, face_mask, rim_mask)
@@ -800,7 +805,7 @@
             (3, 48) + T, (6, 3, 16) + T, (3, 4, 6) + T, (6, 3, 16) + T, (3, 48) + T,
         ]
         apply = call(apply_kernel, [(3, 27) + T] + PARTS, scratch, "apply", flops=13000 * 1024)
-        out = apply(*complete(parts), *masks, weight)
+        out = apply(*complete(parts, token), *masks, weight)
         r, parts = out[0], out[1:]
         out = apply(*complete(parts), *masks, weight)
         v, parts = out[0], out[1:]

time: 96.7 us -> 95.6 us (0.989)
  blocking collectives: 0 us -> 20.2 us
  starting transfers between devices: 48.4 us -> 34.9 us
  waiting for transfers between devices: 17.9 us -> 8.86 us
  Pallas kernels: 26.4 us -> 27.6 us
    all_to_all x0 -> x1, blocking collectives: none -> 20.2 us  [on_device(): sums = lax.all_to_all(sums, ('gx', 'gy'), 0, 0).reshape(-1, 128)]
    all_to_all x1 -> x0, starting transfers between devices: 10.8 us -> none  [on_device(): sums = lax.all_to_all(sums, ('gx', 'gy'), 0, 0).reshape(-1, 128)]
    all_to_all x1 -> x0, waiting for transfers between devices: 8.33 us -> none  [on_device(): sums = lax.all_to_all(sums, ('gx', 'gy'), 0, 0).reshape(-1, 128)]
    ppermute x15, starting transfers between devices: 37.6 us -> 34.9 us  [moved(): return lax.ppermute(value, ('gx', 'gy'), pairs)]
    pallas_call x11, Pallas kernels: 26.4 us -> 27.6 us  [run(): pl.pallas_call(kernel, out_shape=[jax.ShapeDtypeStruct(s, F32) for s in o...]
  transfers between devices with their start and end apart: 16 -> 15, of which waited for: 9 -> 7; matrix products, arithmetic and copies ran while one was open for 0% -> 0% of each run, Pallas kernels for 4% -> 4%
where the time goes in v3:
time: 95.6 us; the launch traced here: 95.3 us
  starting transfers between devices  34.9 us (37%)
  Pallas kernels  27.6 us (29%)
  blocking collectives  20.2 us (21%)
  waiting for transfers between devices  8.86 us (9%)
  local copies, waits for them, and re-layouts  2.94 us (3%)
    ppermute x15, starting transfers between devices, moved(): return lax.ppermute(value, ('gx', 'gy'), pairs)  34.9 us
    pallas_call x11, Pallas kernels, run(): pl.pallas_call(kernel, out_shape=[jax.ShapeDtypeStruct(s, F32) for s in o...  27.6 us
    all_to_all x1, blocking collectives, on_device(): sums = lax.all_to_all(sums, ('gx', 'gy'), 0, 0).reshape(-1, 128)  20.2 us
    ppermute x15, waiting for transfers between devices, moved(): return lax.ppermute(value, ('gx', 'gy'), pairs)  8.86 us
    unnamed x14, local copies, waits for them, and re-layouts  2.94 us
  transfers between devices with their start and end apart: 15, of which 7 were waited for; matrix products, arithmetic and copies ran while one was open for 0% of the time, Pallas kernels for 4%

profile of v3, /device:TPU:1, one launch (start us, length us, event | category | flops | bytes accessed | tf_op | source)
XLA Modules:
  0.0 95.3 jit_solution(14292528966929681336)
XLA Ops:
  0.6 0.0 copy-start
  0.6 0.0 copy-start.6
  0.7 2.1 %pack.1 = (f32[9,24,384]{2,1,0:T(8,128)}, f32[27,384]{1,0:T(8,128)}, f32[9,384]{1,0:T(8,128)}) custom-call(f32[3,3,24,384]{3,2,1,0:T(8,128)} %d_ref.5, f32[3,3,24,384]{3,2,1,0:T(8,128)} %vel_ref.1, s32[3,3,24,384]{3,2,1,0:T(8,128)} %f_ref.3), custom_call_target="tpu_custom_call" | custom-call | bytes 1382400 | tf_op jit(solution)/shard_map/pack/pallas_call | solution.py:720
  2.7 1.4 %collective-permute-start = (f32[9,24,384]{2,1,0:T(8,128)}, f32[9,24,384]{2,1,0:T(8,128)S(1)}, u32[]{:S(2)}, u32[]{:S(2)}) collective-permute-start(f32[9,24,384]{2,1,0:T(8,128)} %get-tuple-element.42), channel_id=1, source_target_pairs={{0,112},{1,113},{2,114},{3,115},{4,116},{5,117},{6,118},{7,119},{8... | collective-permute-start | bytes 995336 | tf_op jit(solution)/shard_map/ppermute | solution.py:747
  4.2 5.0 %collective-permute-start.1 = (f32[27,384]{1,0:T(8,128)}, f32[27,384]{1,0:T(8,128)S(1)}, u32[]{:S(2)}, u32[]{:S(2)}) collective-permute-start(f32[27,384]{1,0:T(8,128)} %get-tuple-element.43), channel_id=1, source_target_pairs={{0,15},{1,0},{2,1},{3,2},{4,3},{5,4},{6,5},{7,6},{8,7},{9,8},{10,9... | collective-permute-start | bytes 124424 | tf_op jit(solution)/shard_map/ppermute | solution.py:747
  9.2 4.2 %collective-permute-start.2 = (f32[9,384]{1,0:T(8,128)}, f32[9,384]{1,0:T(8,128)S(1)}, u32[]{:S(2)}, u32[]{:S(2)}) collective-permute-start(f32[9,384]{1,0:T(8,128)} %get-tuple-element.44), channel_id=1, source_target_pairs={{0,127},{1,112},{2,113},{3,114},{4,115},{5,116},{6,117},{7,118},{8... | collective-permute-start | bytes 41480 | tf_op jit(solution)/shard_map/ppermute | solution.py:747
  13.4 0.0 copy-done
  13.4 0.0 copy-done.6
  13.4 0.0 copy-start.1
  13.4 1.0 %copy-done.1 = f32[3,3,24,384]{3,2,1,0:T(8,128)S(1)} copy-done((f32[3,3,24,384]{3,2,1,0:T(8,128)S(1)}, f32[3,3,24,384]{3,2,1,0:T(8,128)}, u32[]{:S(2)}) %copy-start.1) | copy-done | bytes 331800
  14.3 0.0 copy-start.3
  14.3 1.0 %copy-done.3 = f32[3,3,24,384]{3,2,1,0:T(8,128)S(1)} copy-done((f32[3,3,24,384]{3,2,1,0:T(8,128)S(1)}, f32[3,3,24,384]{3,2,1,0:T(8,128)}, u32[]{:S(2)}) %copy-start.3) | copy-done | bytes 331800
  15.3 0.0 copy-start.5
  15.3 1.0 %copy-done.5 = s32[3,3,24,384]{3,2,1,0:T(8,128)S(1)} copy-done((s32[3,3,24,384]{3,2,1,0:T(8,128)S(1)}, s32[3,3,24,384]{3,2,1,0:T(8,128)}, u32[]{:S(2)}) %copy-start.5) | copy-done | bytes 331800
  16.3 2.3 %prep.1 = (f32[6,27,8,128]{3,2,1,0:T(8,128)S(1)}, f32[3,27,8,128]{3,2,1,0:T(8,128)S(1)}, f32[216,8,128]{2,1,0:T(8,128)S(1)}, f32[27,8,128]{2,1,0:T(8,128)S(1)}) custom-call(f32[3,3,24,384]{3,2,1,0:T(8,128)S(1)} %copy-done.1, f32[3,3,24,384]{3,2,1,0:T(8,128)S(1)} %copy-done.3, s32[3,3,24,384]{3,2,1,0:T(8,128)S(1)} %copy-done.5, f32[27,8,128]{2,1,0:T(8,128)S(1)} %bitcast.14, ...), custom_call_target="tpu_custom_call" | custom-call | flops 4096000 | bytes 3981312 | tf_op jit(solution)/shard_map/prep/pallas_call | solution.py:720
  18.6 0.0 collective-permute-done.2.hc_ref
  18.6 0.0 collective-permute-done.1.hy_ref
  18.7 0.0 collective-permute-done.hx_ref
  18.7 14.1 %force.1 = (f32[232,128]{1,0:T(8,128)S(1)}, f32[232,128]{1,0:T(8,128)S(1)}, f32[2,27,8,128]{3,2,1,0:T(8,128)S(1)}, f32[2,16,128]{2,1,0:T(8,128)S(1)}, f32[27,8,1...) custom-call(f32[6,27,8,128]{3,2,1,0:T(8,128)S(1)} %get-tuple-element.41.u_ref, ...), custom_call_target="tpu_custom_call" | custom-call | flops 92160000 | bytes 4323328 | tf_op jit(solution)/shard_map/force/pallas_call | solution.py:720
  32.8 0.3 collective-permute-start.4
  33.1 1.5 %collective-permute-start.3 = (f32[232,128]{1,0:T(8,128)S(1)}, f32[232,128]{1,0:T(8,128)S(1)}, u32[]{:S(2)}, u32[]{:S(2)}) collective-permute-start(f32[232,128]{1,0:T(8,128)S(1)} %get-tuple-element.47.plus_ref), channel_id=1, source_target_pairs={{0,16},{1,17},{2,18},{3,19},{4,20},{5,21},{6,22},{7,23},{8,24},{9,... | collective-permute-start | bytes 356360 | tf_op jit(solution)/shard_map/ppermute | solution.py:747
  34.6 1.1 %energy.1 = (f32[27,8,128]{2,1,0:T(8,128)}, f32[8,128]{1,0:T(8,128)S(1)}) custom-call(f32[216,8,128]{2,1,0:T(8,128)S(1)} %get-tuple-element.50.power_ref, f32[27,8,128]{2,1,0:T(8,128)S(1)} %get-tuple-element.51.lump_ref, f32[27,8,128]{2,1,0:T(8,128)S(1)} %bitcast.15), custom_call_target="tpu_custom_call" | custom-call | flops 2048000 | bytes 1220608 | tf_op jit(solution)/shard_map/energy/pallas_call | solution.py:720
  35.7 1.4 %collective-permute-done.4.got_high_ref.high_ref = f32[232,128]{1,0:T(8,128)S(1)} collective-permute-done((f32[232,128]{1,0:T(8,128)S(1)}, f32[232,128]{1,0:T(8,128)S(1)}, u32[]{:S(2)}, u32[]{:S(2)}) %collective-permute-start.4) | collective-permute-done | bytes 118816 | tf_op jit(solution)/shard_map/ppermute | solution.py:747
  37.1 0.0 collective-permute-done.3.got_low_ref.low_ref
  37.1 1.0 %collective-permute-start.5 = (f32[40,128]{1,0:T(8,128)S(1)}, f32[40,128]{1,0:T(8,128)S(1)}, u32[]{:S(2)}, u32[]{:S(2)}) collective-permute-start(f32[40,128]{1,0:T(8,128)S(1)} %get-tuple-element.53), channel_id=1, source_target_pairs={{0,1},{1,2},{2,3},{3,4},{4,5},{5,6},{6,7},{7,8},{8,9},{9,10},{10,1... | collective-permute-start | bytes 61448 | tf_op jit(solution)/shard_map/ppermute | solution.py:747
  38.1 3.9 %collective-permute-start.6 = (f32[40,128]{1,0:T(8,128)S(1)}, f32[40,128]{1,0:T(8,128)S(1)}, u32[]{:S(2)}, u32[]{:S(2)}) collective-permute-start(f32[40,128]{1,0:T(8,128)S(1)} %get-tuple-element.54), channel_id=1, source_target_pairs={{0,15},{1,0},{2,1},{3,2},{4,3},{5,4},{6,5},{7,6},{8,7},{9,8},{10,9... | collective-permute-start | bytes 61448 | tf_op jit(solution)/shard_map/ppermute | solution.py:747
  42.0 1.2 %collective-permute-done.5.from_down_ref = f32[40,128]{1,0:T(8,128)S(1)} collective-permute-done((f32[40,128]{1,0:T(8,128)S(1)}, f32[40,128]{1,0:T(8,128)S(1)}, u32[]{:S(2)}, u32[]{:S(2)}) %collective-permute-start.5) | collective-permute-done | bytes 20512 | tf_op jit(solution)/shard_map/ppermute | solution.py:747
  43.1 0.0 collective-permute-done.6.from_up_ref
  43.1 2.2 %apply.2 = (f32[3,27,8,128]{3,2,1,0:T(8,128)S(1)}, f32[232,128]{1,0:T(8,128)S(1)}, f32[232,128]{1,0:T(8,128)S(1)}, f32[2,27,8,128]{3,2,1,0:T(8,128)S(1)}, f32[2,16,128]{2,1,0:T(8,128)S(1)}) custom-call(f32[232,128]{1,0:T(8,128)S(1)} %get-tuple-element.46.minus_ref, f32[232,128]{1,0:T(8,128)S(1)} %get-tuple-element.47.plus_ref, ...), custom_call_target="tpu_custom_call" | custom-call | flops 13312000 | bytes 2920448 | tf_op jit(solution)/shard_map/apply/pallas_call | solution.py:720
  45.4 3.1 %collective-permute-start.8 = (f32[232,128]{1,0:T(8,128)S(1)}, f32[232,128]{1,0:T(8,128)S(1)}, u32[]{:S(2)}, u32[]{:S(2)}) collective-permute-start(f32[232,128]{1,0:T(8,128)S(1)} %get-tuple-element.58.minus_ref), channel_id=1, source_target_pairs={{0,112},{1,113},{2,114},{3,115},{4,116},{5,117},{6,118},{7,119},{8... | collective-permute-start | bytes 356360 | tf_op jit(solution)/shard_map/ppermute | solution.py:747
  48.5 0.0 collective-permute-start.7
  48.5 2.3 %collective-permute-done.8.got_high_ref.high_ref = f32[232,128]{1,0:T(8,128)S(1)} collective-permute-done((f32[232,128]{1,0:T(8,128)S(1)}, f32[232,128]{1,0:T(8,128)S(1)}, u32[]{:S(2)}, u32[]{:S(2)}) %collective-permute-start.8) | collective-permute-done | bytes 118816 | tf_op jit(solution)/shard_map/ppermute | solution.py:747
  50.8 0.0 collective-permute-done.7.got_low_ref.low_ref
  50.8 0.1 collective-permute-start.9
  50.9 5.1 %collective-permute-start.10 = (f32[40,128]{1,0:T(8,128)S(1)}, f32[40,128]{1,0:T(8,128)S(1)}, u32[]{:S(2)}, u32[]{:S(2)}) collective-permute-start(f32[40,128]{1,0:T(8,128)S(1)} %get-tuple-element.63), channel_id=1, source_target_pairs={{0,15},{1,0},{2,1},{3,2},{4,3},{5,4},{6,5},{7,6},{8,7},{9,8},{10,9... | collective-permute-start | bytes 61448 | tf_op jit(solution)/shard_map/ppermute | solution.py:747
  56.0 1.1 %collective-permute-done.9.from_down_ref = f32[40,128]{1,0:T(8,128)S(1)} collective-permute-done((f32[40,128]{1,0:T(8,128)S(1)}, f32[40,128]{1,0:T(8,128)S(1)}, u32[]{:S(2)}, u32[]{:S(2)}) %collective-permute-start.9) | collective-permute-done | bytes 20512 | tf_op jit(solution)/shard_map/ppermute | solution.py:747
  57.1 0.0 collective-permute-done.10.from_up_ref
  57.1 2.2 %apply.3 = (f32[3,27,8,128]{3,2,1,0:T(8,128)S(1)}, f32[232,128]{1,0:T(8,128)S(1)}, f32[232,128]{1,0:T(8,128)S(1)}, f32[2,27,8,128]{3,2,1,0:T(8,128)S(1)}, f32[2,16,128]{2,1,0:T(8,128)S(1)}) custom-call(f32[232,128]{1,0:T(8,128)S(1)} %get-tuple-element.58.minus_ref, f32[232,128]{1,0:T(8,128)S(1)} %get-tuple-element.59.plus_ref, ...), custom_call_target="tpu_custom_call" | custom-call | flops 13312000 | bytes 2920448 | tf_op jit(solution)/shard_map/apply/pallas_call | solution.py:720
  59.4 4.1 %collective-permute-start.12 = (f32[232,128]{1,0:T(8,128)S(1)}, f32[232,128]{1,0:T(8,128)S(1)}, u32[]{:S(2)}, u32[]{:S(2)}) collective-permute-start(f32[232,128]{1,0:T(8,128)S(1)} %get-tuple-element.64.minus_ref), channel_id=1, source_target_pairs={{0,112},{1,113},{2,114},{3,115},{4,116},{5,117},{6,118},{7,119},{8... | collective-permute-start | bytes 356360 | tf_op jit(solution)/shard_map/ppermute | solution.py:747
  63.4 0.0 collective-permute-start.11
  63.4 1.3 %collective-permute-done.12.got_high_ref.high_ref = f32[232,128]{1,0:T(8,128)S(1)} collective-permute-done((f32[232,128]{1,0:T(8,128)S(1)}, f32[232,128]{1,0:T(8,128)S(1)}, u32[]{:S(2)}, u32[]{:S(2)}) %collective-permute-start.12) | collective-permute-done | bytes 118816 | tf_op jit(solution)/shard_map/ppermute | solution.py:747
  64.7 0.5 collective-permute-done.11.got_low_ref.low_ref
  65.3 0.1 collective-permute-start.13
  65.4 5.2 %collective-permute-start.14 = (f32[40,128]{1,0:T(8,128)S(1)}, f32[40,128]{1,0:T(8,128)S(1)}, u32[]{:S(2)}, u32[]{:S(2)}) collective-permute-start(f32[40,128]{1,0:T(8,128)S(1)} %get-tuple-element.69), channel_id=1, source_target_pairs={{0,15},{1,0},{2,1},{3,2},{4,3},{5,4},{6,5},{7,6},{8,7},{9,8},{10,9... | collective-permute-start | bytes 61448 | tf_op jit(solution)/shard_map/ppermute | solution.py:747
  70.6 1.1 %collective-permute-done.13.from_down_ref = f32[40,128]{1,0:T(8,128)S(1)} collective-permute-done((f32[40,128]{1,0:T(8,128)S(1)}, f32[40,128]{1,0:T(8,128)S(1)}, u32[]{:S(2)}, u32[]{:S(2)}) %collective-permute-start.13) | collective-permute-done | bytes 20512 | tf_op jit(solution)/shard_map/ppermute | solution.py:747
  71.7 0.0 collective-permute-done.14.from_up_ref
  71.7 0.0 copy-start.2
  71.7 0.0 copy-start.4
  71.7 1.6 %moments.1 = (f32[3,27,8,128]{3,2,1,0:T(8,128)S(1)}, f32[128,128]{1,0:T(8,128)S(1)}) custom-call(f32[232,128]{1,0:T(8,128)S(1)} %get-tuple-element.64.minus_ref, f32[232,128]{1,0:T(8,128)S(1)} %get-tuple-element.65.plus_ref, f32[2,27,8,128]{3,2,1,0:T(8,128)S(1)} %get-tuple-element.66.inner_ref, f32[2,16,128]{2,1,0:T(8,128)S(1)} %get-tuple-element.67.rim_ref, ...), custom_call_target="tpu_custom_call" | custom-call | flops 8192000 | bytes 3174400 | tf_op jit(solution)/shard_map/moments/pallas_call | solution.py:720
  73.3 20.2 %all_to_all.5 = f32[128,1,128]{2,1,0:T(1,128)S(1)} all-to-all(f32[128,1,128]{2,1,0:T(1,128)S(1)} %bitcast.17), channel_id=1, replica_groups=mesh['gx'=8,'gy'=16] {'gx','gy'}, dimensions={0} | all-to-all | bytes 131072 | tf_op jit(solution)/shard_map/all_to_all | solution.py:816
  93.5 0.0 copy-done.2
  93.5 0.0 copy-done.4
  93.5 1.8 %final.1 = (f32[3,3,24,384]{3,2,1,0:T(8,128)}, f32[3,3,24,384]{3,2,1,0:T(8,128)}, f32[3,3,24,384]{3,2,1,0:T(8,128)}) custom-call(f32[128,128]{1,0:T(8,128)S(1)} %bitcast.16, f32[3,27,8,128]{3,2,1,0:T(8,128)S(1)} %get-tuple-element.70.r_ref, f32[3,27,8,128]{3,2,1,0:T(8,128)S(1)} %get-tuple-element.71.v_ref, f32[3,27,8,128]{3,2,1,0:T(8,128)S(1)} %get-tuple-element.73.w_ref, ...), custom_call_target="tpu_custom_call" | custom-call | flops 1024000 | bytes 2719744 | tf_op jit(solution)/shard_map/final/pallas_call | solution.py:720
  (3 shorter events, 0.1 us)
Async XLA Ops:
  0.6 12.7 %copy-start = (f32[216,1,8,128]{3,2,1,0:T(8,128)S(1)}, f32[216,1,8,128]{3,2,1,0:T(8,128)}, u32[]{:S(2)}) copy-start(f32[216,1,8,128]{3,2,1,0:T(8,128)} %param.8) | copy-start | bytes 2654212
  0.6 12.7 %copy-start.6 = (f32[27,1,8,128]{3,2,1,0:T(8,128)S(1)}, f32[27,1,8,128]{3,2,1,0:T(8,128)}, u32[]{:S(2)}) copy-start(f32[27,1,8,128]{3,2,1,0:T(8,128)} %param.7) | copy-start | bytes 331780
  2.7 15.9 %collective-permute-start = (f32[9,24,384]{2,1,0:T(8,128)}, f32[9,24,384]{2,1,0:T(8,128)S(1)}, u32[]{:S(2)}, u32[]{:S(2)}) collective-permute-start(f32[9,24,384]{2,1,0:T(8,128)} %get-tuple-element.42), channel_id=1, source_target_pairs={{0,112},{1,113},{2,114},{3,115},{4,116},{5,117},{6,118},{7,119},{8... | collective-permute-start | bytes 995336 | tf_op jit(solution)/shard_map/ppermute | solution.py:747
  4.2 14.5 %collective-permute-start.1 = (f32[27,384]{1,0:T(8,128)}, f32[27,384]{1,0:T(8,128)S(1)}, u32[]{:S(2)}, u32[]{:S(2)}) collective-permute-start(f32[27,384]{1,0:T(8,128)} %get-tuple-element.43), channel_id=1, source_target_pairs={{0,15},{1,0},{2,1},{3,2},{4,3},{5,4},{6,5},{7,6},{8,7},{9,8},{10,9... | collective-permute-start | bytes 124424 | tf_op jit(solution)/shard_map/ppermute | solution.py:747
  9.2 9.5 %collective-permute-start.2 = (f32[9,384]{1,0:T(8,128)}, f32[9,384]{1,0:T(8,128)S(1)}, u32[]{:S(2)}, u32[]{:S(2)}) collective-permute-start(f32[9,384]{1,0:T(8,128)} %get-tuple-element.44), channel_id=1, source_target_pairs={{0,127},{1,112},{2,113},{3,114},{4,115},{5,116},{6,117},{7,118},{8... | collective-permute-start | bytes 41480 | tf_op jit(solution)/shard_map/ppermute | solution.py:747
  13.4 1.0 %copy-start.1 = (f32[3,3,24,384]{3,2,1,0:T(8,128)S(1)}, f32[3,3,24,384]{3,2,1,0:T(8,128)}, u32[]{:S(2)}) copy-start(f32[3,3,24,384]{3,2,1,0:T(8,128)} %d_ref.5) | copy-start | bytes 995332
  14.3 1.0 %copy-start.3 = (f32[3,3,24,384]{3,2,1,0:T(8,128)S(1)}, f32[3,3,24,384]{3,2,1,0:T(8,128)}, u32[]{:S(2)}) copy-start(f32[3,3,24,384]{3,2,1,0:T(8,128)} %vel_ref.1) | copy-start | bytes 995332
  15.3 1.0 %copy-start.5 = (s32[3,3,24,384]{3,2,1,0:T(8,128)S(1)}, s32[3,3,24,384]{3,2,1,0:T(8,128)}, u32[]{:S(2)}) copy-start(s32[3,3,24,384]{3,2,1,0:T(8,128)} %f_ref.3) | copy-start | bytes 995332
  32.8 4.3 %collective-permute-start.4 = (f32[232,128]{1,0:T(8,128)S(1)}, f32[232,128]{1,0:T(8,128)S(1)}, u32[]{:S(2)}, u32[]{:S(2)}) collective-permute-start(f32[232,128]{1,0:T(8,128)S(1)} %get-tuple-element.46.minus_ref), channel_id=1, source_target_pairs={{0,112},{1,113},{2,114},{3,115},{4,116},{5,117},{6,118},{7,119},{8... | collective-permute-start | bytes 356360 | tf_op jit(solution)/shard_map/ppermute | solution.py:747
  33.1 4.0 %collective-permute-start.3 = (f32[232,128]{1,0:T(8,128)S(1)}, f32[232,128]{1,0:T(8,128)S(1)}, u32[]{:S(2)}, u32[]{:S(2)}) collective-permute-start(f32[232,128]{1,0:T(8,128)S(1)} %get-tuple-element.47.plus_ref), channel_id=1, source_target_pairs={{0,16},{1,17},{2,18},{3,19},{4,20},{5,21},{6,22},{7,23},{8,24},{9,... | collective-permute-start | bytes 356360 | tf_op jit(solution)/shard_map/ppermute | solution.py:747
  37.1 6.0 %collective-permute-start.5 = (f32[40,128]{1,0:T(8,128)S(1)}, f32[40,128]{1,0:T(8,128)S(1)}, u32[]{:S(2)}, u32[]{:S(2)}) collective-permute-start(f32[40,128]{1,0:T(8,128)S(1)} %get-tuple-element.53), channel_id=1, source_target_pairs={{0,1},{1,2},{2,3},{3,4},{4,5},{5,6},{6,7},{7,8},{8,9},{9,10},{10,1... | collective-permute-start | bytes 61448 | tf_op jit(solution)/shard_map/ppermute | solution.py:747
  38.1 5.0 %collective-permute-start.6 = (f32[40,128]{1,0:T(8,128)S(1)}, f32[40,128]{1,0:T(8,128)S(1)}, u32[]{:S(2)}, u32[]{:S(2)}) collective-permute-start(f32[40,128]{1,0:T(8,128)S(1)} %get-tuple-element.54), channel_id=1, source_target_pairs={{0,15},{1,0},{2,1},{3,2},{4,3},{5,4},{6,5},{7,6},{8,7},{9,8},{10,9... | collective-permute-start | bytes 61448 | tf_op jit(solution)/shard_map/ppermute | solution.py:747
  45.4 5.4 %collective-permute-start.8 = (f32[232,128]{1,0:T(8,128)S(1)}, f32[232,128]{1,0:T(8,128)S(1)}, u32[]{:S(2)}, u32[]{:S(2)}) collective-permute-start(f32[232,128]{1,0:T(8,128)S(1)} %get-tuple-element.58.minus_ref), channel_id=1, source_target_pairs={{0,112},{1,113},{2,114},{3,115},{4,116},{5,117},{6,118},{7,119},{8... | collective-permute-start | bytes 356360 | tf_op jit(solution)/shard_map/ppermute | solution.py:747
  48.5 2.3 %collective-permute-start.7 = (f32[232,128]{1,0:T(8,128)S(1)}, f32[232,128]{1,0:T(8,128)S(1)}, u32[]{:S(2)}, u32[]{:S(2)}) collective-permute-start(f32[232,128]{1,0:T(8,128)S(1)} %get-tuple-element.59.plus_ref), channel_id=1, source_target_pairs={{0,16},{1,17},{2,18},{3,19},{4,20},{5,21},{6,22},{7,23},{8,24},{9,... | collective-permute-start | bytes 356360 | tf_op jit(solution)/shard_map/ppermute | solution.py:747
  50.8 6.3 %collective-permute-start.9 = (f32[40,128]{1,0:T(8,128)S(1)}, f32[40,128]{1,0:T(8,128)S(1)}, u32[]{:S(2)}, u32[]{:S(2)}) collective-permute-start(f32[40,128]{1,0:T(8,128)S(1)} %get-tuple-element.62), channel_id=1, source_target_pairs={{0,1},{1,2},{2,3},{3,4},{4,5},{5,6},{6,7},{7,8},{8,9},{9,10},{10,1... | collective-permute-start | bytes 61448 | tf_op jit(solution)/shard_map/ppermute | solution.py:747
  50.9 6.2 %collective-permute-start.10 = (f32[40,128]{1,0:T(8,128)S(1)}, f32[40,128]{1,0:T(8,128)S(1)}, u32[]{:S(2)}, u32[]{:S(2)}) collective-permute-start(f32[40,128]{1,0:T(8,128)S(1)} %get-tuple-element.63), channel_id=1, source_target_pairs={{0,15},{1,0},{2,1},{3,2},{4,3},{5,4},{6,5},{7,6},{8,7},{9,8},{10,9... | collective-permute-start | bytes 61448 | tf_op jit(solution)/shard_map/ppermute | solution.py:747
  59.4 5.4 %collective-permute-start.12 = (f32[232,128]{1,0:T(8,128)S(1)}, f32[232,128]{1,0:T(8,128)S(1)}, u32[]{:S(2)}, u32[]{:S(2)}) collective-permute-start(f32[232,128]{1,0:T(8,128)S(1)} %get-tuple-element.64.minus_ref), channel_id=1, source_target_pairs={{0,112},{1,113},{2,114},{3,115},{4,116},{5,117},{6,118},{7,119},{8... | collective-permute-start | bytes 356360 | tf_op jit(solution)/shard_map/ppermute | solution.py:747
  63.4 1.8 %collective-permute-start.11 = (f32[232,128]{1,0:T(8,128)S(1)}, f32[232,128]{1,0:T(8,128)S(1)}, u32[]{:S(2)}, u32[]{:S(2)}) collective-permute-start(f32[232,128]{1,0:T(8,128)S(1)} %get-tuple-element.65.plus_ref), channel_id=1, source_target_pairs={{0,16},{1,17},{2,18},{3,19},{4,20},{5,21},{6,22},{7,23},{8,24},{9,... | collective-permute-start | bytes 356360 | tf_op jit(solution)/shard_map/ppermute | solution.py:747
  65.3 6.4 %collective-permute-start.13 = (f32[40,128]{1,0:T(8,128)S(1)}, f32[40,128]{1,0:T(8,128)S(1)}, u32[]{:S(2)}, u32[]{:S(2)}) collective-permute-start(f32[40,128]{1,0:T(8,128)S(1)} %get-tuple-element.68), channel_id=1, source_target_pairs={{0,1},{1,2},{2,3},{3,4},{4,5},{5,6},{6,7},{7,8},{8,9},{9,10},{10,1... | collective-permute-start | bytes 61448 | tf_op jit(solution)/shard_map/ppermute | solution.py:747
  65.4 6.3 %collective-permute-start.14 = (f32[40,128]{1,0:T(8,128)S(1)}, f32[40,128]{1,0:T(8,128)S(1)}, u32[]{:S(2)}, u32[]{:S(2)}) collective-permute-start(f32[40,128]{1,0:T(8,128)S(1)} %get-tuple-element.69), channel_id=1, source_target_pairs={{0,15},{1,0},{2,1},{3,2},{4,3},{5,4},{6,5},{7,6},{8,7},{9,8},{10,9... | collective-permute-start | bytes 61448 | tf_op jit(solution)/shard_map/ppermute | solution.py:747
  71.7 21.8 %copy-start.2 = (f32[3,3,24,384]{3,2,1,0:T(8,128)S(1)}, f32[3,3,24,384]{3,2,1,0:T(8,128)}, u32[]{:S(2)}) copy-start(f32[3,3,24,384]{3,2,1,0:T(8,128)} %d_ref.5) | copy-start | bytes 995332
  71.7 21.8 %copy-start.4 = (f32[3,3,24,384]{3,2,1,0:T(8,128)S(1)}, f32[3,3,24,384]{3,2,1,0:T(8,128)}, u32[]{:S(2)}) copy-start(f32[3,3,24,384]{3,2,1,0:T(8,128)} %vel_ref.1) | copy-start | bytes 995332

commit v4 on v3

--- a/solution.py
+++ b/solution.py
@@ -46,38 +46,41 @@
     return values, slopes, thermo
 
 
-def even_odd(matrix):
-    even = [[float((matrix[q, a] + matrix[q, 3 - a]) / 2) for a in range(2)] for q in range(3)]
-    odd = [[float((matrix[q, a] - matrix[q, 3 - a]) / 2) for a in range(2)] for q in range(3)]
-    return even, odd
-
-
 VALUES, SLOPES, THERMO = tables()
-BE, BO = even_odd(VALUES)
-DE, DO = even_odd(SLOPES)
+LOBATTO = np.array([0.0, 0.5 - 0.5 / math.sqrt(5.0), 0.5 + 0.5 / math.sqrt(5.0), 1.0]) - 0.5
+ABSCISSA = VALUES @ LOBATTO
+INVERSE = float(0.5 / LOBATTO[1])
+RATIO = float(LOBATTO[0] / LOBATTO[1])
+BK = [float((VALUES[q, 0] + VALUES[q, 3]) / 2) for q in range(3)]
+BM = [float((VALUES[q, 0] - VALUES[q, 3]) / 2) for q in range(3)]
+BL = [float(ABSCISSA[q]) for q in range(3)]
+DK = [float((SLOPES[q, 0] + SLOPES[q, 3]) / 2) for q in range(3)]
+DM = [float((SLOPES[q, 0] - SLOPES[q, 3]) / 2) for q in range(3)]
 TE = [float((THERMO[q, 0] + THERMO[q, 2]) / 2) for q in range(3)]
 TO = [float((THERMO[q, 0] - THERMO[q, 2]) / 2) for q in range(3)]
 TM = [float(THERMO[q, 1]) for q in range(3)]
 
 
 def butterfly(u):
-    return [u[0] + u[3], u[1] + u[2], u[0] - u[3], u[1] - u[2]]
+    e0, e1, o0, o1 = u[0] + u[3], u[1] + u[2], u[0] - u[3], u[1] - u[2]
+    return [0.5 * e1, e0 - e1, INVERSE * o1, o0 - RATIO * o1]
 
 
 def unbutterfly(r):
-    return [r[0] + r[2], r[1] + r[3], r[1] - r[3], r[0] - r[2]]
+    e0, e1, o0, o1 = r[1], 0.5 * r[0] - r[1], r[3], INVERSE * r[2] - RATIO * r[3]
+    return [e0 + o0, e1 + o1, e1 - o1, e0 - o0]
 
 
 def interp_pair(h, q):
-    even = BE[q][0] * h[0] + BE[q][1] * h[1]
-    odd = BO[q][0] * h[2] + BO[q][1] * h[3]
+    even = h[0] + BK[q] * h[1]
+    odd = BL[q] * h[2] + BM[q] * h[3]
     return even + odd, even - odd
 
 
 def slope_pair(h, q):
-    even = DE[q][0] * h[0] + DE[q][1] * h[1]
-    odd = DO[q][0] * h[2] + DO[q][1] * h[3]
-    return odd + even, odd - even
+    even = h[2] + DM[q] * h[3]
+    odd = DK[q] * h[1]
+    return even + odd, even - odd
 
 
 def along(pair_fn, h):
@@ -91,23 +94,30 @@
     return term if total is None else total + term
 
 
-def interp_back(f, h=None, sign=1.0):
+def interp_back_pair(h, q, even, odd):
+    h[0] = plus(h[0], even)
+    h[1] = plus(h[1], BK[q] * even)
+    h[2] = plus(h[2], BL[q] * odd)
+    h[3] = plus(h[3], BM[q] * odd)
+
+
+def slope_back_pair(h, q, even, odd):
+    h[1] = plus(h[1], DK[q] * odd)
+    h[2] = plus(h[2], even)
+    h[3] = plus(h[3], DM[q] * even)
+
+
+def interp_back(f, h=None):
     h = [None] * 4 if h is None else list(h)
     for q in range(3):
-        even, odd = f[q] + f[5 - q], f[q] - f[5 - q]
-        for a in range(2):
-            h[a] = plus(h[a], (sign * BE[q][a]) * even)
-            h[2 + a] = plus(h[2 + a], (sign * BO[q][a]) * odd)
+        interp_back_pair(h, q, f[q] + f[5 - q], f[q] - f[5 - q])
     return h
 
 
-def slope_back(f, h=None, sign=1.0):
+def slope_back(f, h=None):
     h = [None] * 4 if h is None else list(h)
     for q in range(3):
-        even, odd = f[q] + f[5 - q], f[q] - f[5 - q]
-        for a in range(2):
-            h[a] = plus(h[a], (sign * DE[q][a]) * odd)
-            h[2 + a] = plus(h[2 + a], (sign * DO[q][a]) * even)
+        slope_back_pair(h, q, f[q] + f[5 - q], f[q] - f[5 - q])
     return h
 
 
@@ -273,9 +283,9 @@
     det = jac[0][0] * cof[0][0] + jac[0][1] * cof[0][1] + jac[0][2] * cof[0][2]
     inv = pl.reciprocal(det, approx=True)
     inv = inv * (2.0 - det * inv)
-    inv = inv * (2.0 - det * inv)
     scale = mass * inv
     shear = (viscosity * scale) * inv
+    twice = shear + shear
     press = scale * energy
     rate = [
         [vel[c][0] * cof[e][0] + vel[c][1] * cof[e][1] + vel[c][2] * cof[e][2] for e in range(3)]
@@ -284,7 +294,7 @@
     stress = [[None] * 3 for _ in range(3)]
     power = None
     for c in range(3):
-        stress[c][c] = shear * (rate[c][c] + rate[c][c]) - press
+        stress[c][c] = twice * rate[c][c] - press
         power = plus(power, stress[c][c] * rate[c][c])
         for d in range(c + 1, 3):
             both = rate[c][d] + rate[d][c]
@@ -329,11 +339,7 @@
     lax.fori_loop(0, 3, body, 0)
 
 
-def force_kernel(
-    u_ref, hx_ref, hy_ref, hc_ref, eq_ref, w_ref,
-    minus_ref, plus_ref, inner_ref, rim_ref, face_mask_ref, rim_mask_ref, power_ref,
-    hx_s, hy_s, q_s, zv_s, zs_s, w_s, xt_s, ya_s, yb_s, zn_s, place,
-):
+def rim_rows(hy_ref, hc_ref, hy_s):
     rows = [
         jnp.concatenate(
             [hy_ref[:, 128 * v : 128 * v + 128], hc_ref[:, 128 * v : 128 * v + 128]], axis=0
@@ -344,25 +350,31 @@
     for t in range(5):
         for g, tile in enumerate(split_lanes([r[8 * t : 8 * t + 8] for r in rows])):
             hy_s[g, 8 * t : 8 * t + 8, :] = tile
+
+
+def mask_kernel(hx_ref, hy_ref, hc_ref, face_mask_ref, rim_mask_ref, hy_s, place):
+    rim_rows(hy_ref, hc_ref, hy_s)
     for x in range(4):
         for c in range(3):
             for g in range(3):
                 r = 9 * x + 6 + c
                 rim_mask_ref[x, c * 3 + g : c * 3 + g + 1, :] = 1.0 - hy_s[g, r : r + 1, :]
-
-    def face(j, _):
-        for i in range(3):
-            k = 3 * j + i
-            tiles = element_rows(lambda s, l: hx_ref[k, s : s + 8, l : l + 128], place.at[i])
-            for n in range(9):
-                hx_s[k, n] = tiles[n]
-        return 0
-
-    lax.fori_loop(0, 3, face, 0)
     for c in range(3):
+        tiles = element_rows(lambda s, l: hx_ref[6 + c, s : s + 8, l : l + 128], place.at[c])
         for n in range(9):
-            face_mask_ref[c * 9 + n] = 1.0 - hx_s[6 + c, n]
-
+            face_mask_ref[c * 9 + n] = 1.0 - tiles[n]
+
+
+def force_kernel(
+    u_ref, hx_ref, hy_ref, hc_ref, eq_ref, w_ref,
+    minus_ref, plus_ref, inner_ref, rim_ref, power_ref,
+    hx_s, hy_s, q_s, zv_s, zs_s, w_s, xt_s, ya_s, yb_s, zn_s, place,
+):
+    rim_rows(hy_ref, hc_ref, hy_s)
+    for k in range(6):
+        tiles = element_rows(lambda s, l: hx_ref[k, s : s + 8, l : l + 128], place.at[k])
+        for n in range(9):
+            hx_s[k, n] = tiles[n]
     def gather_nodes(c, _):
         for g in range(3):
             cols = []
@@ -380,12 +392,17 @@
         return 0
 
     lax.fori_loop(0, 6, gather_nodes, 0)
+    for c, n in ((0, 2 * 4), (1, 2)):
+        for g in range(3):
+            q_s[c, n * 3 + g] = q_s[c, n * 3 + g] + 1.0
 
     def along_z(c, _):
         for n in range(16):
             u = [q_s[c, 3 * n + g] for g in range(3)]
             u.append(next_lane(u[0]))
             h = butterfly(u)
+            if n == 0:
+                h[2] = h[2] + jnp.where(c == 2, 1.0, 0.0)
             for q, t in enumerate(along(interp_pair, h)):
                 zv_s[q, c, n] = t
             for q, t in enumerate(along(slope_pair, h)):
@@ -418,8 +435,7 @@
                         h = [w_s[y, d, c * 4 + x] for x in range(4)]
                         pair = slope_pair(h, q) if d == 0 else interp_pair(h, q)
                         for side in range(2):
-                            t = pair[side]
-                            grads[side][c][d] = t + 1.0 if c == d else t
+                            grads[side][c][d] = pair[side]
                 flux = []
                 for side in range(2):
                     p = q if side == 0 else 5 - q
@@ -430,29 +446,26 @@
                     for f in range(3):
                         even = flux[0][c][f] + flux[1][c][f]
                         odd = flux[0][c][f] - flux[1][c][f]
-                        h = back[c][f]
-                        for a in range(2):
-                            if f == 0:
-                                h[a] = plus(h[a], DE[q][a] * odd)
-                                h[2 + a] = plus(h[2 + a], DO[q][a] * even)
-                            else:
-                                h[a] = plus(h[a], BE[q][a] * even)
-                                h[2 + a] = plus(h[2 + a], BO[q][a] * odd)
+                        (slope_back_pair if f == 0 else interp_back_pair)(back[c][f], q, even, odd)
             for c in range(3):
                 for f in range(3):
                     for x in range(4):
-                        xt_s[y, f, c * 4 + x] = back[c][f][x]
+                        if back[c][f][x] is not None:
+                            xt_s[y, f, c * 4 + x] = back[c][f][x]
             return 0
 
         lax.fori_loop(0, 6, line, 0)
 
         def back_y(c, _):
             for x in range(4):
-                f = [[xt_s[q, d, c * 4 + x] for q in range(6)] for d in range(3)]
-                h = slope_back(f[1], interp_back(f[0]))
+                f = [
+                    [xt_s[q, d, c * 4 + x] for q in range(6)] if d or x else None
+                    for d in range(3)
+                ]
+                h = slope_back(f[1], interp_back(f[0]) if x else None)
                 s = interp_back(f[2])
                 for y in range(4):
-                    ya_s[z, c, x * 4 + y] = h[y]
+                    ya_s[z, c, x * 4 + y] = jnp.zeros((8, 128), F32) if h[y] is None else h[y]
                     yb_s[z, c, x * 4 + y] = s[y]
             return 0
 
@@ -463,12 +476,12 @@
 
     def back_z(c, _):
         for n in range(16):
-            h = interp_back([ya_s[q, c, n] for q in range(6)], sign=-1.0)
-            h = slope_back([yb_s[q, c, n] for q in range(6)], h, sign=-1.0)
+            h = interp_back([ya_s[q, c, n] for q in range(6)])
+            h = slope_back([yb_s[q, c, n] for q in range(6)], h)
             u = unbutterfly(h)
-            zn_s[c, n * 3] = u[0] + previous_lane(u[3])
-            zn_s[c, n * 3 + 1] = u[1]
-            zn_s[c, n * 3 + 2] = u[2]
+            zn_s[c, n * 3] = -(u[0] + previous_lane(u[3]))
+            zn_s[c, n * 3 + 1] = -u[1]
+            zn_s[c, n * 3 + 2] = -u[2]
         return 0
 
     lax.fori_loop(0, 3, back_z, 0)
@@ -786,16 +799,20 @@
         )(displacement, velocity, pinned, dofs, weight)
         out = call(
             force_kernel,
-            PARTS + [(27,) + T, (4, 16, 128), (216,) + T],
+            PARTS + [(216,) + T],
             [
-                (9, 9) + T, (3, 40, 128), (6, 48) + T, (6, 6, 16) + T, (6, 6, 16) + T,
+                (6, 9) + T, (3, 40, 128), (6, 48) + T, (6, 6, 16) + T, (6, 6, 16) + T,
                 (6, 3, 24) + T, (6, 3, 12) + T, (6, 3, 16) + T,
-                (6, 3, 16) + T, (3, 48) + T, (3, 3, 24, 128),
+                (6, 3, 16) + T, (3, 48) + T, (6, 3, 24, 128),
             ],
             "force",
             flops=90000 * 1024,
         )(nodes, hx, hy, hc, heat, weight)
-        parts, (face_mask, rim_mask, power) = out[:4], out[4:]
+        parts, power = out[:4], out[4]
+        face_mask, rim_mask = call(
+            mask_kernel, [(27,) + T, (4, 16, 128)], [(3, 40, 128), (3, 3, 24, 128)], "masks",
+            flops=100 * 1024,
+        )(hx, hy, hc)
         energy_new, token = call(
             energy_kernel, [(27,) + T, T], [(27,) + T, (6, 9) + T, (6, 3) + T], "energy",
             flops=2000 * 1024,

time: 95.6 us -> 99 us (1.036)
  waiting for transfers between devices: 8.86 us -> 15.2 us
  starting transfers between devices: 34.9 us -> 32.4 us
  Pallas kernels: 27.6 us -> 25.8 us
  blocking collectives: 20.2 us -> 21.6 us
    ppermute x15, waiting for transfers between devices: 8.86 us -> 15.2 us  [moved(): return lax.ppermute(value, ('gx', 'gy'), pairs)]
    ppermute x15, starting transfers between devices: 34.9 us -> 32.4 us  [moved(): return lax.ppermute(value, ('gx', 'gy'), pairs)]
    pallas_call x11 -> x12, Pallas kernels: 27.6 us -> 25.8 us  [run(): pl.pallas_call(kernel, out_shape=[jax.ShapeDtypeStruct(s, F32) for s in o...]
    all_to_all x1, blocking collectives: 20.2 us -> 21.6 us  [on_device(): sums = lax.all_to_all(sums, ('gx', 'gy'), 0, 0).reshape(-1, 128)]
  transfers between devices with their start and end apart: 15 -> 15, of which waited for: 7 -> 10; matrix products, arithmetic and copies ran while one was open for 0% -> 0% of each run, Pallas kernels for 4% -> 4%
where the time goes in v4:
time: 99 us; the launch traced here: 98.7 us
  starting transfers between devices  32.4 us (33%)
  Pallas kernels  25.8 us (26%)
  blocking collectives  21.6 us (22%)
  waiting for transfers between devices  15.2 us (15%)
  local copies, waits for them, and re-layouts  2.94 us (3%)
    ppermute x15, starting transfers between devices, moved(): return lax.ppermute(value, ('gx', 'gy'), pairs)  32.4 us
    pallas_call x12, Pallas kernels, run(): pl.pallas_call(kernel, out_shape=[jax.ShapeDtypeStruct(s, F32) for s in o...  25.8 us
    all_to_all x1, blocking collectives, on_device(): sums = lax.all_to_all(sums, ('gx', 'gy'), 0, 0).reshape(-1, 128)  21.6 us
    ppermute x15, waiting for transfers between devices, moved(): return lax.ppermute(value, ('gx', 'gy'), pairs)  15.2 us
    unnamed x14, local copies, waits for them, and re-layouts  2.94 us
  transfers between devices with their start and end apart: 15, of which 10 were waited for; matrix products, arithmetic and copies ran while one was open for 0% of the time, Pallas kernels for 4%

profile of v4, /device:TPU:1, one launch (start us, length us, event | category | flops | bytes accessed | tf_op | source)
XLA Modules:
  0.0 98.7 jit_solution(2998479324353166302)
XLA Ops:
  0.6 0.0 copy-start
  0.6 0.0 copy-start.6
  0.7 2.1 %pack.1 = (f32[9,24,384]{2,1,0:T(8,128)}, f32[27,384]{1,0:T(8,128)}, f32[9,384]{1,0:T(8,128)}) custom-call(f32[3,3,24,384]{3,2,1,0:T(8,128)} %d_ref.5, f32[3,3,24,384]{3,2,1,0:T(8,128)} %vel_ref.1, s32[3,3,24,384]{3,2,1,0:T(8,128)} %f_ref.3), custom_call_target="tpu_custom_call" | custom-call | bytes 1382400 | tf_op jit(solution)/shard_map/pack/pallas_call | solution.py:733
  2.7 1.4 %collective-permute-start = (f32[9,24,384]{2,1,0:T(8,128)}, f32[9,24,384]{2,1,0:T(8,128)S(1)}, u32[]{:S(2)}, u32[]{:S(2)}) collective-permute-start(f32[9,24,384]{2,1,0:T(8,128)} %get-tuple-element.42), channel_id=1, source_target_pairs={{0,112},{1,113},{2,114},{3,115},{4,116},{5,117},{6,118},{7,119},{8... | collective-permute-start | bytes 995336 | tf_op jit(solution)/shard_map/ppermute | solution.py:760
  4.2 5.0 %collective-permute-start.1 = (f32[27,384]{1,0:T(8,128)}, f32[27,384]{1,0:T(8,128)S(1)}, u32[]{:S(2)}, u32[]{:S(2)}) collective-permute-start(f32[27,384]{1,0:T(8,128)} %get-tuple-element.43), channel_id=1, source_target_pairs={{0,15},{1,0},{2,1},{3,2},{4,3},{5,4},{6,5},{7,6},{8,7},{9,8},{10,9... | collective-permute-start | bytes 124424 | tf_op jit(solution)/shard_map/ppermute | solution.py:760
  9.2 4.2 %collective-permute-start.2 = (f32[9,384]{1,0:T(8,128)}, f32[9,384]{1,0:T(8,128)S(1)}, u32[]{:S(2)}, u32[]{:S(2)}) collective-permute-start(f32[9,384]{1,0:T(8,128)} %get-tuple-element.44), channel_id=1, source_target_pairs={{0,127},{1,112},{2,113},{3,114},{4,115},{5,116},{6,117},{7,118},{8... | collective-permute-start | bytes 41480 | tf_op jit(solution)/shard_map/ppermute | solution.py:760
  13.4 0.0 copy-done
  13.4 0.0 copy-done.6
  13.4 0.0 copy-start.1
  13.4 1.0 copy-done.1
  14.3 0.0 copy-start.3
  14.3 1.0 copy-done.3
  15.3 0.0 copy-start.5
  15.3 1.0 copy-done.5
  16.3 2.3 %prep.1 = (f32[6,27,8,128]{3,2,1,0:T(8,128)S(1)}, f32[3,27,8,128]{3,2,1,0:T(8,128)S(1)}, f32[216,8,128]{2,1,0:T(8,128)S(1)}, f32[27,8,128]{2,1,0:T(8,128)S(1)}) custom-call(f32[3,3,24,384]{3,2,1,0:T(8,128)S(1)} %copy-done.1, f32[3,3,24,384]{3,2,1,0:T(8,128)S(1)} %copy-done.3, s32[3,3,24,384]{3,2,1,0:T(8,128)S(1)} %copy-done.5, f32[27,8,128]{2,1,0:T(8,128)S(1)} %bitcast.14, ...), custom_call_target="tpu_custom_call" | custom-call | flops 4096000 | bytes 3981312 | tf_op jit(solution)/shard_map/prep/pallas_call | solution.py:733
  18.6 0.0 collective-permute-done.2.hc_ref
  18.6 0.0 collective-permute-done.1.hy_ref
  18.7 0.0 collective-permute-done.hx_ref
  18.7 12.2 %force.1 = (f32[232,128]{1,0:T(8,128)S(1)}, f32[232,128]{1,0:T(8,128)S(1)}, f32[2,27,8,128]{3,2,1,0:T(8,128)S(1)}, f32[2,16,128]{2,1,0:T(8,128)S(1)}, f32[216,8,128]{2,1,0:T(8,128)S(1)}) custom-call(f32[6,27,8,128]{3,2,1,0:T(8,128)S(1)} %get-tuple-element.41.u_ref, f32[9,24,384]{2,1,0:T(8,128)S(1)} %collective-permute-done.hx_ref, ...), custom_call_target="tpu_custom_call" | custom-call | flops 92160000 | bytes 4179968 | tf_op jit(solution)/shard_map/force/pallas_call | solution.py:733
  30.9 0.0 collective-permute-start.3
  30.9 0.5 collective-permute-start.4
  31.4 1.1 %energy.1 = (f32[27,8,128]{2,1,0:T(8,128)}, f32[8,128]{1,0:T(8,128)S(1)}) custom-call(f32[216,8,128]{2,1,0:T(8,128)S(1)} %get-tuple-element.50.power_ref, f32[27,8,128]{2,1,0:T(8,128)S(1)} %get-tuple-element.51.lump_ref, f32[27,8,128]{2,1,0:T(8,128)S(1)} %bitcast.15), custom_call_target="tpu_custom_call" | custom-call | flops 2048000 | bytes 1220608 | tf_op jit(solution)/shard_map/energy/pallas_call | solution.py:733
  32.5 0.2 collective-permute-done.3.got_low_ref.low_ref
  32.7 2.7 %collective-permute-done.4.got_high_ref.high_ref = f32[232,128]{1,0:T(8,128)S(1)} collective-permute-done((f32[232,128]{1,0:T(8,128)S(1)}, f32[232,128]{1,0:T(8,128)S(1)}, u32[]{:S(2)}, u32[]{:S(2)}) %collective-permute-start.4) | collective-permute-done | bytes 118816 | tf_op jit(solution)/shard_map/ppermute | solution.py:760
  35.5 1.0 collective-permute-start.5
  36.5 3.9 %collective-permute-start.6 = (f32[40,128]{1,0:T(8,128)S(1)}, f32[40,128]{1,0:T(8,128)S(1)}, u32[]{:S(2)}, u32[]{:S(2)}) collective-permute-start(f32[40,128]{1,0:T(8,128)S(1)} %get-tuple-element.54), channel_id=1, source_target_pairs={{0,15},{1,0},{2,1},{3,2},{4,3},{5,4},{6,5},{7,6},{8,7},{9,8},{10,9... | collective-permute-start | bytes 61448 | tf_op jit(solution)/shard_map/ppermute | solution.py:760
  40.4 0.4 masks.1
  40.7 0.8 collective-permute-done.5.from_down_ref
  41.5 0.0 collective-permute-done.6.from_up_ref
  41.5 2.1 %apply.2 = (f32[3,27,8,128]{3,2,1,0:T(8,128)S(1)}, f32[232,128]{1,0:T(8,128)S(1)}, f32[232,128]{1,0:T(8,128)S(1)}, f32[2,27,8,128]{3,2,1,0:T(8,128)S(1)}, f32[2,16,128]{2,1,0:T(8,128)S(1)}) custom-call(f32[232,128]{1,0:T(8,128)S(1)} %get-tuple-element.46.minus_ref, f32[232,128]{1,0:T(8,128)S(1)} %get-tuple-element.47.plus_ref, ...), custom_call_target="tpu_custom_call" | custom-call | flops 13312000 | bytes 2920448 | tf_op jit(solution)/shard_map/apply/pallas_call | solution.py:733
  43.7 0.9 collective-permute-start.7
  44.5 1.5 %collective-permute-start.8 = (f32[232,128]{1,0:T(8,128)S(1)}, f32[232,128]{1,0:T(8,128)S(1)}, u32[]{:S(2)}, u32[]{:S(2)}) collective-permute-start(f32[232,128]{1,0:T(8,128)S(1)} %get-tuple-element.58.minus_ref), channel_id=1, source_target_pairs={{0,112},{1,113},{2,114},{3,115},{4,116},{5,117},{6,118},{7,119},{8... | collective-permute-start | bytes 356360 | tf_op jit(solution)/shard_map/ppermute | solution.py:760
  46.0 0.8 collective-permute-done.7.got_low_ref.low_ref
  46.8 2.0 %collective-permute-done.8.got_high_ref.high_ref = f32[232,128]{1,0:T(8,128)S(1)} collective-permute-done((f32[232,128]{1,0:T(8,128)S(1)}, f32[232,128]{1,0:T(8,128)S(1)}, u32[]{:S(2)}, u32[]{:S(2)}) %collective-permute-start.8) | collective-permute-done | bytes 118816 | tf_op jit(solution)/shard_map/ppermute | solution.py:760
  48.8 5.1 %collective-permute-start.10 = (f32[40,128]{1,0:T(8,128)S(1)}, f32[40,128]{1,0:T(8,128)S(1)}, u32[]{:S(2)}, u32[]{:S(2)}) collective-permute-start(f32[40,128]{1,0:T(8,128)S(1)} %get-tuple-element.63), channel_id=1, source_target_pairs={{0,15},{1,0},{2,1},{3,2},{4,3},{5,4},{6,5},{7,6},{8,7},{9,8},{10,9... | collective-permute-start | bytes 61448 | tf_op jit(solution)/shard_map/ppermute | solution.py:760
  53.9 0.0 collective-permute-start.9
  53.9 0.9 collective-permute-done.10.from_up_ref
  54.8 5.0 %collective-permute-done.9.from_down_ref = f32[40,128]{1,0:T(8,128)S(1)} collective-permute-done((f32[40,128]{1,0:T(8,128)S(1)}, f32[40,128]{1,0:T(8,128)S(1)}, u32[]{:S(2)}, u32[]{:S(2)}) %collective-permute-start.9) | collective-permute-done | bytes 20512 | tf_op jit(solution)/shard_map/ppermute | solution.py:760
  59.9 2.1 %apply.3 = (f32[3,27,8,128]{3,2,1,0:T(8,128)S(1)}, f32[232,128]{1,0:T(8,128)S(1)}, f32[232,128]{1,0:T(8,128)S(1)}, f32[2,27,8,128]{3,2,1,0:T(8,128)S(1)}, f32[2,16,128]{2,1,0:T(8,128)S(1)}) custom-call(f32[232,128]{1,0:T(8,128)S(1)} %get-tuple-element.58.minus_ref, f32[232,128]{1,0:T(8,128)S(1)} %get-tuple-element.59.plus_ref, ...), custom_call_target="tpu_custom_call" | custom-call | flops 13312000 | bytes 2920448 | tf_op jit(solution)/shard_map/apply/pallas_call | solution.py:733
  62.0 1.4 %collective-permute-start.11 = (f32[232,128]{1,0:T(8,128)S(1)}, f32[232,128]{1,0:T(8,128)S(1)}, u32[]{:S(2)}, u32[]{:S(2)}) collective-permute-start(f32[232,128]{1,0:T(8,128)S(1)} %get-tuple-element.65.plus_ref), channel_id=1, source_target_pairs={{0,16},{1,17},{2,18},{3,19},{4,20},{5,21},{6,22},{7,23},{8,24},{9,... | collective-permute-start | bytes 356360 | tf_op jit(solution)/shard_map/ppermute | solution.py:760
  63.5 2.7 %collective-permute-start.12 = (f32[232,128]{1,0:T(8,128)S(1)}, f32[232,128]{1,0:T(8,128)S(1)}, u32[]{:S(2)}, u32[]{:S(2)}) collective-permute-start(f32[232,128]{1,0:T(8,128)S(1)} %get-tuple-element.64.minus_ref), channel_id=1, source_target_pairs={{0,112},{1,113},{2,114},{3,115},{4,116},{5,117},{6,118},{7,119},{8... | collective-permute-start | bytes 356360 | tf_op jit(solution)/shard_map/ppermute | solution.py:760
  66.2 0.8 collective-permute-done.11.got_low_ref.low_ref
  67.0 0.8 collective-permute-done.12.got_high_ref.high_ref
  67.8 0.1 collective-permute-start.13
  67.8 4.8 %collective-permute-start.14 = (f32[40,128]{1,0:T(8,128)S(1)}, f32[40,128]{1,0:T(8,128)S(1)}, u32[]{:S(2)}, u32[]{:S(2)}) collective-permute-start(f32[40,128]{1,0:T(8,128)S(1)} %get-tuple-element.69), channel_id=1, source_target_pairs={{0,15},{1,0},{2,1},{3,2},{4,3},{5,4},{6,5},{7,6},{8,7},{9,8},{10,9... | collective-permute-start | bytes 61448 | tf_op jit(solution)/shard_map/ppermute | solution.py:760
  72.6 1.2 %collective-permute-done.13.from_down_ref = f32[40,128]{1,0:T(8,128)S(1)} collective-permute-done((f32[40,128]{1,0:T(8,128)S(1)}, f32[40,128]{1,0:T(8,128)S(1)}, u32[]{:S(2)}, u32[]{:S(2)}) %collective-permute-start.13) | collective-permute-done | bytes 20512 | tf_op jit(solution)/shard_map/ppermute | solution.py:760
  73.8 0.0 collective-permute-done.14.from_up_ref
  73.8 0.0 copy-start.2
  73.8 0.0 copy-start.4
  73.8 1.6 %moments.1 = (f32[3,27,8,128]{3,2,1,0:T(8,128)S(1)}, f32[128,128]{1,0:T(8,128)S(1)}) custom-call(f32[232,128]{1,0:T(8,128)S(1)} %get-tuple-element.64.minus_ref, f32[232,128]{1,0:T(8,128)S(1)} %get-tuple-element.65.plus_ref, f32[2,27,8,128]{3,2,1,0:T(8,128)S(1)} %get-tuple-element.66.inner_ref, f32[2,16,128]{2,1,0:T(8,128)S(1)} %get-tuple-element.67.rim_ref, ...), custom_call_target="tpu_custom_call" | custom-call | flops 8192000 | bytes 3174400 | tf_op jit(solution)/shard_map/moments/pallas_call | solution.py:733
  75.4 21.6 %all_to_all.5 = f32[128,1,128]{2,1,0:T(1,128)S(1)} all-to-all(f32[128,1,128]{2,1,0:T(1,128)S(1)} %bitcast.17), channel_id=1, replica_groups=mesh['gx'=8,'gy'=16] {'gx','gy'}, dimensions={0} | all-to-all | bytes 131072 | tf_op jit(solution)/shard_map/all_to_all | solution.py:833
  96.9 0.0 copy-done.2
  96.9 0.0 copy-done.4
  96.9 1.8 %final.1 = (f32[3,3,24,384]{3,2,1,0:T(8,128)}, f32[3,3,24,384]{3,2,1,0:T(8,128)}, f32[3,3,24,384]{3,2,1,0:T(8,128)}) custom-call(f32[128,128]{1,0:T(8,128)S(1)} %bitcast.16, f32[3,27,8,128]{3,2,1,0:T(8,128)S(1)} %get-tuple-element.70.r_ref, f32[3,27,8,128]{3,2,1,0:T(8,128)S(1)} %get-tuple-element.71.v_ref, f32[3,27,8,128]{3,2,1,0:T(8,128)S(1)} %get-tuple-element.73.w_ref, ...), custom_call_target="tpu_custom_call" | custom-call | flops 1024000 | bytes 2719744 | tf_op jit(solution)/shard_map/final/pallas_call | solution.py:733
  (3 shorter events, 0.1 us)
Async XLA Ops:
  0.6 12.7 %copy-start = (f32[216,1,8,128]{3,2,1,0:T(8,128)S(1)}, f32[216,1,8,128]{3,2,1,0:T(8,128)}, u32[]{:S(2)}) copy-start(f32[216,1,8,128]{3,2,1,0:T(8,128)} %param.8) | copy-start | bytes 2654212
  0.6 12.7 %copy-start.6 = (f32[27,1,8,128]{3,2,1,0:T(8,128)S(1)}, f32[27,1,8,128]{3,2,1,0:T(8,128)}, u32[]{:S(2)}) copy-start(f32[27,1,8,128]{3,2,1,0:T(8,128)} %param.7) | copy-start | bytes 331780
  2.7 15.9 %collective-permute-start = (f32[9,24,384]{2,1,0:T(8,128)}, f32[9,24,384]{2,1,0:T(8,128)S(1)}, u32[]{:S(2)}, u32[]{:S(2)}) collective-permute-start(f32[9,24,384]{2,1,0:T(8,128)} %get-tuple-element.42), channel_id=1, source_target_pairs={{0,112},{1,113},{2,114},{3,115},{4,116},{5,117},{6,118},{7,119},{8... | collective-permute-start | bytes 995336 | tf_op jit(solution)/shard_map/ppermute | solution.py:760
  4.2 14.5 %collective-permute-start.1 = (f32[27,384]{1,0:T(8,128)}, f32[27,384]{1,0:T(8,128)S(1)}, u32[]{:S(2)}, u32[]{:S(2)}) collective-permute-start(f32[27,384]{1,0:T(8,128)} %get-tuple-element.43), channel_id=1, source_target_pairs={{0,15},{1,0},{2,1},{3,2},{4,3},{5,4},{6,5},{7,6},{8,7},{9,8},{10,9... | collective-permute-start | bytes 124424 | tf_op jit(solution)/shard_map/ppermute | solution.py:760
  9.2 9.5 %collective-permute-start.2 = (f32[9,384]{1,0:T(8,128)}, f32[9,384]{1,0:T(8,128)S(1)}, u32[]{:S(2)}, u32[]{:S(2)}) collective-permute-start(f32[9,384]{1,0:T(8,128)} %get-tuple-element.44), channel_id=1, source_target_pairs={{0,127},{1,112},{2,113},{3,114},{4,115},{5,116},{6,117},{7,118},{8... | collective-permute-start | bytes 41480 | tf_op jit(solution)/shard_map/ppermute | solution.py:760
  13.4 1.0 copy-start.1
  14.3 1.0 copy-start.3
  15.3 1.0 copy-start.5
  30.9 1.9 %collective-permute-start.3 = (f32[232,128]{1,0:T(8,128)S(1)}, f32[232,128]{1,0:T(8,128)S(1)}, u32[]{:S(2)}, u32[]{:S(2)}) collective-permute-start(f32[232,128]{1,0:T(8,128)S(1)} %get-tuple-element.47.plus_ref), channel_id=1, source_target_pairs={{0,16},{1,17},{2,18},{3,19},{4,20},{5,21},{6,22},{7,23},{8,24},{9,... | collective-permute-start | bytes 356360 | tf_op jit(solution)/shard_map/ppermute | solution.py:760
  30.9 4.6 %collective-permute-start.4 = (f32[232,128]{1,0:T(8,128)S(1)}, f32[232,128]{1,0:T(8,128)S(1)}, u32[]{:S(2)}, u32[]{:S(2)}) collective-permute-start(f32[232,128]{1,0:T(8,128)S(1)} %get-tuple-element.46.minus_ref), channel_id=1, source_target_pairs={{0,112},{1,113},{2,114},{3,115},{4,116},{5,117},{6,118},{7,119},{8... | collective-permute-start | bytes 356360 | tf_op jit(solution)/shard_map/ppermute | solution.py:760
  35.5 6.0 %collective-permute-start.5 = (f32[40,128]{1,0:T(8,128)S(1)}, f32[40,128]{1,0:T(8,128)S(1)}, u32[]{:S(2)}, u32[]{:S(2)}) collective-permute-start(f32[40,128]{1,0:T(8,128)S(1)} %get-tuple-element.53), channel_id=1, source_target_pairs={{0,1},{1,2},{2,3},{3,4},{4,5},{5,6},{6,7},{7,8},{8,9},{9,10},{10,1... | collective-permute-start | bytes 61448 | tf_op jit(solution)/shard_map/ppermute | solution.py:760
  36.5 5.0 %collective-permute-start.6 = (f32[40,128]{1,0:T(8,128)S(1)}, f32[40,128]{1,0:T(8,128)S(1)}, u32[]{:S(2)}, u32[]{:S(2)}) collective-permute-start(f32[40,128]{1,0:T(8,128)S(1)} %get-tuple-element.54), channel_id=1, source_target_pairs={{0,15},{1,0},{2,1},{3,2},{4,3},{5,4},{6,5},{7,6},{8,7},{9,8},{10,9... | collective-permute-start | bytes 61448 | tf_op jit(solution)/shard_map/ppermute | solution.py:760
  43.7 3.1 %collective-permute-start.7 = (f32[232,128]{1,0:T(8,128)S(1)}, f32[232,128]{1,0:T(8,128)S(1)}, u32[]{:S(2)}, u32[]{:S(2)}) collective-permute-start(f32[232,128]{1,0:T(8,128)S(1)} %get-tuple-element.59.plus_ref), channel_id=1, source_target_pairs={{0,16},{1,17},{2,18},{3,19},{4,20},{5,21},{6,22},{7,23},{8,24},{9,... | collective-permute-start | bytes 356360 | tf_op jit(solution)/shard_map/ppermute | solution.py:760
  44.5 4.3 %collective-permute-start.8 = (f32[232,128]{1,0:T(8,128)S(1)}, f32[232,128]{1,0:T(8,128)S(1)}, u32[]{:S(2)}, u32[]{:S(2)}) collective-permute-start(f32[232,128]{1,0:T(8,128)S(1)} %get-tuple-element.58.minus_ref), channel_id=1, source_target_pairs={{0,112},{1,113},{2,114},{3,115},{4,116},{5,117},{6,118},{7,119},{8... | collective-permute-start | bytes 356360 | tf_op jit(solution)/shard_map/ppermute | solution.py:760
  48.8 6.0 %collective-permute-start.10 = (f32[40,128]{1,0:T(8,128)S(1)}, f32[40,128]{1,0:T(8,128)S(1)}, u32[]{:S(2)}, u32[]{:S(2)}) collective-permute-start(f32[40,128]{1,0:T(8,128)S(1)} %get-tuple-element.63), channel_id=1, source_target_pairs={{0,15},{1,0},{2,1},{3,2},{4,3},{5,4},{6,5},{7,6},{8,7},{9,8},{10,9... | collective-permute-start | bytes 61448 | tf_op jit(solution)/shard_map/ppermute | solution.py:760
  53.9 6.0 %collective-permute-start.9 = (f32[40,128]{1,0:T(8,128)S(1)}, f32[40,128]{1,0:T(8,128)S(1)}, u32[]{:S(2)}, u32[]{:S(2)}) collective-permute-start(f32[40,128]{1,0:T(8,128)S(1)} %get-tuple-element.62), channel_id=1, source_target_pairs={{0,1},{1,2},{2,3},{3,4},{4,5},{5,6},{6,7},{7,8},{8,9},{9,10},{10,1... | collective-permute-start | bytes 61448 | tf_op jit(solution)/shard_map/ppermute | solution.py:760
  62.0 4.9 %collective-permute-start.11 = (f32[232,128]{1,0:T(8,128)S(1)}, f32[232,128]{1,0:T(8,128)S(1)}, u32[]{:S(2)}, u32[]{:S(2)}) collective-permute-start(f32[232,128]{1,0:T(8,128)S(1)} %get-tuple-element.65.plus_ref), channel_id=1, source_target_pairs={{0,16},{1,17},{2,18},{3,19},{4,20},{5,21},{6,22},{7,23},{8,24},{9,... | collective-permute-start | bytes 356360 | tf_op jit(solution)/shard_map/ppermute | solution.py:760
  63.5 4.3 %collective-permute-start.12 = (f32[232,128]{1,0:T(8,128)S(1)}, f32[232,128]{1,0:T(8,128)S(1)}, u32[]{:S(2)}, u32[]{:S(2)}) collective-permute-start(f32[232,128]{1,0:T(8,128)S(1)} %get-tuple-element.64.minus_ref), channel_id=1, source_target_pairs={{0,112},{1,113},{2,114},{3,115},{4,116},{5,117},{6,118},{7,119},{8... | collective-permute-start | bytes 356360 | tf_op jit(solution)/shard_map/ppermute | solution.py:760
  67.8 6.0 %collective-permute-start.13 = (f32[40,128]{1,0:T(8,128)S(1)}, f32[40,128]{1,0:T(8,128)S(1)}, u32[]{:S(2)}, u32[]{:S(2)}) collective-permute-start(f32[40,128]{1,0:T(8,128)S(1)} %get-tuple-element.68), channel_id=1, source_target_pairs={{0,1},{1,2},{2,3},{3,4},{4,5},{5,6},{6,7},{7,8},{8,9},{9,10},{10,1... | collective-permute-start | bytes 61448 | tf_op jit(solution)/shard_map/ppermute | solution.py:760
  67.8 5.9 %collective-permute-start.14 = (f32[40,128]{1,0:T(8,128)S(1)}, f32[40,128]{1,0:T(8,128)S(1)}, u32[]{:S(2)}, u32[]{:S(2)}) collective-permute-start(f32[40,128]{1,0:T(8,128)S(1)} %get-tuple-element.69), channel_id=1, source_target_pairs={{0,15},{1,0},{2,1},{3,2},{4,3},{5,4},{6,5},{7,6},{8,7},{9,8},{10,9... | collective-permute-start | bytes 61448 | tf_op jit(solution)/shard_map/ppermute | solution.py:760
  73.8 23.2 %copy-start.2 = (f32[3,3,24,384]{3,2,1,0:T(8,128)S(1)}, f32[3,3,24,384]{3,2,1,0:T(8,128)}, u32[]{:S(2)}) copy-start(f32[3,3,24,384]{3,2,1,0:T(8,128)} %d_ref.5) | copy-start | bytes 995332
  73.8 23.2 %copy-start.4 = (f32[3,3,24,384]{3,2,1,0:T(8,128)S(1)}, f32[3,3,24,384]{3,2,1,0:T(8,128)}, u32[]{:S(2)}) copy-start(f32[3,3,24,384]{3,2,1,0:T(8,128)} %vel_ref.1) | copy-start | bytes 995332

commit v5 on v4

--- a/solution.py
+++ b/solution.py
@@ -260,7 +260,11 @@
             out_ref[3 * n + g] = t
 
 
-def energy_kernel(power_ref, lump_ref, e_ref, out_ref, token_ref, sum_s, z_s, x_s):
+def energy_kernel(
+    power_ref, lump_ref, e_ref, hx_ref, hy_ref, hc_ref,
+    out_ref, token_ref, face_mask_ref, rim_mask_ref, sum_s, z_s, x_s, hy_s, place,
+):
+    masks(hx_ref, hy_ref, hc_ref, face_mask_ref, rim_mask_ref, hy_s, place)
     project(power_ref, z_s, x_s, sum_s)
 
     def body(n, _):
@@ -352,7 +356,7 @@
             hy_s[g, 8 * t : 8 * t + 8, :] = tile
 
 
-def mask_kernel(hx_ref, hy_ref, hc_ref, face_mask_ref, rim_mask_ref, hy_s, place):
+def masks(hx_ref, hy_ref, hc_ref, face_mask_ref, rim_mask_ref, hy_s, place):
     rim_rows(hy_ref, hc_ref, hy_s)
     for x in range(4):
         for c in range(3):
@@ -809,26 +813,25 @@
             flops=90000 * 1024,
         )(nodes, hx, hy, hc, heat, weight)
         parts, power = out[:4], out[4]
-        face_mask, rim_mask = call(
-            mask_kernel, [(27,) + T, (4, 16, 128)], [(3, 40, 128), (3, 3, 24, 128)], "masks",
-            flops=100 * 1024,
-        )(hx, hy, hc)
-        energy_new, token = call(
-            energy_kernel, [(27,) + T, T], [(27,) + T, (6, 9) + T, (6, 3) + T], "energy",
+        energy_new, token, face_mask, rim_mask = call(
+            energy_kernel,
+            [(27,) + T, T, (27,) + T, (4, 16, 128)],
+            [(27,) + T, (6, 9) + T, (6, 3) + T, (3, 40, 128), (3, 3, 24, 128)],
+            "energy",
             flops=2000 * 1024,
-        )(power, lump, dofs)
-        masks = (mask, face_mask, rim_mask)
+        )(power, lump, dofs, hx, hy, hc)
+        free = (mask, face_mask, rim_mask)
         scratch = [
             (3, 48) + T, (6, 3, 16) + T, (3, 4, 6) + T, (6, 3, 16) + T, (3, 48) + T,
         ]
         apply = call(apply_kernel, [(3, 27) + T] + PARTS, scratch, "apply", flops=13000 * 1024)
-        out = apply(*complete(parts, token), *masks, weight)
+        out = apply(*complete(parts, token), *free, weight)
         r, parts = out[0], out[1:]
-        out = apply(*complete(parts), *masks, weight)
+        out = apply(*complete(parts), *free, weight)
         v, parts = out[0], out[1:]
         w, sums = call(
             moments_kernel, [(3, 27) + T, (gx * gy, 128)], scratch[:2], "moments", flops=8000 * 1024
-        )(*complete(parts), *masks, weight, r, v)
+        )(*complete(parts), *free, weight, r, v)
         sums = sums.reshape(gx * gy, -1, 128)
         sums = lax.all_to_all(sums, ("gx", "gy"), 0, 0).reshape(-1, 128)
         shape = displacement.shape

time: 99 us -> 93.4 us (0.943)
  waiting for transfers between devices: 15.2 us -> 8.49 us
  starting transfers between devices: 32.4 us -> 34.9 us
  blocking collectives: 21.6 us -> 20.2 us
    ppermute x15, waiting for transfers between devices: 15.2 us -> 8.49 us  [moved(): return lax.ppermute(value, ('gx', 'gy'), pairs)]
    ppermute x15, starting transfers between devices: 32.4 us -> 34.9 us  [moved(): return lax.ppermute(value, ('gx', 'gy'), pairs)]
    all_to_all x1, blocking collectives: 21.6 us -> 20.2 us  [on_device(): sums = lax.all_to_all(sums, ('gx', 'gy'), 0, 0).reshape(-1, 128)]
    pallas_call x12 -> x11, Pallas kernels: 25.8 us -> 25.8 us  [run(): pl.pallas_call(kernel, out_shape=[jax.ShapeDtypeStruct(s, F32) for s in o...]
  transfers between devices with their start and end apart: 15 -> 15, of which waited for: 10 -> 7; matrix products, arithmetic and copies ran while one was open for 0% -> 0% of each run, Pallas kernels for 4% -> 4%
where the time goes in v5:
time: 93.4 us; the launch traced here: 93.1 us
  starting transfers between devices  34.9 us (37%)
  Pallas kernels  25.8 us (28%)
  blocking collectives  20.2 us (22%)
  waiting for transfers between devices  8.49 us (9%)
  local copies, waits for them, and re-layouts  2.94 us (3%)
    ppermute x15, starting transfers between devices, moved(): return lax.ppermute(value, ('gx', 'gy'), pairs)  34.9 us
    pallas_call x11, Pallas kernels, run(): pl.pallas_call(kernel, out_shape=[jax.ShapeDtypeStruct(s, F32) for s in o...  25.8 us
    all_to_all x1, blocking collectives, on_device(): sums = lax.all_to_all(sums, ('gx', 'gy'), 0, 0).reshape(-1, 128)  20.2 us
    ppermute x15, waiting for transfers between devices, moved(): return lax.ppermute(value, ('gx', 'gy'), pairs)  8.49 us
    unnamed x14, local copies, waits for them, and re-layouts  2.94 us
  transfers between devices with their start and end apart: 15, of which 7 were waited for; matrix products, arithmetic and copies ran while one was open for 0% of the time, Pallas kernels for 4%

profile of v5, /device:TPU:1, one launch (start us, length us, event | category | flops | bytes accessed | tf_op | source)
XLA Modules:
  0.0 93.1 jit_solution(1585379362923959892)
XLA Ops:
  0.6 0.0 copy-start
  0.6 0.0 copy-start.6
  0.7 2.1 %pack.1 = (f32[9,24,384]{2,1,0:T(8,128)}, f32[27,384]{1,0:T(8,128)}, f32[9,384]{1,0:T(8,128)}) custom-call(f32[3,3,24,384]{3,2,1,0:T(8,128)} %d_ref.5, f32[3,3,24,384]{3,2,1,0:T(8,128)} %vel_ref.1, s32[3,3,24,384]{3,2,1,0:T(8,128)} %f_ref.3), custom_call_target="tpu_custom_call" | custom-call | bytes 1382400 | tf_op jit(solution)/shard_map/pack/pallas_call | solution.py:737
  2.7 1.4 %collective-permute-start = (f32[9,24,384]{2,1,0:T(8,128)}, f32[9,24,384]{2,1,0:T(8,128)S(1)}, u32[]{:S(2)}, u32[]{:S(2)}) collective-permute-start(f32[9,24,384]{2,1,0:T(8,128)} %get-tuple-element.42), channel_id=1, source_target_pairs={{0,112},{1,113},{2,114},{3,115},{4,116},{5,117},{6,118},{7,119},{8... | collective-permute-start | bytes 995336 | tf_op jit(solution)/shard_map/ppermute | solution.py:764
  4.2 5.0 %collective-permute-start.1 = (f32[27,384]{1,0:T(8,128)}, f32[27,384]{1,0:T(8,128)S(1)}, u32[]{:S(2)}, u32[]{:S(2)}) collective-permute-start(f32[27,384]{1,0:T(8,128)} %get-tuple-element.43), channel_id=1, source_target_pairs={{0,15},{1,0},{2,1},{3,2},{4,3},{5,4},{6,5},{7,6},{8,7},{9,8},{10,9... | collective-permute-start | bytes 124424 | tf_op jit(solution)/shard_map/ppermute | solution.py:764
  9.2 4.2 %collective-permute-start.2 = (f32[9,384]{1,0:T(8,128)}, f32[9,384]{1,0:T(8,128)S(1)}, u32[]{:S(2)}, u32[]{:S(2)}) collective-permute-start(f32[9,384]{1,0:T(8,128)} %get-tuple-element.44), channel_id=1, source_target_pairs={{0,127},{1,112},{2,113},{3,114},{4,115},{5,116},{6,117},{7,118},{8... | collective-permute-start | bytes 41480 | tf_op jit(solution)/shard_map/ppermute | solution.py:764
  13.4 0.0 copy-done
  13.4 0.0 copy-done.6
  13.4 0.0 copy-start.1
  13.4 1.0 %copy-done.1 = f32[3,3,24,384]{3,2,1,0:T(8,128)S(1)} copy-done((f32[3,3,24,384]{3,2,1,0:T(8,128)S(1)}, f32[3,3,24,384]{3,2,1,0:T(8,128)}, u32[]{:S(2)}) %copy-start.1) | copy-done | bytes 331800
  14.3 0.0 copy-start.3
  14.3 1.0 %copy-done.3 = f32[3,3,24,384]{3,2,1,0:T(8,128)S(1)} copy-done((f32[3,3,24,384]{3,2,1,0:T(8,128)S(1)}, f32[3,3,24,384]{3,2,1,0:T(8,128)}, u32[]{:S(2)}) %copy-start.3) | copy-done | bytes 331800
  15.3 0.0 copy-start.5
  15.3 1.0 %copy-done.5 = s32[3,3,24,384]{3,2,1,0:T(8,128)S(1)} copy-done((s32[3,3,24,384]{3,2,1,0:T(8,128)S(1)}, s32[3,3,24,384]{3,2,1,0:T(8,128)}, u32[]{:S(2)}) %copy-start.5) | copy-done | bytes 331800
  16.3 2.3 %prep.1 = (f32[6,27,8,128]{3,2,1,0:T(8,128)S(1)}, f32[3,27,8,128]{3,2,1,0:T(8,128)S(1)}, f32[216,8,128]{2,1,0:T(8,128)S(1)}, f32[27,8,128]{2,1,0:T(8,128)S(1)}) custom-call(f32[3,3,24,384]{3,2,1,0:T(8,128)S(1)} %copy-done.1, f32[3,3,24,384]{3,2,1,0:T(8,128)S(1)} %copy-done.3, s32[3,3,24,384]{3,2,1,0:T(8,128)S(1)} %copy-done.5, f32[27,8,128]{2,1,0:T(8,128)S(1)} %bitcast.14, ...), custom_call_target="tpu_custom_call" | custom-call | flops 4096000 | bytes 3981312 | tf_op jit(solution)/shard_map/prep/pallas_call | solution.py:737
  18.6 0.0 collective-permute-done.2.hc_ref
  18.6 0.0 collective-permute-done.1.hy_ref
  18.7 0.0 collective-permute-done.hx_ref
  18.7 12.2 %force.1 = (f32[232,128]{1,0:T(8,128)S(1)}, f32[232,128]{1,0:T(8,128)S(1)}, f32[2,27,8,128]{3,2,1,0:T(8,128)S(1)}, f32[2,16,128]{2,1,0:T(8,128)S(1)}, f32[216,8,128]{2,1,0:T(8,128)S(1)}) custom-call(f32[6,27,8,128]{3,2,1,0:T(8,128)S(1)} %get-tuple-element.41.u_ref, f32[9,24,384]{2,1,0:T(8,128)S(1)} %collective-permute-done.hx_ref, ...), custom_call_target="tpu_custom_call" | custom-call | flops 92160000 | bytes 4179968 | tf_op jit(solution)/shard_map/force/pallas_call | solution.py:737
  30.9 0.3 collective-permute-start.4
  31.1 1.5 %collective-permute-start.3 = (f32[232,128]{1,0:T(8,128)S(1)}, f32[232,128]{1,0:T(8,128)S(1)}, u32[]{:S(2)}, u32[]{:S(2)}) collective-permute-start(f32[232,128]{1,0:T(8,128)S(1)} %get-tuple-element.47.plus_ref), channel_id=1, source_target_pairs={{0,16},{1,17},{2,18},{3,19},{4,20},{5,21},{6,22},{7,23},{8,24},{9,... | collective-permute-start | bytes 356360 | tf_op jit(solution)/shard_map/ppermute | solution.py:764
  32.6 1.5 %energy.1 = (f32[27,8,128]{2,1,0:T(8,128)}, f32[8,128]{1,0:T(8,128)S(1)}, f32[27,8,128]{2,1,0:T(8,128)S(1)}, f32[4,16,128]{2,1,0:T(8,128)S(1)}) custom-call(f32[216,8,128]{2,1,0:T(8,128)S(1)} %get-tuple-element.50.power_ref, f32[27,8,128]{2,1,0:T(8,128)S(1)} %get-tuple-element.51.lump_ref, f32[27,8,128]{2,1,0:T(8,128)S(1)} %bitcast.15, ...), custom_call_target="tpu_custom_call" | custom-call | flops 2048000 | bytes 1751040 | tf_op jit(solution)/shard_map/energy/pallas_call | solution.py:737
  34.2 1.0 %collective-permute-done.4.got_high_ref.high_ref = f32[232,128]{1,0:T(8,128)S(1)} collective-permute-done((f32[232,128]{1,0:T(8,128)S(1)}, f32[232,128]{1,0:T(8,128)S(1)}, u32[]{:S(2)}, u32[]{:S(2)}) %collective-permute-start.4) | collective-permute-done | bytes 118816 | tf_op jit(solution)/shard_map/ppermute | solution.py:764
  35.1 0.0 collective-permute-done.3.got_low_ref.low_ref
  35.2 1.0 %collective-permute-start.5 = (f32[40,128]{1,0:T(8,128)S(1)}, f32[40,128]{1,0:T(8,128)S(1)}, u32[]{:S(2)}, u32[]{:S(2)}) collective-permute-start(f32[40,128]{1,0:T(8,128)S(1)} %get-tuple-element.53), channel_id=1, source_target_pairs={{0,1},{1,2},{2,3},{3,4},{4,5},{5,6},{6,7},{7,8},{8,9},{9,10},{10,1... | collective-permute-start | bytes 61448 | tf_op jit(solution)/shard_map/ppermute | solution.py:764
  36.2 3.9 %collective-permute-start.6 = (f32[40,128]{1,0:T(8,128)S(1)}, f32[40,128]{1,0:T(8,128)S(1)}, u32[]{:S(2)}, u32[]{:S(2)}) collective-permute-start(f32[40,128]{1,0:T(8,128)S(1)} %get-tuple-element.54), channel_id=1, source_target_pairs={{0,15},{1,0},{2,1},{3,2},{4,3},{5,4},{6,5},{7,6},{8,7},{9,8},{10,9... | collective-permute-start | bytes 61448 | tf_op jit(solution)/shard_map/ppermute | solution.py:764
  40.0 1.2 %collective-permute-done.5.from_down_ref = f32[40,128]{1,0:T(8,128)S(1)} collective-permute-done((f32[40,128]{1,0:T(8,128)S(1)}, f32[40,128]{1,0:T(8,128)S(1)}, u32[]{:S(2)}, u32[]{:S(2)}) %collective-permute-start.5) | collective-permute-done | bytes 20512 | tf_op jit(solution)/shard_map/ppermute | solution.py:764
  41.2 0.0 collective-permute-done.6.from_up_ref
  41.2 2.1 %apply.2 = (f32[3,27,8,128]{3,2,1,0:T(8,128)S(1)}, f32[232,128]{1,0:T(8,128)S(1)}, f32[232,128]{1,0:T(8,128)S(1)}, f32[2,27,8,128]{3,2,1,0:T(8,128)S(1)}, f32[2,16,128]{2,1,0:T(8,128)S(1)}) custom-call(f32[232,128]{1,0:T(8,128)S(1)} %get-tuple-element.46.minus_ref, f32[232,128]{1,0:T(8,128)S(1)} %get-tuple-element.47.plus_ref, ...), custom_call_target="tpu_custom_call" | custom-call | flops 13312000 | bytes 2920448 | tf_op jit(solution)/shard_map/apply/pallas_call | solution.py:737
  43.3 3.1 %collective-permute-start.8 = (f32[232,128]{1,0:T(8,128)S(1)}, f32[232,128]{1,0:T(8,128)S(1)}, u32[]{:S(2)}, u32[]{:S(2)}) collective-permute-start(f32[232,128]{1,0:T(8,128)S(1)} %get-tuple-element.58.minus_ref), channel_id=1, source_target_pairs={{0,112},{1,113},{2,114},{3,115},{4,116},{5,117},{6,118},{7,119},{8... | collective-permute-start | bytes 356360 | tf_op jit(solution)/shard_map/ppermute | solution.py:764
  46.5 0.0 collective-permute-start.7
  46.5 2.3 %collective-permute-done.8.got_high_ref.high_ref = f32[232,128]{1,0:T(8,128)S(1)} collective-permute-done((f32[232,128]{1,0:T(8,128)S(1)}, f32[232,128]{1,0:T(8,128)S(1)}, u32[]{:S(2)}, u32[]{:S(2)}) %collective-permute-start.8) | collective-permute-done | bytes 118816 | tf_op jit(solution)/shard_map/ppermute | solution.py:764
  48.8 0.0 collective-permute-done.7.got_low_ref.low_ref
  48.8 0.1 collective-permute-start.9
  48.9 5.1 %collective-permute-start.10 = (f32[40,128]{1,0:T(8,128)S(1)}, f32[40,128]{1,0:T(8,128)S(1)}, u32[]{:S(2)}, u32[]{:S(2)}) collective-permute-start(f32[40,128]{1,0:T(8,128)S(1)} %get-tuple-element.63), channel_id=1, source_target_pairs={{0,15},{1,0},{2,1},{3,2},{4,3},{5,4},{6,5},{7,6},{8,7},{9,8},{10,9... | collective-permute-start | bytes 61448 | tf_op jit(solution)/shard_map/ppermute | solution.py:764
  54.0 1.1 %collective-permute-done.9.from_down_ref = f32[40,128]{1,0:T(8,128)S(1)} collective-permute-done((f32[40,128]{1,0:T(8,128)S(1)}, f32[40,128]{1,0:T(8,128)S(1)}, u32[]{:S(2)}, u32[]{:S(2)}) %collective-permute-start.9) | collective-permute-done | bytes 20512 | tf_op jit(solution)/shard_map/ppermute | solution.py:764
  55.1 0.0 collective-permute-done.10.from_up_ref
  55.1 2.1 %apply.3 = (f32[3,27,8,128]{3,2,1,0:T(8,128)S(1)}, f32[232,128]{1,0:T(8,128)S(1)}, f32[232,128]{1,0:T(8,128)S(1)}, f32[2,27,8,128]{3,2,1,0:T(8,128)S(1)}, f32[2,16,128]{2,1,0:T(8,128)S(1)}) custom-call(f32[232,128]{1,0:T(8,128)S(1)} %get-tuple-element.58.minus_ref, f32[232,128]{1,0:T(8,128)S(1)} %get-tuple-element.59.plus_ref, ...), custom_call_target="tpu_custom_call" | custom-call | flops 13312000 | bytes 2920448 | tf_op jit(solution)/shard_map/apply/pallas_call | solution.py:737
  57.2 4.1 %collective-permute-start.12 = (f32[232,128]{1,0:T(8,128)S(1)}, f32[232,128]{1,0:T(8,128)S(1)}, u32[]{:S(2)}, u32[]{:S(2)}) collective-permute-start(f32[232,128]{1,0:T(8,128)S(1)} %get-tuple-element.64.minus_ref), channel_id=1, source_target_pairs={{0,112},{1,113},{2,114},{3,115},{4,116},{5,117},{6,118},{7,119},{8... | collective-permute-start | bytes 356360 | tf_op jit(solution)/shard_map/ppermute | solution.py:764
  61.3 0.0 collective-permute-start.11
  61.3 1.3 %collective-permute-done.12.got_high_ref.high_ref = f32[232,128]{1,0:T(8,128)S(1)} collective-permute-done((f32[232,128]{1,0:T(8,128)S(1)}, f32[232,128]{1,0:T(8,128)S(1)}, u32[]{:S(2)}, u32[]{:S(2)}) %collective-permute-start.12) | collective-permute-done | bytes 118816 | tf_op jit(solution)/shard_map/ppermute | solution.py:764
  62.6 0.5 collective-permute-done.11.got_low_ref.low_ref
  63.2 0.1 collective-permute-start.13
  63.3 5.2 %collective-permute-start.14 = (f32[40,128]{1,0:T(8,128)S(1)}, f32[40,128]{1,0:T(8,128)S(1)}, u32[]{:S(2)}, u32[]{:S(2)}) collective-permute-start(f32[40,128]{1,0:T(8,128)S(1)} %get-tuple-element.69), channel_id=1, source_target_pairs={{0,15},{1,0},{2,1},{3,2},{4,3},{5,4},{6,5},{7,6},{8,7},{9,8},{10,9... | collective-permute-start | bytes 61448 | tf_op jit(solution)/shard_map/ppermute | solution.py:764
  68.5 1.1 %collective-permute-done.13.from_down_ref = f32[40,128]{1,0:T(8,128)S(1)} collective-permute-done((f32[40,128]{1,0:T(8,128)S(1)}, f32[40,128]{1,0:T(8,128)S(1)}, u32[]{:S(2)}, u32[]{:S(2)}) %collective-permute-start.13) | collective-permute-done | bytes 20512 | tf_op jit(solution)/shard_map/ppermute | solution.py:764
  69.6 0.0 collective-permute-done.14.from_up_ref
  69.6 0.0 copy-start.2
  69.6 0.0 copy-start.4
  69.6 1.6 %moments.1 = (f32[3,27,8,128]{3,2,1,0:T(8,128)S(1)}, f32[128,128]{1,0:T(8,128)S(1)}) custom-call(f32[232,128]{1,0:T(8,128)S(1)} %get-tuple-element.64.minus_ref, f32[232,128]{1,0:T(8,128)S(1)} %get-tuple-element.65.plus_ref, f32[2,27,8,128]{3,2,1,0:T(8,128)S(1)} %get-tuple-element.66.inner_ref, f32[2,16,128]{2,1,0:T(8,128)S(1)} %get-tuple-element.67.rim_ref, ...), custom_call_target="tpu_custom_call" | custom-call | flops 8192000 | bytes 3174400 | tf_op jit(solution)/shard_map/moments/pallas_call | solution.py:737
  71.2 20.2 %all_to_all.5 = f32[128,1,128]{2,1,0:T(1,128)S(1)} all-to-all(f32[128,1,128]{2,1,0:T(1,128)S(1)} %bitcast.17), channel_id=1, replica_groups=mesh['gx'=8,'gy'=16] {'gx','gy'}, dimensions={0} | all-to-all | bytes 131072 | tf_op jit(solution)/shard_map/all_to_all | solution.py:836
  91.4 0.0 copy-done.2
  91.4 0.0 copy-done.4
  91.4 1.8 %final.1 = (f32[3,3,24,384]{3,2,1,0:T(8,128)}, f32[3,3,24,384]{3,2,1,0:T(8,128)}, f32[3,3,24,384]{3,2,1,0:T(8,128)}) custom-call(f32[128,128]{1,0:T(8,128)S(1)} %bitcast.16, f32[3,27,8,128]{3,2,1,0:T(8,128)S(1)} %get-tuple-element.70.r_ref, f32[3,27,8,128]{3,2,1,0:T(8,128)S(1)} %get-tuple-element.71.v_ref, f32[3,27,8,128]{3,2,1,0:T(8,128)S(1)} %get-tuple-element.73.w_ref, ...), custom_call_target="tpu_custom_call" | custom-call | flops 1024000 | bytes 2719744 | tf_op jit(solution)/shard_map/final/pallas_call | solution.py:737
  (3 shorter events, 0.1 us)
Async XLA Ops:
  0.6 12.7 %copy-start = (f32[216,1,8,128]{3,2,1,0:T(8,128)S(1)}, f32[216,1,8,128]{3,2,1,0:T(8,128)}, u32[]{:S(2)}) copy-start(f32[216,1,8,128]{3,2,1,0:T(8,128)} %param.8) | copy-start | bytes 2654212
  0.6 12.7 %copy-start.6 = (f32[27,1,8,128]{3,2,1,0:T(8,128)S(1)}, f32[27,1,8,128]{3,2,1,0:T(8,128)}, u32[]{:S(2)}) copy-start(f32[27,1,8,128]{3,2,1,0:T(8,128)} %param.7) | copy-start | bytes 331780
  2.7 15.9 %collective-permute-start = (f32[9,24,384]{2,1,0:T(8,128)}, f32[9,24,384]{2,1,0:T(8,128)S(1)}, u32[]{:S(2)}, u32[]{:S(2)}) collective-permute-start(f32[9,24,384]{2,1,0:T(8,128)} %get-tuple-element.42), channel_id=1, source_target_pairs={{0,112},{1,113},{2,114},{3,115},{4,116},{5,117},{6,118},{7,119},{8... | collective-permute-start | bytes 995336 | tf_op jit(solution)/shard_map/ppermute | solution.py:764
  4.2 14.5 %collective-permute-start.1 = (f32[27,384]{1,0:T(8,128)}, f32[27,384]{1,0:T(8,128)S(1)}, u32[]{:S(2)}, u32[]{:S(2)}) collective-permute-start(f32[27,384]{1,0:T(8,128)} %get-tuple-element.43), channel_id=1, source_target_pairs={{0,15},{1,0},{2,1},{3,2},{4,3},{5,4},{6,5},{7,6},{8,7},{9,8},{10,9... | collective-permute-start | bytes 124424 | tf_op jit(solution)/shard_map/ppermute | solution.py:764
  9.2 9.5 %collective-permute-start.2 = (f32[9,384]{1,0:T(8,128)}, f32[9,384]{1,0:T(8,128)S(1)}, u32[]{:S(2)}, u32[]{:S(2)}) collective-permute-start(f32[9,384]{1,0:T(8,128)} %get-tuple-element.44), channel_id=1, source_target_pairs={{0,127},{1,112},{2,113},{3,114},{4,115},{5,116},{6,117},{7,118},{8... | collective-permute-start | bytes 41480 | tf_op jit(solution)/shard_map/ppermute | solution.py:764
  13.4 1.0 %copy-start.1 = (f32[3,3,24,384]{3,2,1,0:T(8,128)S(1)}, f32[3,3,24,384]{3,2,1,0:T(8,128)}, u32[]{:S(2)}) copy-start(f32[3,3,24,384]{3,2,1,0:T(8,128)} %d_ref.5) | copy-start | bytes 995332
  14.3 1.0 %copy-start.3 = (f32[3,3,24,384]{3,2,1,0:T(8,128)S(1)}, f32[3,3,24,384]{3,2,1,0:T(8,128)}, u32[]{:S(2)}) copy-start(f32[3,3,24,384]{3,2,1,0:T(8,128)} %vel_ref.1) | copy-start | bytes 995332
  15.3 1.0 %copy-start.5 = (s32[3,3,24,384]{3,2,1,0:T(8,128)S(1)}, s32[3,3,24,384]{3,2,1,0:T(8,128)}, u32[]{:S(2)}) copy-start(s32[3,3,24,384]{3,2,1,0:T(8,128)} %f_ref.3) | copy-start | bytes 995332
  30.9 4.3 %collective-permute-start.4 = (f32[232,128]{1,0:T(8,128)S(1)}, f32[232,128]{1,0:T(8,128)S(1)}, u32[]{:S(2)}, u32[]{:S(2)}) collective-permute-start(f32[232,128]{1,0:T(8,128)S(1)} %get-tuple-element.46.minus_ref), channel_id=1, source_target_pairs={{0,112},{1,113},{2,114},{3,115},{4,116},{5,117},{6,118},{7,119},{8... | collective-permute-start | bytes 356360 | tf_op jit(solution)/shard_map/ppermute | solution.py:764
  31.1 4.0 %collective-permute-start.3 = (f32[232,128]{1,0:T(8,128)S(1)}, f32[232,128]{1,0:T(8,128)S(1)}, u32[]{:S(2)}, u32[]{:S(2)}) collective-permute-start(f32[232,128]{1,0:T(8,128)S(1)} %get-tuple-element.47.plus_ref), channel_id=1, source_target_pairs={{0,16},{1,17},{2,18},{3,19},{4,20},{5,21},{6,22},{7,23},{8,24},{9,... | collective-permute-start | bytes 356360 | tf_op jit(solution)/shard_map/ppermute | solution.py:764
  35.2 6.0 %collective-permute-start.5 = (f32[40,128]{1,0:T(8,128)S(1)}, f32[40,128]{1,0:T(8,128)S(1)}, u32[]{:S(2)}, u32[]{:S(2)}) collective-permute-start(f32[40,128]{1,0:T(8,128)S(1)} %get-tuple-element.53), channel_id=1, source_target_pairs={{0,1},{1,2},{2,3},{3,4},{4,5},{5,6},{6,7},{7,8},{8,9},{9,10},{10,1... | collective-permute-start | bytes 61448 | tf_op jit(solution)/shard_map/ppermute | solution.py:764
  36.2 5.0 %collective-permute-start.6 = (f32[40,128]{1,0:T(8,128)S(1)}, f32[40,128]{1,0:T(8,128)S(1)}, u32[]{:S(2)}, u32[]{:S(2)}) collective-permute-start(f32[40,128]{1,0:T(8,128)S(1)} %get-tuple-element.54), channel_id=1, source_target_pairs={{0,15},{1,0},{2,1},{3,2},{4,3},{5,4},{6,5},{7,6},{8,7},{9,8},{10,9... | collective-permute-start | bytes 61448 | tf_op jit(solution)/shard_map/ppermute | solution.py:764
  43.3 5.4 %collective-permute-start.8 = (f32[232,128]{1,0:T(8,128)S(1)}, f32[232,128]{1,0:T(8,128)S(1)}, u32[]{:S(2)}, u32[]{:S(2)}) collective-permute-start(f32[232,128]{1,0:T(8,128)S(1)} %get-tuple-element.58.minus_ref), channel_id=1, source_target_pairs={{0,112},{1,113},{2,114},{3,115},{4,116},{5,117},{6,118},{7,119},{8... | collective-permute-start | bytes 356360 | tf_op jit(solution)/shard_map/ppermute | solution.py:764
  46.5 2.3 %collective-permute-start.7 = (f32[232,128]{1,0:T(8,128)S(1)}, f32[232,128]{1,0:T(8,128)S(1)}, u32[]{:S(2)}, u32[]{:S(2)}) collective-permute-start(f32[232,128]{1,0:T(8,128)S(1)} %get-tuple-element.59.plus_ref), channel_id=1, source_target_pairs={{0,16},{1,17},{2,18},{3,19},{4,20},{5,21},{6,22},{7,23},{8,24},{9,... | collective-permute-start | bytes 356360 | tf_op jit(solution)/shard_map/ppermute | solution.py:764
  48.8 6.3 %collective-permute-start.9 = (f32[40,128]{1,0:T(8,128)S(1)}, f32[40,128]{1,0:T(8,128)S(1)}, u32[]{:S(2)}, u32[]{:S(2)}) collective-permute-start(f32[40,128]{1,0:T(8,128)S(1)} %get-tuple-element.62), channel_id=1, source_target_pairs={{0,1},{1,2},{2,3},{3,4},{4,5},{5,6},{6,7},{7,8},{8,9},{9,10},{10,1... | collective-permute-start | bytes 61448 | tf_op jit(solution)/shard_map/ppermute | solution.py:764
  48.9 6.2 %collective-permute-start.10 = (f32[40,128]{1,0:T(8,128)S(1)}, f32[40,128]{1,0:T(8,128)S(1)}, u32[]{:S(2)}, u32[]{:S(2)}) collective-permute-start(f32[40,128]{1,0:T(8,128)S(1)} %get-tuple-element.63), channel_id=1, source_target_pairs={{0,15},{1,0},{2,1},{3,2},{4,3},{5,4},{6,5},{7,6},{8,7},{9,8},{10,9... | collective-permute-start | bytes 61448 | tf_op jit(solution)/shard_map/ppermute | solution.py:764
  57.2 5.4 %collective-permute-start.12 = (f32[232,128]{1,0:T(8,128)S(1)}, f32[232,128]{1,0:T(8,128)S(1)}, u32[]{:S(2)}, u32[]{:S(2)}) collective-permute-start(f32[232,128]{1,0:T(8,128)S(1)} %get-tuple-element.64.minus_ref), channel_id=1, source_target_pairs={{0,112},{1,113},{2,114},{3,115},{4,116},{5,117},{6,118},{7,119},{8... | collective-permute-start | bytes 356360 | tf_op jit(solution)/shard_map/ppermute | solution.py:764
  61.3 1.8 %collective-permute-start.11 = (f32[232,128]{1,0:T(8,128)S(1)}, f32[232,128]{1,0:T(8,128)S(1)}, u32[]{:S(2)}, u32[]{:S(2)}) collective-permute-start(f32[232,128]{1,0:T(8,128)S(1)} %get-tuple-element.65.plus_ref), channel_id=1, source_target_pairs={{0,16},{1,17},{2,18},{3,19},{4,20},{5,21},{6,22},{7,23},{8,24},{9,... | collective-permute-start | bytes 356360 | tf_op jit(solution)/shard_map/ppermute | solution.py:764
  63.2 6.4 %collective-permute-start.13 = (f32[40,128]{1,0:T(8,128)S(1)}, f32[40,128]{1,0:T(8,128)S(1)}, u32[]{:S(2)}, u32[]{:S(2)}) collective-permute-start(f32[40,128]{1,0:T(8,128)S(1)} %get-tuple-element.68), channel_id=1, source_target_pairs={{0,1},{1,2},{2,3},{3,4},{4,5},{5,6},{6,7},{7,8},{8,9},{9,10},{10,1... | collective-permute-start | bytes 61448 | tf_op jit(solution)/shard_map/ppermute | solution.py:764
  63.3 6.3 %collective-permute-start.14 = (f32[40,128]{1,0:T(8,128)S(1)}, f32[40,128]{1,0:T(8,128)S(1)}, u32[]{:S(2)}, u32[]{:S(2)}) collective-permute-start(f32[40,128]{1,0:T(8,128)S(1)} %get-tuple-element.69), channel_id=1, source_target_pairs={{0,15},{1,0},{2,1},{3,2},{4,3},{5,4},{6,5},{7,6},{8,7},{9,8},{10,9... | collective-permute-start | bytes 61448 | tf_op jit(solution)/shard_map/ppermute | solution.py:764
  69.6 21.8 %copy-start.2 = (f32[3,3,24,384]{3,2,1,0:T(8,128)S(1)}, f32[3,3,24,384]{3,2,1,0:T(8,128)}, u32[]{:S(2)}) copy-start(f32[3,3,24,384]{3,2,1,0:T(8,128)} %d_ref.5) | copy-start | bytes 995332
  69.6 21.8 %copy-start.4 = (f32[3,3,24,384]{3,2,1,0:T(8,128)S(1)}, f32[3,3,24,384]{3,2,1,0:T(8,128)}, u32[]{:S(2)}) copy-start(f32[3,3,24,384]{3,2,1,0:T(8,128)} %vel_ref.1) | copy-start | bytes 995332

commit v6 on v5

--- a/solution.py
+++ b/solution.py
@@ -212,18 +212,15 @@
     return [place[g, pl.ds(b, 8, stride=3), :] for b in range(3) for g in range(3)]
 
 
-def prep_kernel(d_ref, v_ref, f_ref, e_ref, w_ref, u_ref, m_ref, eq_ref, lump_ref, place, ez_s, ey_s):
+def prep_kernel(d_ref, v_ref, e_ref, u_ref, eq_ref, place, ez_s, ey_s):
     def body(c, _):
         for x in range(3):
-            for k, ref in enumerate((d_ref, v_ref, f_ref)):
+            for k, ref in enumerate((d_ref, v_ref)):
                 tiles = element_rows(
-                    lambda s, l: ref[c, x, s : s + 8, l : l + 128].astype(F32), place.at[3 * x + k]
+                    lambda s, l: ref[c, x, s : s + 8, l : l + 128], place.at[2 * x + k]
                 )
                 for n in range(9):
-                    if k < 2:
-                        u_ref[3 * k + c, x * 9 + n] = tiles[n]
-                    else:
-                        m_ref[x, c * 9 + n] = 1.0 - tiles[n]
+                    u_ref[3 * k + c, x * 9 + n] = tiles[n]
         return 0
 
     lax.fori_loop(0, 3, body, 0)
@@ -241,7 +238,6 @@
         return 0
 
     lax.fori_loop(0, 6, plane, 0)
-    project(w_ref, ez_s, ey_s, lump_ref)
 
 
 def project(at_ref, z_s, x_s, out_ref):
@@ -261,10 +257,23 @@
 
 
 def energy_kernel(
-    power_ref, lump_ref, e_ref, hx_ref, hy_ref, hc_ref,
-    out_ref, token_ref, face_mask_ref, rim_mask_ref, sum_s, z_s, x_s, hy_s, place,
+    power_ref, w_ref, e_ref, f_ref, hx_ref, hy_ref, hc_ref,
+    out_ref, token_ref, mask_ref, face_mask_ref, rim_mask_ref,
+    lump_ref, sum_s, z_s, x_s, hy_s, place,
 ):
     masks(hx_ref, hy_ref, hc_ref, face_mask_ref, rim_mask_ref, hy_s, place)
+
+    def own(c, _):
+        for x in range(3):
+            tiles = element_rows(
+                lambda s, l: f_ref[c, x, s : s + 8, l : l + 128].astype(F32), place.at[x]
+            )
+            for n in range(9):
+                mask_ref[x, c * 9 + n] = 1.0 - tiles[n]
+        return 0
+
+    lax.fori_loop(0, 3, own, 0)
+    project(w_ref, z_s, x_s, lump_ref)
     project(power_ref, z_s, x_s, sum_s)
 
     def body(n, _):
@@ -794,13 +803,13 @@
         hx = moved(face, -1, 0)
         hy = moved(row, 0, -1)
         hc = moved(corner, -1, -1)
-        nodes, mask, heat, lump = call(
+        nodes, heat = call(
             prep_kernel,
-            [(6, 27) + T, (3, 27) + T, (216,) + T, (27,) + T],
-            [(9, 3, 24, 128), (6, 9) + T, (6, 3) + T],
+            [(6, 27) + T, (216,) + T],
+            [(6, 3, 24, 128), (6, 9) + T, (6, 3) + T],
             "prep",
             flops=4000 * 1024,
-        )(displacement, velocity, pinned, dofs, weight)
+        )(displacement, velocity, dofs)
         out = call(
             force_kernel,
             PARTS + [(216,) + T],
@@ -813,13 +822,13 @@
             flops=90000 * 1024,
         )(nodes, hx, hy, hc, heat, weight)
         parts, power = out[:4], out[4]
-        energy_new, token, face_mask, rim_mask = call(
+        energy_new, token, mask, face_mask, rim_mask = call(
             energy_kernel,
-            [(27,) + T, T, (27,) + T, (4, 16, 128)],
-            [(27,) + T, (6, 9) + T, (6, 3) + T, (3, 40, 128), (3, 3, 24, 128)],
+            [(27,) + T, T, (3, 27) + T, (27,) + T, (4, 16, 128)],
+            [(27,) + T, (27,) + T, (6, 9) + T, (6, 3) + T, (3, 40, 128), (3, 3, 24, 128)],
             "energy",
             flops=2000 * 1024,
-        )(power, lump, dofs, hx, hy, hc)
+        )(power, weight, dofs, pinned, hx, hy, hc)
         free = (mask, face_mask, rim_mask)
         scratch = [
             (3, 48) + T, (6, 3, 16) + T, (3, 4, 6) + T, (6, 3, 16) + T, (3, 48) + T,

time: 93.4 us -> 92.8 us (level)
  starting transfers between devices: 34.9 us -> 38.1 us
  local copies, waits for them, and re-layouts: 2.94 us -> 0.02 us
  waiting for transfers between devices: 8.49 us -> 7.54 us
    ppermute x15, starting transfers between devices: 34.9 us -> 38.1 us  [moved(): return lax.ppermute(value, ('gx', 'gy'), pairs)]
    unnamed x14 -> x10, local copies, waits for them, and re-layouts: 2.94 us -> 0.02 us
    ppermute x15, waiting for transfers between devices: 8.49 us -> 7.54 us  [moved(): return lax.ppermute(value, ('gx', 'gy'), pairs)]
  transfers between devices with their start and end apart: 15 -> 15, of which waited for: 7 -> 8; matrix products, arithmetic and copies ran while one was open for 0% -> 0% of each run, Pallas kernels for 4% -> 4%
where the time goes in v6:
time: 92.8 us; the launch traced here: 92.7 us
  starting transfers between devices  38.1 us (41%)
  Pallas kernels  26 us (28%)
  blocking collectives  20.2 us (22%)
  waiting for transfers between devices  7.54 us (8%)
    ppermute x15, starting transfers between devices, moved(): return lax.ppermute(value, ('gx', 'gy'), pairs)  38.1 us
    pallas_call x11, Pallas kernels, run(): pl.pallas_call(kernel, out_shape=[jax.ShapeDtypeStruct(s, F32) for s in o...  26 us
    all_to_all x1, blocking collectives, on_device(): sums = lax.all_to_all(sums, ('gx', 'gy'), 0, 0).reshape(-1, 128)  20.2 us
    ppermute x15, waiting for transfers between devices, moved(): return lax.ppermute(value, ('gx', 'gy'), pairs)  7.54 us
  transfers between devices with their start and end apart: 15, of which 8 were waited for; matrix products, arithmetic and copies ran while one was open for 0% of the time, Pallas kernels for 4%

profile of v6, /device:TPU:1, one launch (start us, length us, event | category | flops | bytes accessed | tf_op | source)
XLA Modules:
  0.0 92.7 jit_solution(15485700503633008051)
XLA Ops:
  0.6 0.0 copy-start.2
  0.6 0.0 copy-start.1
  0.7 0.0 copy-start.4
  0.7 0.0 copy-start
  0.7 2.1 %pack.1 = (f32[9,24,384]{2,1,0:T(8,128)}, f32[27,384]{1,0:T(8,128)}, f32[9,384]{1,0:T(8,128)}) custom-call(f32[3,3,24,384]{3,2,1,0:T(8,128)} %d_ref.5, f32[3,3,24,384]{3,2,1,0:T(8,128)} %vel_ref.1, s32[3,3,24,384]{3,2,1,0:T(8,128)} %f_ref.3), custom_call_target="tpu_custom_call" | custom-call | bytes 1382400 | tf_op jit(solution)/shard_map/pack/pallas_call | solution.py:746
  2.8 1.4 %collective-permute-start = (f32[9,24,384]{2,1,0:T(8,128)}, f32[9,24,384]{2,1,0:T(8,128)S(1)}, u32[]{:S(2)}, u32[]{:S(2)}) collective-permute-start(f32[9,24,384]{2,1,0:T(8,128)} %get-tuple-element.41), channel_id=1, source_target_pairs={{0,112},{1,113},{2,114},{3,115},{4,116},{5,117},{6,118},{7,119},{8... | collective-permute-start | bytes 995336 | tf_op jit(solution)/shard_map/ppermute | solution.py:773
  4.2 5.0 %collective-permute-start.1 = (f32[27,384]{1,0:T(8,128)}, f32[27,384]{1,0:T(8,128)S(1)}, u32[]{:S(2)}, u32[]{:S(2)}) collective-permute-start(f32[27,384]{1,0:T(8,128)} %get-tuple-element.42), channel_id=1, source_target_pairs={{0,15},{1,0},{2,1},{3,2},{4,3},{5,4},{6,5},{7,6},{8,7},{9,8},{10,9... | collective-permute-start | bytes 124424 | tf_op jit(solution)/shard_map/ppermute | solution.py:773
  9.2 4.2 %collective-permute-start.2 = (f32[9,384]{1,0:T(8,128)}, f32[9,384]{1,0:T(8,128)S(1)}, u32[]{:S(2)}, u32[]{:S(2)}) collective-permute-start(f32[9,384]{1,0:T(8,128)} %get-tuple-element.43), channel_id=1, source_target_pairs={{0,127},{1,112},{2,113},{3,114},{4,115},{5,116},{6,117},{7,118},{8... | collective-permute-start | bytes 41480 | tf_op jit(solution)/shard_map/ppermute | solution.py:773
  13.4 0.0 copy-done.2
  13.4 0.0 copy-done.1
  13.4 0.0 copy-done.4
  13.4 1.5 %prep.1 = (f32[6,27,8,128]{3,2,1,0:T(8,128)S(1)}, f32[216,8,128]{2,1,0:T(8,128)S(1)}) custom-call(f32[3,3,24,384]{3,2,1,0:T(8,128)S(1)} %copy-done.1, f32[3,3,24,384]{3,2,1,0:T(8,128)S(1)} %copy-done.2, f32[27,8,128]{2,1,0:T(8,128)S(1)} %bitcast.14), custom_call_target="tpu_custom_call" | custom-call | flops 4096000 | bytes 2322432 | tf_op jit(solution)/shard_map/prep/pallas_call | solution.py:746
  15.0 0.0 collective-permute-done.2.hc_ref
  15.0 0.0 collective-permute-done.1.hy_ref
  15.0 0.0 collective-permute-done.hx_ref
  15.0 0.0 copy-done
  15.0 0.0 copy-start.3
  15.0 12.2 %force.1 = (f32[232,128]{1,0:T(8,128)S(1)}, f32[232,128]{1,0:T(8,128)S(1)}, f32[2,27,8,128]{3,2,1,0:T(8,128)S(1)}, f32[2,16,128]{2,1,0:T(8,128)S(1)}, f32[216,8,128]{2,1,0:T(8,128)S(1)}) custom-call(f32[6,27,8,128]{3,2,1,0:T(8,128)S(1)} %get-tuple-element.40.u_ref, f32[9,24,384]{2,1,0:T(8,128)S(1)} %collective-permute-done.hx_ref, ...), custom_call_target="tpu_custom_call" | custom-call | flops 92160000 | bytes 4179968 | tf_op jit(solution)/shard_map/force/pallas_call | solution.py:746
  27.2 1.5 %collective-permute-start.4 = (f32[232,128]{1,0:T(8,128)S(1)}, f32[232,128]{1,0:T(8,128)S(1)}, u32[]{:S(2)}, u32[]{:S(2)}) collective-permute-start(f32[232,128]{1,0:T(8,128)S(1)} %get-tuple-element.45.minus_ref), channel_id=1, source_target_pairs={{0,112},{1,113},{2,114},{3,115},{4,116},{5,117},{6,118},{7,119},{8... | collective-permute-start | bytes 356360 | tf_op jit(solution)/shard_map/ppermute | solution.py:773
  28.7 0.3 collective-permute-start.3
  29.0 0.0 copy-done.3
  29.0 2.5 %energy.1 = (f32[27,8,128]{2,1,0:T(8,128)}, f32[8,128]{1,0:T(8,128)S(1)}, f32[3,27,8,128]{3,2,1,0:T(8,128)S(1)}, f32[27,8,128]{2,1,0:T(8,128)S(1)}, f32[4,16,128]{2,1,0:T(8,128)S(1)}) custom-call(f32[216,8,128]{2,1,0:T(8,128)S(1)} %get-tuple-element.49.power_ref, f32[216,8,128]{2,1,0:T(8,128)S(1)} %bitcast.10, f32[27,8,128]{2,1,0:T(8,128)S(1)} %bitcast.15, ...), custom_call_target="tpu_custom_call" | custom-call | flops 2048000 | bytes 3188736 | tf_op jit(solution)/shard_map/energy/pallas_call | solution.py:746
  31.5 0.0 collective-permute-done.4.got_high_ref.high_ref
  31.5 0.5 collective-permute-done.3.got_low_ref.low_ref
  32.1 0.5 collective-permute-start.5
  32.5 4.4 %collective-permute-start.6 = (f32[40,128]{1,0:T(8,128)S(1)}, f32[40,128]{1,0:T(8,128)S(1)}, u32[]{:S(2)}, u32[]{:S(2)}) collective-permute-start(f32[40,128]{1,0:T(8,128)S(1)} %get-tuple-element.52), channel_id=1, source_target_pairs={{0,15},{1,0},{2,1},{3,2},{4,3},{5,4},{6,5},{7,6},{8,7},{9,8},{10,9... | collective-permute-start | bytes 61448 | tf_op jit(solution)/shard_map/ppermute | solution.py:773
  36.9 1.2 %collective-permute-done.5.from_down_ref = f32[40,128]{1,0:T(8,128)S(1)} collective-permute-done((f32[40,128]{1,0:T(8,128)S(1)}, f32[40,128]{1,0:T(8,128)S(1)}, u32[]{:S(2)}, u32[]{:S(2)}) %collective-permute-start.5) | collective-permute-done | bytes 20512 | tf_op jit(solution)/shard_map/ppermute | solution.py:773
  38.1 0.0 collective-permute-done.6.from_up_ref
  38.1 2.1 %apply.2 = (f32[3,27,8,128]{3,2,1,0:T(8,128)S(1)}, f32[232,128]{1,0:T(8,128)S(1)}, f32[232,128]{1,0:T(8,128)S(1)}, f32[2,27,8,128]{3,2,1,0:T(8,128)S(1)}, f32[2,16,128]{2,1,0:T(8,128)S(1)}) custom-call(f32[232,128]{1,0:T(8,128)S(1)} %get-tuple-element.45.minus_ref, f32[232,128]{1,0:T(8,128)S(1)} %get-tuple-element.46.plus_ref, ...), custom_call_target="tpu_custom_call" | custom-call | flops 13312000 | bytes 2920448 | tf_op jit(solution)/shard_map/apply/pallas_call | solution.py:746
  40.2 5.8 %collective-permute-start.8 = (f32[232,128]{1,0:T(8,128)S(1)}, f32[232,128]{1,0:T(8,128)S(1)}, u32[]{:S(2)}, u32[]{:S(2)}) collective-permute-start(f32[232,128]{1,0:T(8,128)S(1)} %get-tuple-element.56.minus_ref), channel_id=1, source_target_pairs={{0,112},{1,113},{2,114},{3,115},{4,116},{5,117},{6,118},{7,119},{8... | collective-permute-start | bytes 356360 | tf_op jit(solution)/shard_map/ppermute | solution.py:773
  46.0 0.0 collective-permute-start.7
  46.0 1.0 %collective-permute-done.8.got_high_ref.high_ref = f32[232,128]{1,0:T(8,128)S(1)} collective-permute-done((f32[232,128]{1,0:T(8,128)S(1)}, f32[232,128]{1,0:T(8,128)S(1)}, u32[]{:S(2)}, u32[]{:S(2)}) %collective-permute-start.8) | collective-permute-done | bytes 118816 | tf_op jit(solution)/shard_map/ppermute | solution.py:773
  47.0 0.9 collective-permute-done.7.got_low_ref.low_ref
  47.9 0.1 collective-permute-start.9
  48.0 5.1 %collective-permute-start.10 = (f32[40,128]{1,0:T(8,128)S(1)}, f32[40,128]{1,0:T(8,128)S(1)}, u32[]{:S(2)}, u32[]{:S(2)}) collective-permute-start(f32[40,128]{1,0:T(8,128)S(1)} %get-tuple-element.61), channel_id=1, source_target_pairs={{0,15},{1,0},{2,1},{3,2},{4,3},{5,4},{6,5},{7,6},{8,7},{9,8},{10,9... | collective-permute-start | bytes 61448 | tf_op jit(solution)/shard_map/ppermute | solution.py:773
  53.1 1.1 %collective-permute-done.9.from_down_ref = f32[40,128]{1,0:T(8,128)S(1)} collective-permute-done((f32[40,128]{1,0:T(8,128)S(1)}, f32[40,128]{1,0:T(8,128)S(1)}, u32[]{:S(2)}, u32[]{:S(2)}) %collective-permute-start.9) | collective-permute-done | bytes 20512 | tf_op jit(solution)/shard_map/ppermute | solution.py:773
  54.2 0.0 collective-permute-done.10.from_up_ref
  54.2 2.1 %apply.3 = (f32[3,27,8,128]{3,2,1,0:T(8,128)S(1)}, f32[232,128]{1,0:T(8,128)S(1)}, f32[232,128]{1,0:T(8,128)S(1)}, f32[2,27,8,128]{3,2,1,0:T(8,128)S(1)}, f32[2,16,128]{2,1,0:T(8,128)S(1)}) custom-call(f32[232,128]{1,0:T(8,128)S(1)} %get-tuple-element.56.minus_ref, f32[232,128]{1,0:T(8,128)S(1)} %get-tuple-element.57.plus_ref, ...), custom_call_target="tpu_custom_call" | custom-call | flops 13312000 | bytes 2920448 | tf_op jit(solution)/shard_map/apply/pallas_call | solution.py:746
  56.3 4.5 %collective-permute-start.12 = (f32[232,128]{1,0:T(8,128)S(1)}, f32[232,128]{1,0:T(8,128)S(1)}, u32[]{:S(2)}, u32[]{:S(2)}) collective-permute-start(f32[232,128]{1,0:T(8,128)S(1)} %get-tuple-element.62.minus_ref), channel_id=1, source_target_pairs={{0,112},{1,113},{2,114},{3,115},{4,116},{5,117},{6,118},{7,119},{8... | collective-permute-start | bytes 356360 | tf_op jit(solution)/shard_map/ppermute | solution.py:773
  60.9 0.0 collective-permute-start.11
  60.9 1.3 %collective-permute-done.12.got_high_ref.high_ref = f32[232,128]{1,0:T(8,128)S(1)} collective-permute-done((f32[232,128]{1,0:T(8,128)S(1)}, f32[232,128]{1,0:T(8,128)S(1)}, u32[]{:S(2)}, u32[]{:S(2)}) %collective-permute-start.12) | collective-permute-done | bytes 118816 | tf_op jit(solution)/shard_map/ppermute | solution.py:773
  62.2 0.5 collective-permute-done.11.got_low_ref.low_ref
  62.8 0.1 collective-permute-start.13
  62.8 5.2 %collective-permute-start.14 = (f32[40,128]{1,0:T(8,128)S(1)}, f32[40,128]{1,0:T(8,128)S(1)}, u32[]{:S(2)}, u32[]{:S(2)}) collective-permute-start(f32[40,128]{1,0:T(8,128)S(1)} %get-tuple-element.67), channel_id=1, source_target_pairs={{0,15},{1,0},{2,1},{3,2},{4,3},{5,4},{6,5},{7,6},{8,7},{9,8},{10,9... | collective-permute-start | bytes 61448 | tf_op jit(solution)/shard_map/ppermute | solution.py:773
  68.0 1.1 %collective-permute-done.13.from_down_ref = f32[40,128]{1,0:T(8,128)S(1)} collective-permute-done((f32[40,128]{1,0:T(8,128)S(1)}, f32[40,128]{1,0:T(8,128)S(1)}, u32[]{:S(2)}, u32[]{:S(2)}) %collective-permute-start.13) | collective-permute-done | bytes 20512 | tf_op jit(solution)/shard_map/ppermute | solution.py:773
  69.1 0.0 collective-permute-done.14.from_up_ref
  69.1 1.6 %moments.1 = (f32[3,27,8,128]{3,2,1,0:T(8,128)S(1)}, f32[128,128]{1,0:T(8,128)S(1)}) custom-call(f32[232,128]{1,0:T(8,128)S(1)} %get-tuple-element.62.minus_ref, f32[232,128]{1,0:T(8,128)S(1)} %get-tuple-element.63.plus_ref, f32[2,27,8,128]{3,2,1,0:T(8,128)S(1)} %get-tuple-element.64.inner_ref, f32[2,16,128]{2,1,0:T(8,128)S(1)} %get-tuple-element.65.rim_ref, ...), custom_call_target="tpu_custom_call" | custom-call | flops 8192000 | bytes 3174400 | tf_op jit(solution)/shard_map/moments/pallas_call | solution.py:746
  70.7 20.2 %all_to_all.5 = f32[128,1,128]{2,1,0:T(1,128)S(1)} all-to-all(f32[128,1,128]{2,1,0:T(1,128)S(1)} %bitcast.17), channel_id=1, replica_groups=mesh['gx'=8,'gy'=16] {'gx','gy'}, dimensions={0} | all-to-all | bytes 131072 | tf_op jit(solution)/shard_map/all_to_all | solution.py:845
  90.9 1.8 %final.1 = (f32[3,3,24,384]{3,2,1,0:T(8,128)}, f32[3,3,24,384]{3,2,1,0:T(8,128)}, f32[3,3,24,384]{3,2,1,0:T(8,128)}) custom-call(f32[128,128]{1,0:T(8,128)S(1)} %bitcast.16, f32[3,27,8,128]{3,2,1,0:T(8,128)S(1)} %get-tuple-element.68.r_ref, f32[3,27,8,128]{3,2,1,0:T(8,128)S(1)} %get-tuple-element.69.v_ref, f32[3,27,8,128]{3,2,1,0:T(8,128)S(1)} %get-tuple-element.71.w_ref, ...), custom_call_target="tpu_custom_call" | custom-call | flops 1024000 | bytes 2719744 | tf_op jit(solution)/shard_map/final/pallas_call | solution.py:746
  (3 shorter events, 0.1 us)
Async XLA Ops:
  0.6 12.8 %copy-start.2 = (f32[3,3,24,384]{3,2,1,0:T(8,128)S(1)}, f32[3,3,24,384]{3,2,1,0:T(8,128)}, u32[]{:S(2)}) copy-start(f32[3,3,24,384]{3,2,1,0:T(8,128)} %vel_ref.1) | copy-start | bytes 995332
  0.6 12.8 %copy-start.1 = (f32[3,3,24,384]{3,2,1,0:T(8,128)S(1)}, f32[3,3,24,384]{3,2,1,0:T(8,128)}, u32[]{:S(2)}) copy-start(f32[3,3,24,384]{3,2,1,0:T(8,128)} %d_ref.5) | copy-start | bytes 995332
  0.7 12.8 %copy-start.4 = (f32[27,1,8,128]{3,2,1,0:T(8,128)S(1)}, f32[27,1,8,128]{3,2,1,0:T(8,128)}, u32[]{:S(2)}) copy-start(f32[27,1,8,128]{3,2,1,0:T(8,128)} %param.7) | copy-start | bytes 331780
  0.7 14.3 %copy-start = (f32[216,1,8,128]{3,2,1,0:T(8,128)S(1)}, f32[216,1,8,128]{3,2,1,0:T(8,128)}, u32[]{:S(2)}) copy-start(f32[216,1,8,128]{3,2,1,0:T(8,128)} %param.8) | copy-start | bytes 2654212
  2.8 12.2 %collective-permute-start = (f32[9,24,384]{2,1,0:T(8,128)}, f32[9,24,384]{2,1,0:T(8,128)S(1)}, u32[]{:S(2)}, u32[]{:S(2)}) collective-permute-start(f32[9,24,384]{2,1,0:T(8,128)} %get-tuple-element.41), channel_id=1, source_target_pairs={{0,112},{1,113},{2,114},{3,115},{4,116},{5,117},{6,118},{7,119},{8... | collective-permute-start | bytes 995336 | tf_op jit(solution)/shard_map/ppermute | solution.py:773
  4.2 10.8 %collective-permute-start.1 = (f32[27,384]{1,0:T(8,128)}, f32[27,384]{1,0:T(8,128)S(1)}, u32[]{:S(2)}, u32[]{:S(2)}) collective-permute-start(f32[27,384]{1,0:T(8,128)} %get-tuple-element.42), channel_id=1, source_target_pairs={{0,15},{1,0},{2,1},{3,2},{4,3},{5,4},{6,5},{7,6},{8,7},{9,8},{10,9... | collective-permute-start | bytes 124424 | tf_op jit(solution)/shard_map/ppermute | solution.py:773
  9.2 5.7 %collective-permute-start.2 = (f32[9,384]{1,0:T(8,128)}, f32[9,384]{1,0:T(8,128)S(1)}, u32[]{:S(2)}, u32[]{:S(2)}) collective-permute-start(f32[9,384]{1,0:T(8,128)} %get-tuple-element.43), channel_id=1, source_target_pairs={{0,127},{1,112},{2,113},{3,114},{4,115},{5,116},{6,117},{7,118},{8... | collective-permute-start | bytes 41480 | tf_op jit(solution)/shard_map/ppermute | solution.py:773
  15.0 14.0 %copy-start.3 = (s32[3,3,24,384]{3,2,1,0:T(8,128)S(1)}, s32[3,3,24,384]{3,2,1,0:T(8,128)}, u32[]{:S(2)}) copy-start(s32[3,3,24,384]{3,2,1,0:T(8,128)} %f_ref.3) | copy-start | bytes 995332
  27.2 4.3 %collective-permute-start.4 = (f32[232,128]{1,0:T(8,128)S(1)}, f32[232,128]{1,0:T(8,128)S(1)}, u32[]{:S(2)}, u32[]{:S(2)}) collective-permute-start(f32[232,128]{1,0:T(8,128)S(1)} %get-tuple-element.45.minus_ref), channel_id=1, source_target_pairs={{0,112},{1,113},{2,114},{3,115},{4,116},{5,117},{6,118},{7,119},{8... | collective-permute-start | bytes 356360 | tf_op jit(solution)/shard_map/ppermute | solution.py:773
  28.7 3.3 %collective-permute-start.3 = (f32[232,128]{1,0:T(8,128)S(1)}, f32[232,128]{1,0:T(8,128)S(1)}, u32[]{:S(2)}, u32[]{:S(2)}) collective-permute-start(f32[232,128]{1,0:T(8,128)S(1)} %get-tuple-element.46.plus_ref), channel_id=1, source_target_pairs={{0,16},{1,17},{2,18},{3,19},{4,20},{5,21},{6,22},{7,23},{8,24},{9,... | collective-permute-start | bytes 356360 | tf_op jit(solution)/shard_map/ppermute | solution.py:773
  32.1 6.0 %collective-permute-start.5 = (f32[40,128]{1,0:T(8,128)S(1)}, f32[40,128]{1,0:T(8,128)S(1)}, u32[]{:S(2)}, u32[]{:S(2)}) collective-permute-start(f32[40,128]{1,0:T(8,128)S(1)} %get-tuple-element.51), channel_id=1, source_target_pairs={{0,1},{1,2},{2,3},{3,4},{4,5},{5,6},{6,7},{7,8},{8,9},{9,10},{10,1... | collective-permute-start | bytes 61448 | tf_op jit(solution)/shard_map/ppermute | solution.py:773
  32.5 5.5 %collective-permute-start.6 = (f32[40,128]{1,0:T(8,128)S(1)}, f32[40,128]{1,0:T(8,128)S(1)}, u32[]{:S(2)}, u32[]{:S(2)}) collective-permute-start(f32[40,128]{1,0:T(8,128)S(1)} %get-tuple-element.52), channel_id=1, source_target_pairs={{0,15},{1,0},{2,1},{3,2},{4,3},{5,4},{6,5},{7,6},{8,7},{9,8},{10,9... | collective-permute-start | bytes 61448 | tf_op jit(solution)/shard_map/ppermute | solution.py:773
  40.2 6.8 %collective-permute-start.8 = (f32[232,128]{1,0:T(8,128)S(1)}, f32[232,128]{1,0:T(8,128)S(1)}, u32[]{:S(2)}, u32[]{:S(2)}) collective-permute-start(f32[232,128]{1,0:T(8,128)S(1)} %get-tuple-element.56.minus_ref), channel_id=1, source_target_pairs={{0,112},{1,113},{2,114},{3,115},{4,116},{5,117},{6,118},{7,119},{8... | collective-permute-start | bytes 356360 | tf_op jit(solution)/shard_map/ppermute | solution.py:773
  46.0 1.8 %collective-permute-start.7 = (f32[232,128]{1,0:T(8,128)S(1)}, f32[232,128]{1,0:T(8,128)S(1)}, u32[]{:S(2)}, u32[]{:S(2)}) collective-permute-start(f32[232,128]{1,0:T(8,128)S(1)} %get-tuple-element.57.plus_ref), channel_id=1, source_target_pairs={{0,16},{1,17},{2,18},{3,19},{4,20},{5,21},{6,22},{7,23},{8,24},{9,... | collective-permute-start | bytes 356360 | tf_op jit(solution)/shard_map/ppermute | solution.py:773
  47.9 6.3 %collective-permute-start.9 = (f32[40,128]{1,0:T(8,128)S(1)}, f32[40,128]{1,0:T(8,128)S(1)}, u32[]{:S(2)}, u32[]{:S(2)}) collective-permute-start(f32[40,128]{1,0:T(8,128)S(1)} %get-tuple-element.60), channel_id=1, source_target_pairs={{0,1},{1,2},{2,3},{3,4},{4,5},{5,6},{6,7},{7,8},{8,9},{9,10},{10,1... | collective-permute-start | bytes 61448 | tf_op jit(solution)/shard_map/ppermute | solution.py:773
  48.0 6.2 %collective-permute-start.10 = (f32[40,128]{1,0:T(8,128)S(1)}, f32[40,128]{1,0:T(8,128)S(1)}, u32[]{:S(2)}, u32[]{:S(2)}) collective-permute-start(f32[40,128]{1,0:T(8,128)S(1)} %get-tuple-element.61), channel_id=1, source_target_pairs={{0,15},{1,0},{2,1},{3,2},{4,3},{5,4},{6,5},{7,6},{8,7},{9,8},{10,9... | collective-permute-start | bytes 61448 | tf_op jit(solution)/shard_map/ppermute | solution.py:773
  56.3 5.8 %collective-permute-start.12 = (f32[232,128]{1,0:T(8,128)S(1)}, f32[232,128]{1,0:T(8,128)S(1)}, u32[]{:S(2)}, u32[]{:S(2)}) collective-permute-start(f32[232,128]{1,0:T(8,128)S(1)} %get-tuple-element.62.minus_ref), channel_id=1, source_target_pairs={{0,112},{1,113},{2,114},{3,115},{4,116},{5,117},{6,118},{7,119},{8... | collective-permute-start | bytes 356360 | tf_op jit(solution)/shard_map/ppermute | solution.py:773
  60.9 1.8 %collective-permute-start.11 = (f32[232,128]{1,0:T(8,128)S(1)}, f32[232,128]{1,0:T(8,128)S(1)}, u32[]{:S(2)}, u32[]{:S(2)}) collective-permute-start(f32[232,128]{1,0:T(8,128)S(1)} %get-tuple-element.63.plus_ref), channel_id=1, source_target_pairs={{0,16},{1,17},{2,18},{3,19},{4,20},{5,21},{6,22},{7,23},{8,24},{9,... | collective-permute-start | bytes 356360 | tf_op jit(solution)/shard_map/ppermute | solution.py:773
  62.8 6.4 %collective-permute-start.13 = (f32[40,128]{1,0:T(8,128)S(1)}, f32[40,128]{1,0:T(8,128)S(1)}, u32[]{:S(2)}, u32[]{:S(2)}) collective-permute-start(f32[40,128]{1,0:T(8,128)S(1)} %get-tuple-element.66), channel_id=1, source_target_pairs={{0,1},{1,2},{2,3},{3,4},{4,5},{5,6},{6,7},{7,8},{8,9},{9,10},{10,1... | collective-permute-start | bytes 61448 | tf_op jit(solution)/shard_map/ppermute | solution.py:773
  62.8 6.3 %collective-permute-start.14 = (f32[40,128]{1,0:T(8,128)S(1)}, f32[40,128]{1,0:T(8,128)S(1)}, u32[]{:S(2)}, u32[]{:S(2)}) collective-permute-start(f32[40,128]{1,0:T(8,128)S(1)} %get-tuple-element.67), channel_id=1, source_target_pairs={{0,15},{1,0},{2,1},{3,2},{4,3},{5,4},{6,5},{7,6},{8,7},{9,8},{10,9... | collective-permute-start | bytes 61448 | tf_op jit(solution)/shard_map/ppermute | solution.py:773

commit v7 on v6

--- a/solution.py
+++ b/solution.py
@@ -153,23 +153,18 @@
     lane = iotas(rows)[1]
     out = []
     for g in range(3):
-        place = 3 * lane + g
-        index = place & 127
-        moved = [gather_lanes(p, index) for p in parts]
-        out.append(
-            jnp.where(place < 128, moved[0], jnp.where(place < 256, moved[1], moved[2]))
-        )
+        place = 3 * ((43 * (lane - g)) & 127) + g
+        held = jnp.where(place < 128, parts[0], jnp.where(place < 256, parts[1], parts[2]))
+        out.append(gather_lanes(held, (3 * lane + g) & 127))
     return out
 
 
 def join_lanes(parts):
     lane = iotas()[1]
+    moved = [gather_lanes(p, (43 * (lane - g)) & 127) for g, p in enumerate(parts)]
     out = []
     for v in range(3):
-        place = lane + 128 * v
-        index = place // 3
-        g = place - 3 * index
-        moved = [gather_lanes(p, index) for p in parts]
+        g = (lane + 128 * v) % 3
         out.append(jnp.where(g == 0, moved[0], jnp.where(g == 1, moved[1], moved[2])))
     return out
 

time: 92.8 us -> 92.2 us (level)
  Pallas kernels: 26 us -> 24.2 us
  waiting for transfers between devices: 7.54 us -> 8.72 us
    pallas_call x11, Pallas kernels: 26 us -> 24.2 us  [run(): pl.pallas_call(kernel, out_shape=[jax.ShapeDtypeStruct(s, F32) for s in o...]
    ppermute x15, waiting for transfers between devices: 7.54 us -> 8.72 us  [moved(): return lax.ppermute(value, ('gx', 'gy'), pairs)]
  transfers between devices with their start and end apart: 15 -> 15, of which waited for: 8 -> 10; matrix products, arithmetic and copies ran while one was open for 0% -> 0% of each run, Pallas kernels for 4% -> 3%
where the time goes in v7:
time: 92.2 us; the launch traced here: 92 us
  starting transfers between devices  38.1 us (41%)
  Pallas kernels  24.2 us (26%)
  blocking collectives  20.2 us (22%)
  waiting for transfers between devices  8.72 us (9%)
    ppermute x15, starting transfers between devices, moved(): return lax.ppermute(value, ('gx', 'gy'), pairs)  38.1 us
    pallas_call x11, Pallas kernels, run(): pl.pallas_call(kernel, out_shape=[jax.ShapeDtypeStruct(s, F32) for s in o...  24.2 us
    all_to_all x1, blocking collectives, on_device(): sums = lax.all_to_all(sums, ('gx', 'gy'), 0, 0).reshape(-1, 128)  20.2 us
    ppermute x15, waiting for transfers between devices, moved(): return lax.ppermute(value, ('gx', 'gy'), pairs)  8.72 us
  transfers between devices with their start and end apart: 15, of which 10 were waited for; matrix products, arithmetic and copies ran while one was open for 0% of the time, Pallas kernels for 3%

profile of v7, /device:TPU:1, one launch (start us, length us, event | category | flops | bytes accessed | tf_op | source)
XLA Modules:
  0.0 92.0 jit_solution(6600355977304103403)
XLA Ops:
  0.6 0.0 copy-start.2
  0.6 0.0 copy-start.1
  0.7 0.0 copy-start.4
  0.7 0.0 copy-start
  0.7 2.1 %pack.1 = (f32[9,24,384]{2,1,0:T(8,128)}, f32[27,384]{1,0:T(8,128)}, f32[9,384]{1,0:T(8,128)}) custom-call(f32[3,3,24,384]{3,2,1,0:T(8,128)} %d_ref.5, f32[3,3,24,384]{3,2,1,0:T(8,128)} %vel_ref.1, s32[3,3,24,384]{3,2,1,0:T(8,128)} %f_ref.3), custom_call_target="tpu_custom_call" | custom-call | bytes 1382400 | tf_op jit(solution)/shard_map/pack/pallas_call | solution.py:741
  2.8 1.4 %collective-permute-start = (f32[9,24,384]{2,1,0:T(8,128)}, f32[9,24,384]{2,1,0:T(8,128)S(1)}, u32[]{:S(2)}, u32[]{:S(2)}) collective-permute-start(f32[9,24,384]{2,1,0:T(8,128)} %get-tuple-element.41), channel_id=1, source_target_pairs={{0,112},{1,113},{2,114},{3,115},{4,116},{5,117},{6,118},{7,119},{8... | collective-permute-start | bytes 995336 | tf_op jit(solution)/shard_map/ppermute | solution.py:768
  4.2 5.0 %collective-permute-start.1 = (f32[27,384]{1,0:T(8,128)}, f32[27,384]{1,0:T(8,128)S(1)}, u32[]{:S(2)}, u32[]{:S(2)}) collective-permute-start(f32[27,384]{1,0:T(8,128)} %get-tuple-element.42), channel_id=1, source_target_pairs={{0,15},{1,0},{2,1},{3,2},{4,3},{5,4},{6,5},{7,6},{8,7},{9,8},{10,9... | collective-permute-start | bytes 124424 | tf_op jit(solution)/shard_map/ppermute | solution.py:768
  9.2 4.2 %collective-permute-start.2 = (f32[9,384]{1,0:T(8,128)}, f32[9,384]{1,0:T(8,128)S(1)}, u32[]{:S(2)}, u32[]{:S(2)}) collective-permute-start(f32[9,384]{1,0:T(8,128)} %get-tuple-element.43), channel_id=1, source_target_pairs={{0,127},{1,112},{2,113},{3,114},{4,115},{5,116},{6,117},{7,118},{8... | collective-permute-start | bytes 41480 | tf_op jit(solution)/shard_map/ppermute | solution.py:768
  13.4 0.0 copy-done.2
  13.4 0.0 copy-done.1
  13.4 0.0 copy-done.4
  13.4 0.9 prep.1
  14.3 0.4 collective-permute-done.2.hc_ref
  14.7 0.0 collective-permute-done.1.hy_ref
  14.7 0.0 collective-permute-done.hx_ref
  14.7 0.0 copy-done
  14.7 0.0 copy-start.3
  14.7 11.9 %force.1 = (f32[232,128]{1,0:T(8,128)S(1)}, f32[232,128]{1,0:T(8,128)S(1)}, f32[2,27,8,128]{3,2,1,0:T(8,128)S(1)}, f32[2,16,128]{2,1,0:T(8,128)S(1)}, f32[216,8,128]{2,1,0:T(8,128)S(1)}) custom-call(f32[6,27,8,128]{3,2,1,0:T(8,128)S(1)} %get-tuple-element.40.u_ref, f32[9,24,384]{2,1,0:T(8,128)S(1)} %collective-permute-done.hx_ref, ...), custom_call_target="tpu_custom_call" | custom-call | flops 92160000 | bytes 4179968 | tf_op jit(solution)/shard_map/force/pallas_call | solution.py:741
  26.6 1.8 %collective-permute-start.4 = (f32[232,128]{1,0:T(8,128)S(1)}, f32[232,128]{1,0:T(8,128)S(1)}, u32[]{:S(2)}, u32[]{:S(2)}) collective-permute-start(f32[232,128]{1,0:T(8,128)S(1)} %get-tuple-element.45.minus_ref), channel_id=1, source_target_pairs={{0,112},{1,113},{2,114},{3,115},{4,116},{5,117},{6,118},{7,119},{8... | collective-permute-start | bytes 356360 | tf_op jit(solution)/shard_map/ppermute | solution.py:768
  28.4 0.0 collective-permute-start.3
  28.4 0.0 copy-done.3
  28.4 2.0 %energy.1 = (f32[27,8,128]{2,1,0:T(8,128)}, f32[8,128]{1,0:T(8,128)S(1)}, f32[3,27,8,128]{3,2,1,0:T(8,128)S(1)}, f32[27,8,128]{2,1,0:T(8,128)S(1)}, f32[4,16,128]{2,1,0:T(8,128)S(1)}) custom-call(f32[216,8,128]{2,1,0:T(8,128)S(1)} %get-tuple-element.49.power_ref, f32[216,8,128]{2,1,0:T(8,128)S(1)} %bitcast.10, f32[27,8,128]{2,1,0:T(8,128)S(1)} %bitcast.15, ...), custom_call_target="tpu_custom_call" | custom-call | flops 2048000 | bytes 3188736 | tf_op jit(solution)/shard_map/energy/pallas_call | solution.py:741
  30.4 0.5 collective-permute-done.4.got_high_ref.high_ref
  30.9 0.9 collective-permute-done.3.got_low_ref.low_ref
  31.8 0.1 collective-permute-start.5
  31.9 4.8 %collective-permute-start.6 = (f32[40,128]{1,0:T(8,128)S(1)}, f32[40,128]{1,0:T(8,128)S(1)}, u32[]{:S(2)}, u32[]{:S(2)}) collective-permute-start(f32[40,128]{1,0:T(8,128)S(1)} %get-tuple-element.52), channel_id=1, source_target_pairs={{0,15},{1,0},{2,1},{3,2},{4,3},{5,4},{6,5},{7,6},{8,7},{9,8},{10,9... | collective-permute-start | bytes 61448 | tf_op jit(solution)/shard_map/ppermute | solution.py:768
  36.6 1.2 %collective-permute-done.5.from_down_ref = f32[40,128]{1,0:T(8,128)S(1)} collective-permute-done((f32[40,128]{1,0:T(8,128)S(1)}, f32[40,128]{1,0:T(8,128)S(1)}, u32[]{:S(2)}, u32[]{:S(2)}) %collective-permute-start.5) | collective-permute-done | bytes 20512 | tf_op jit(solution)/shard_map/ppermute | solution.py:768
  37.8 0.0 collective-permute-done.6.from_up_ref
  37.8 2.1 %apply.2 = (f32[3,27,8,128]{3,2,1,0:T(8,128)S(1)}, f32[232,128]{1,0:T(8,128)S(1)}, f32[232,128]{1,0:T(8,128)S(1)}, f32[2,27,8,128]{3,2,1,0:T(8,128)S(1)}, f32[2,16,128]{2,1,0:T(8,128)S(1)}) custom-call(f32[232,128]{1,0:T(8,128)S(1)} %get-tuple-element.45.minus_ref, f32[232,128]{1,0:T(8,128)S(1)} %get-tuple-element.46.plus_ref, ...), custom_call_target="tpu_custom_call" | custom-call | flops 13312000 | bytes 2920448 | tf_op jit(solution)/shard_map/apply/pallas_call | solution.py:741
  40.0 5.8 %collective-permute-start.8 = (f32[232,128]{1,0:T(8,128)S(1)}, f32[232,128]{1,0:T(8,128)S(1)}, u32[]{:S(2)}, u32[]{:S(2)}) collective-permute-start(f32[232,128]{1,0:T(8,128)S(1)} %get-tuple-element.56.minus_ref), channel_id=1, source_target_pairs={{0,112},{1,113},{2,114},{3,115},{4,116},{5,117},{6,118},{7,119},{8... | collective-permute-start | bytes 356360 | tf_op jit(solution)/shard_map/ppermute | solution.py:768
  45.8 0.0 collective-permute-start.7
  45.8 1.0 %collective-permute-done.8.got_high_ref.high_ref = f32[232,128]{1,0:T(8,128)S(1)} collective-permute-done((f32[232,128]{1,0:T(8,128)S(1)}, f32[232,128]{1,0:T(8,128)S(1)}, u32[]{:S(2)}, u32[]{:S(2)}) %collective-permute-start.8) | collective-permute-done | bytes 118816 | tf_op jit(solution)/shard_map/ppermute | solution.py:768
  46.7 0.9 collective-permute-done.7.got_low_ref.low_ref
  47.6 0.1 collective-permute-start.9
  47.7 5.1 %collective-permute-start.10 = (f32[40,128]{1,0:T(8,128)S(1)}, f32[40,128]{1,0:T(8,128)S(1)}, u32[]{:S(2)}, u32[]{:S(2)}) collective-permute-start(f32[40,128]{1,0:T(8,128)S(1)} %get-tuple-element.61), channel_id=1, source_target_pairs={{0,15},{1,0},{2,1},{3,2},{4,3},{5,4},{6,5},{7,6},{8,7},{9,8},{10,9... | collective-permute-start | bytes 61448 | tf_op jit(solution)/shard_map/ppermute | solution.py:768
  52.8 1.1 %collective-permute-done.9.from_down_ref = f32[40,128]{1,0:T(8,128)S(1)} collective-permute-done((f32[40,128]{1,0:T(8,128)S(1)}, f32[40,128]{1,0:T(8,128)S(1)}, u32[]{:S(2)}, u32[]{:S(2)}) %collective-permute-start.9) | collective-permute-done | bytes 20512 | tf_op jit(solution)/shard_map/ppermute | solution.py:768
  53.9 0.0 collective-permute-done.10.from_up_ref
  53.9 2.1 %apply.3 = (f32[3,27,8,128]{3,2,1,0:T(8,128)S(1)}, f32[232,128]{1,0:T(8,128)S(1)}, f32[232,128]{1,0:T(8,128)S(1)}, f32[2,27,8,128]{3,2,1,0:T(8,128)S(1)}, f32[2,16,128]{2,1,0:T(8,128)S(1)}) custom-call(f32[232,128]{1,0:T(8,128)S(1)} %get-tuple-element.56.minus_ref, f32[232,128]{1,0:T(8,128)S(1)} %get-tuple-element.57.plus_ref, ...), custom_call_target="tpu_custom_call" | custom-call | flops 13312000 | bytes 2920448 | tf_op jit(solution)/shard_map/apply/pallas_call | solution.py:741
  56.1 4.5 %collective-permute-start.12 = (f32[232,128]{1,0:T(8,128)S(1)}, f32[232,128]{1,0:T(8,128)S(1)}, u32[]{:S(2)}, u32[]{:S(2)}) collective-permute-start(f32[232,128]{1,0:T(8,128)S(1)} %get-tuple-element.62.minus_ref), channel_id=1, source_target_pairs={{0,112},{1,113},{2,114},{3,115},{4,116},{5,117},{6,118},{7,119},{8... | collective-permute-start | bytes 356360 | tf_op jit(solution)/shard_map/ppermute | solution.py:768
  60.6 0.0 collective-permute-start.11
  60.6 1.3 %collective-permute-done.12.got_high_ref.high_ref = f32[232,128]{1,0:T(8,128)S(1)} collective-permute-done((f32[232,128]{1,0:T(8,128)S(1)}, f32[232,128]{1,0:T(8,128)S(1)}, u32[]{:S(2)}, u32[]{:S(2)}) %collective-permute-start.12) | collective-permute-done | bytes 118816 | tf_op jit(solution)/shard_map/ppermute | solution.py:768
  61.9 0.5 collective-permute-done.11.got_low_ref.low_ref
  62.5 0.1 collective-permute-start.13
  62.6 5.2 %collective-permute-start.14 = (f32[40,128]{1,0:T(8,128)S(1)}, f32[40,128]{1,0:T(8,128)S(1)}, u32[]{:S(2)}, u32[]{:S(2)}) collective-permute-start(f32[40,128]{1,0:T(8,128)S(1)} %get-tuple-element.67), channel_id=1, source_target_pairs={{0,15},{1,0},{2,1},{3,2},{4,3},{5,4},{6,5},{7,6},{8,7},{9,8},{10,9... | collective-permute-start | bytes 61448 | tf_op jit(solution)/shard_map/ppermute | solution.py:768
  67.8 1.1 %collective-permute-done.13.from_down_ref = f32[40,128]{1,0:T(8,128)S(1)} collective-permute-done((f32[40,128]{1,0:T(8,128)S(1)}, f32[40,128]{1,0:T(8,128)S(1)}, u32[]{:S(2)}, u32[]{:S(2)}) %collective-permute-start.13) | collective-permute-done | bytes 20512 | tf_op jit(solution)/shard_map/ppermute | solution.py:768
  68.9 0.0 collective-permute-done.14.from_up_ref
  68.9 1.6 %moments.1 = (f32[3,27,8,128]{3,2,1,0:T(8,128)S(1)}, f32[128,128]{1,0:T(8,128)S(1)}) custom-call(f32[232,128]{1,0:T(8,128)S(1)} %get-tuple-element.62.minus_ref, f32[232,128]{1,0:T(8,128)S(1)} %get-tuple-element.63.plus_ref, f32[2,27,8,128]{3,2,1,0:T(8,128)S(1)} %get-tuple-element.64.inner_ref, f32[2,16,128]{2,1,0:T(8,128)S(1)} %get-tuple-element.65.rim_ref, ...), custom_call_target="tpu_custom_call" | custom-call | flops 8192000 | bytes 3174400 | tf_op jit(solution)/shard_map/moments/pallas_call | solution.py:741
  70.4 20.2 %all_to_all.5 = f32[128,1,128]{2,1,0:T(1,128)S(1)} all-to-all(f32[128,1,128]{2,1,0:T(1,128)S(1)} %bitcast.17), channel_id=1, replica_groups=mesh['gx'=8,'gy'=16] {'gx','gy'}, dimensions={0} | all-to-all | bytes 131072 | tf_op jit(solution)/shard_map/all_to_all | solution.py:840
  90.6 1.4 %final.1 = (f32[3,3,24,384]{3,2,1,0:T(8,128)}, f32[3,3,24,384]{3,2,1,0:T(8,128)}, f32[3,3,24,384]{3,2,1,0:T(8,128)}) custom-call(f32[128,128]{1,0:T(8,128)S(1)} %bitcast.16, f32[3,27,8,128]{3,2,1,0:T(8,128)S(1)} %get-tuple-element.68.r_ref, f32[3,27,8,128]{3,2,1,0:T(8,128)S(1)} %get-tuple-element.69.v_ref, f32[3,27,8,128]{3,2,1,0:T(8,128)S(1)} %get-tuple-element.71.w_ref, ...), custom_call_target="tpu_custom_call" | custom-call | flops 1024000 | bytes 2719744 | tf_op jit(solution)/shard_map/final/pallas_call | solution.py:741
  (3 shorter events, 0.1 us)
Async XLA Ops:
  0.6 12.8 %copy-start.2 = (f32[3,3,24,384]{3,2,1,0:T(8,128)S(1)}, f32[3,3,24,384]{3,2,1,0:T(8,128)}, u32[]{:S(2)}) copy-start(f32[3,3,24,384]{3,2,1,0:T(8,128)} %vel_ref.1) | copy-start | bytes 995332
  0.6 12.8 %copy-start.1 = (f32[3,3,24,384]{3,2,1,0:T(8,128)S(1)}, f32[3,3,24,384]{3,2,1,0:T(8,128)}, u32[]{:S(2)}) copy-start(f32[3,3,24,384]{3,2,1,0:T(8,128)} %d_ref.5) | copy-start | bytes 995332
  0.7 12.8 %copy-start.4 = (f32[27,1,8,128]{3,2,1,0:T(8,128)S(1)}, f32[27,1,8,128]{3,2,1,0:T(8,128)}, u32[]{:S(2)}) copy-start(f32[27,1,8,128]{3,2,1,0:T(8,128)} %param.7) | copy-start | bytes 331780
  0.7 14.0 %copy-start = (f32[216,1,8,128]{3,2,1,0:T(8,128)S(1)}, f32[216,1,8,128]{3,2,1,0:T(8,128)}, u32[]{:S(2)}) copy-start(f32[216,1,8,128]{3,2,1,0:T(8,128)} %param.8) | copy-start | bytes 2654212
  2.8 11.9 %collective-permute-start = (f32[9,24,384]{2,1,0:T(8,128)}, f32[9,24,384]{2,1,0:T(8,128)S(1)}, u32[]{:S(2)}, u32[]{:S(2)}) collective-permute-start(f32[9,24,384]{2,1,0:T(8,128)} %get-tuple-element.41), channel_id=1, source_target_pairs={{0,112},{1,113},{2,114},{3,115},{4,116},{5,117},{6,118},{7,119},{8... | collective-permute-start | bytes 995336 | tf_op jit(solution)/shard_map/ppermute | solution.py:768
  4.2 10.5 %collective-permute-start.1 = (f32[27,384]{1,0:T(8,128)}, f32[27,384]{1,0:T(8,128)S(1)}, u32[]{:S(2)}, u32[]{:S(2)}) collective-permute-start(f32[27,384]{1,0:T(8,128)} %get-tuple-element.42), channel_id=1, source_target_pairs={{0,15},{1,0},{2,1},{3,2},{4,3},{5,4},{6,5},{7,6},{8,7},{9,8},{10,9... | collective-permute-start | bytes 124424 | tf_op jit(solution)/shard_map/ppermute | solution.py:768
  9.2 5.4 %collective-permute-start.2 = (f32[9,384]{1,0:T(8,128)}, f32[9,384]{1,0:T(8,128)S(1)}, u32[]{:S(2)}, u32[]{:S(2)}) collective-permute-start(f32[9,384]{1,0:T(8,128)} %get-tuple-element.43), channel_id=1, source_target_pairs={{0,127},{1,112},{2,113},{3,114},{4,115},{5,116},{6,117},{7,118},{8... | collective-permute-start | bytes 41480 | tf_op jit(solution)/shard_map/ppermute | solution.py:768
  14.7 13.8 %copy-start.3 = (s32[3,3,24,384]{3,2,1,0:T(8,128)S(1)}, s32[3,3,24,384]{3,2,1,0:T(8,128)}, u32[]{:S(2)}) copy-start(s32[3,3,24,384]{3,2,1,0:T(8,128)} %f_ref.3) | copy-start | bytes 995332
  26.6 4.3 %collective-permute-start.4 = (f32[232,128]{1,0:T(8,128)S(1)}, f32[232,128]{1,0:T(8,128)S(1)}, u32[]{:S(2)}, u32[]{:S(2)}) collective-permute-start(f32[232,128]{1,0:T(8,128)S(1)} %get-tuple-element.45.minus_ref), channel_id=1, source_target_pairs={{0,112},{1,113},{2,114},{3,115},{4,116},{5,117},{6,118},{7,119},{8... | collective-permute-start | bytes 356360 | tf_op jit(solution)/shard_map/ppermute | solution.py:768
  28.4 3.3 %collective-permute-start.3 = (f32[232,128]{1,0:T(8,128)S(1)}, f32[232,128]{1,0:T(8,128)S(1)}, u32[]{:S(2)}, u32[]{:S(2)}) collective-permute-start(f32[232,128]{1,0:T(8,128)S(1)} %get-tuple-element.46.plus_ref), channel_id=1, source_target_pairs={{0,16},{1,17},{2,18},{3,19},{4,20},{5,21},{6,22},{7,23},{8,24},{9,... | collective-permute-start | bytes 356360 | tf_op jit(solution)/shard_map/ppermute | solution.py:768
  31.8 6.0 %collective-permute-start.5 = (f32[40,128]{1,0:T(8,128)S(1)}, f32[40,128]{1,0:T(8,128)S(1)}, u32[]{:S(2)}, u32[]{:S(2)}) collective-permute-start(f32[40,128]{1,0:T(8,128)S(1)} %get-tuple-element.51), channel_id=1, source_target_pairs={{0,1},{1,2},{2,3},{3,4},{4,5},{5,6},{6,7},{7,8},{8,9},{9,10},{10,1... | collective-permute-start | bytes 61448 | tf_op jit(solution)/shard_map/ppermute | solution.py:768
  31.9 5.9 %collective-permute-start.6 = (f32[40,128]{1,0:T(8,128)S(1)}, f32[40,128]{1,0:T(8,128)S(1)}, u32[]{:S(2)}, u32[]{:S(2)}) collective-permute-start(f32[40,128]{1,0:T(8,128)S(1)} %get-tuple-element.52), channel_id=1, source_target_pairs={{0,15},{1,0},{2,1},{3,2},{4,3},{5,4},{6,5},{7,6},{8,7},{9,8},{10,9... | collective-permute-start | bytes 61448 | tf_op jit(solution)/shard_map/ppermute | solution.py:768
  40.0 6.8 %collective-permute-start.8 = (f32[232,128]{1,0:T(8,128)S(1)}, f32[232,128]{1,0:T(8,128)S(1)}, u32[]{:S(2)}, u32[]{:S(2)}) collective-permute-start(f32[232,128]{1,0:T(8,128)S(1)} %get-tuple-element.56.minus_ref), channel_id=1, source_target_pairs={{0,112},{1,113},{2,114},{3,115},{4,116},{5,117},{6,118},{7,119},{8... | collective-permute-start | bytes 356360 | tf_op jit(solution)/shard_map/ppermute | solution.py:768
  45.8 1.8 %collective-permute-start.7 = (f32[232,128]{1,0:T(8,128)S(1)}, f32[232,128]{1,0:T(8,128)S(1)}, u32[]{:S(2)}, u32[]{:S(2)}) collective-permute-start(f32[232,128]{1,0:T(8,128)S(1)} %get-tuple-element.57.plus_ref), channel_id=1, source_target_pairs={{0,16},{1,17},{2,18},{3,19},{4,20},{5,21},{6,22},{7,23},{8,24},{9,... | collective-permute-start | bytes 356360 | tf_op jit(solution)/shard_map/ppermute | solution.py:768
  47.6 6.3 %collective-permute-start.9 = (f32[40,128]{1,0:T(8,128)S(1)}, f32[40,128]{1,0:T(8,128)S(1)}, u32[]{:S(2)}, u32[]{:S(2)}) collective-permute-start(f32[40,128]{1,0:T(8,128)S(1)} %get-tuple-element.60), channel_id=1, source_target_pairs={{0,1},{1,2},{2,3},{3,4},{4,5},{5,6},{6,7},{7,8},{8,9},{9,10},{10,1... | collective-permute-start | bytes 61448 | tf_op jit(solution)/shard_map/ppermute | solution.py:768
  47.7 6.2 %collective-permute-start.10 = (f32[40,128]{1,0:T(8,128)S(1)}, f32[40,128]{1,0:T(8,128)S(1)}, u32[]{:S(2)}, u32[]{:S(2)}) collective-permute-start(f32[40,128]{1,0:T(8,128)S(1)} %get-tuple-element.61), channel_id=1, source_target_pairs={{0,15},{1,0},{2,1},{3,2},{4,3},{5,4},{6,5},{7,6},{8,7},{9,8},{10,9... | collective-permute-start | bytes 61448 | tf_op jit(solution)/shard_map/ppermute | solution.py:768
  56.1 5.8 %collective-permute-start.12 = (f32[232,128]{1,0:T(8,128)S(1)}, f32[232,128]{1,0:T(8,128)S(1)}, u32[]{:S(2)}, u32[]{:S(2)}) collective-permute-start(f32[232,128]{1,0:T(8,128)S(1)} %get-tuple-element.62.minus_ref), channel_id=1, source_target_pairs={{0,112},{1,113},{2,114},{3,115},{4,116},{5,117},{6,118},{7,119},{8... | collective-permute-start | bytes 356360 | tf_op jit(solution)/shard_map/ppermute | solution.py:768
  60.6 1.8 %collective-permute-start.11 = (f32[232,128]{1,0:T(8,128)S(1)}, f32[232,128]{1,0:T(8,128)S(1)}, u32[]{:S(2)}, u32[]{:S(2)}) collective-permute-start(f32[232,128]{1,0:T(8,128)S(1)} %get-tuple-element.63.plus_ref), channel_id=1, source_target_pairs={{0,16},{1,17},{2,18},{3,19},{4,20},{5,21},{6,22},{7,23},{8,24},{9,... | collective-permute-start | bytes 356360 | tf_op jit(solution)/shard_map/ppermute | solution.py:768
  62.5 6.4 %collective-permute-start.13 = (f32[40,128]{1,0:T(8,128)S(1)}, f32[40,128]{1,0:T(8,128)S(1)}, u32[]{:S(2)}, u32[]{:S(2)}) collective-permute-start(f32[40,128]{1,0:T(8,128)S(1)} %get-tuple-element.66), channel_id=1, source_target_pairs={{0,1},{1,2},{2,3},{3,4},{4,5},{5,6},{6,7},{7,8},{8,9},{9,10},{10,1... | collective-permute-start | bytes 61448 | tf_op jit(solution)/shard_map/ppermute | solution.py:768
  62.6 6.3 %collective-permute-start.14 = (f32[40,128]{1,0:T(8,128)S(1)}, f32[40,128]{1,0:T(8,128)S(1)}, u32[]{:S(2)}, u32[]{:S(2)}) collective-permute-start(f32[40,128]{1,0:T(8,128)S(1)} %get-tuple-element.67), channel_id=1, source_target_pairs={{0,15},{1,0},{2,1},{3,2},{4,3},{5,4},{6,5},{7,6},{8,7},{9,8},{10,9... | collective-permute-start | bytes 61448 | tf_op jit(solution)/shard_map/ppermute | solution.py:768

commit v8 on v7

--- a/solution.py
+++ b/solution.py
@@ -580,7 +580,7 @@
         mass_along_z(c, q_s, zv_s)
         return 0
 
-    lax.fori_loop(0, 3, first, 0)
+    lax.fori_loop(0, 3, first, 0, unroll=True)
 
     def plane(z, _):
         for c in range(3):
@@ -630,7 +630,7 @@
         mass_along_z(c, q_s, zv_s)
         return 0
 
-    lax.fori_loop(0, 3, first, 0)
+    lax.fori_loop(0, 3, first, 0, unroll=True)
     zero = jnp.zeros((8, 128), F32)
 
     def dots(n, s):

time: 92.2 us -> 92.1 us (level)
  no operation moved by 1% of the time
where the time goes in v8:
time: 92.1 us; the launch traced here: 91.9 us
  starting transfers between devices  38.1 us (41%)
  Pallas kernels  24.1 us (26%)
  blocking collectives  20.2 us (22%)
  waiting for transfers between devices  8.72 us (9%)
    ppermute x15, starting transfers between devices, moved(): return lax.ppermute(value, ('gx', 'gy'), pairs)  38.1 us
    pallas_call x11, Pallas kernels, run(): pl.pallas_call(kernel, out_shape=[jax.ShapeDtypeStruct(s, F32) for s in o...  24.1 us
    all_to_all x1, blocking collectives, on_device(): sums = lax.all_to_all(sums, ('gx', 'gy'), 0, 0).reshape(-1, 128)  20.2 us
    ppermute x15, waiting for transfers between devices, moved(): return lax.ppermute(value, ('gx', 'gy'), pairs)  8.72 us
  transfers between devices with their start and end apart: 15, of which 10 were waited for; matrix products, arithmetic and copies ran while one was open for 0% of the time, Pallas kernels for 3%

profile of v8, /device:TPU:1, one launch (start us, length us, event | category | flops | bytes accessed | tf_op | source)
XLA Modules:
  0.0 91.9 jit_solution(15700621450404702453)
XLA Ops:
  0.6 0.0 copy-start.2
  0.6 0.0 copy-start.1
  0.7 0.0 copy-start.4
  0.7 0.0 copy-start
  0.7 2.1 %pack.1 = (f32[9,24,384]{2,1,0:T(8,128)}, f32[27,384]{1,0:T(8,128)}, f32[9,384]{1,0:T(8,128)}) custom-call(f32[3,3,24,384]{3,2,1,0:T(8,128)} %d_ref.5, f32[3,3,24,384]{3,2,1,0:T(8,128)} %vel_ref.1, s32[3,3,24,384]{3,2,1,0:T(8,128)} %f_ref.3), custom_call_target="tpu_custom_call" | custom-call | bytes 1382400 | tf_op jit(solution)/shard_map/pack/pallas_call | solution.py:741
  2.8 1.4 %collective-permute-start = (f32[9,24,384]{2,1,0:T(8,128)}, f32[9,24,384]{2,1,0:T(8,128)S(1)}, u32[]{:S(2)}, u32[]{:S(2)}) collective-permute-start(f32[9,24,384]{2,1,0:T(8,128)} %get-tuple-element.41), channel_id=1, source_target_pairs={{0,112},{1,113},{2,114},{3,115},{4,116},{5,117},{6,118},{7,119},{8... | collective-permute-start | bytes 995336 | tf_op jit(solution)/shard_map/ppermute | solution.py:768
  4.2 5.0 %collective-permute-start.1 = (f32[27,384]{1,0:T(8,128)}, f32[27,384]{1,0:T(8,128)S(1)}, u32[]{:S(2)}, u32[]{:S(2)}) collective-permute-start(f32[27,384]{1,0:T(8,128)} %get-tuple-element.42), channel_id=1, source_target_pairs={{0,15},{1,0},{2,1},{3,2},{4,3},{5,4},{6,5},{7,6},{8,7},{9,8},{10,9... | collective-permute-start | bytes 124424 | tf_op jit(solution)/shard_map/ppermute | solution.py:768
  9.2 4.2 %collective-permute-start.2 = (f32[9,384]{1,0:T(8,128)}, f32[9,384]{1,0:T(8,128)S(1)}, u32[]{:S(2)}, u32[]{:S(2)}) collective-permute-start(f32[9,384]{1,0:T(8,128)} %get-tuple-element.43), channel_id=1, source_target_pairs={{0,127},{1,112},{2,113},{3,114},{4,115},{5,116},{6,117},{7,118},{8... | collective-permute-start | bytes 41480 | tf_op jit(solution)/shard_map/ppermute | solution.py:768
  13.4 0.0 copy-done.2
  13.4 0.0 copy-done.1
  13.4 0.0 copy-done.4
  13.4 0.9 prep.1
  14.3 0.4 collective-permute-done.2.hc_ref
  14.7 0.0 collective-permute-done.1.hy_ref
  14.7 0.0 collective-permute-done.hx_ref
  14.7 0.0 copy-done
  14.7 0.0 copy-start.3
  14.7 11.9 %force.1 = (f32[232,128]{1,0:T(8,128)S(1)}, f32[232,128]{1,0:T(8,128)S(1)}, f32[2,27,8,128]{3,2,1,0:T(8,128)S(1)}, f32[2,16,128]{2,1,0:T(8,128)S(1)}, f32[216,8,128]{2,1,0:T(8,128)S(1)}) custom-call(f32[6,27,8,128]{3,2,1,0:T(8,128)S(1)} %get-tuple-element.40.u_ref, f32[9,24,384]{2,1,0:T(8,128)S(1)} %collective-permute-done.hx_ref, ...), custom_call_target="tpu_custom_call" | custom-call | flops 92160000 | bytes 4179968 | tf_op jit(solution)/shard_map/force/pallas_call | solution.py:741
  26.6 1.8 %collective-permute-start.4 = (f32[232,128]{1,0:T(8,128)S(1)}, f32[232,128]{1,0:T(8,128)S(1)}, u32[]{:S(2)}, u32[]{:S(2)}) collective-permute-start(f32[232,128]{1,0:T(8,128)S(1)} %get-tuple-element.45.minus_ref), channel_id=1, source_target_pairs={{0,112},{1,113},{2,114},{3,115},{4,116},{5,117},{6,118},{7,119},{8... | collective-permute-start | bytes 356360 | tf_op jit(solution)/shard_map/ppermute | solution.py:768
  28.4 0.0 collective-permute-start.3
  28.4 0.0 copy-done.3
  28.4 2.0 %energy.1 = (f32[27,8,128]{2,1,0:T(8,128)}, f32[8,128]{1,0:T(8,128)S(1)}, f32[3,27,8,128]{3,2,1,0:T(8,128)S(1)}, f32[27,8,128]{2,1,0:T(8,128)S(1)}, f32[4,16,128]{2,1,0:T(8,128)S(1)}) custom-call(f32[216,8,128]{2,1,0:T(8,128)S(1)} %get-tuple-element.49.power_ref, f32[216,8,128]{2,1,0:T(8,128)S(1)} %bitcast.10, f32[27,8,128]{2,1,0:T(8,128)S(1)} %bitcast.15, ...), custom_call_target="tpu_custom_call" | custom-call | flops 2048000 | bytes 3188736 | tf_op jit(solution)/shard_map/energy/pallas_call | solution.py:741
  30.4 0.5 collective-permute-done.4.got_high_ref.high_ref
  30.9 0.9 collective-permute-done.3.got_low_ref.low_ref
  31.8 0.1 collective-permute-start.5
  31.9 4.8 %collective-permute-start.6 = (f32[40,128]{1,0:T(8,128)S(1)}, f32[40,128]{1,0:T(8,128)S(1)}, u32[]{:S(2)}, u32[]{:S(2)}) collective-permute-start(f32[40,128]{1,0:T(8,128)S(1)} %get-tuple-element.52), channel_id=1, source_target_pairs={{0,15},{1,0},{2,1},{3,2},{4,3},{5,4},{6,5},{7,6},{8,7},{9,8},{10,9... | collective-permute-start | bytes 61448 | tf_op jit(solution)/shard_map/ppermute | solution.py:768
  36.6 1.2 %collective-permute-done.5.from_down_ref = f32[40,128]{1,0:T(8,128)S(1)} collective-permute-done((f32[40,128]{1,0:T(8,128)S(1)}, f32[40,128]{1,0:T(8,128)S(1)}, u32[]{:S(2)}, u32[]{:S(2)}) %collective-permute-start.5) | collective-permute-done | bytes 20512 | tf_op jit(solution)/shard_map/ppermute | solution.py:768
  37.8 0.0 collective-permute-done.6.from_up_ref
  37.8 2.1 %apply.2 = (f32[3,27,8,128]{3,2,1,0:T(8,128)S(1)}, f32[232,128]{1,0:T(8,128)S(1)}, f32[232,128]{1,0:T(8,128)S(1)}, f32[2,27,8,128]{3,2,1,0:T(8,128)S(1)}, f32[2,16,128]{2,1,0:T(8,128)S(1)}) custom-call(f32[232,128]{1,0:T(8,128)S(1)} %get-tuple-element.45.minus_ref, f32[232,128]{1,0:T(8,128)S(1)} %get-tuple-element.46.plus_ref, ...), custom_call_target="tpu_custom_call" | custom-call | flops 13312000 | bytes 2920448 | tf_op jit(solution)/shard_map/apply/pallas_call | solution.py:741
  39.9 5.8 %collective-permute-start.8 = (f32[232,128]{1,0:T(8,128)S(1)}, f32[232,128]{1,0:T(8,128)S(1)}, u32[]{:S(2)}, u32[]{:S(2)}) collective-permute-start(f32[232,128]{1,0:T(8,128)S(1)} %get-tuple-element.56.minus_ref), channel_id=1, source_target_pairs={{0,112},{1,113},{2,114},{3,115},{4,116},{5,117},{6,118},{7,119},{8... | collective-permute-start | bytes 356360 | tf_op jit(solution)/shard_map/ppermute | solution.py:768
  45.7 0.0 collective-permute-start.7
  45.7 1.0 %collective-permute-done.8.got_high_ref.high_ref = f32[232,128]{1,0:T(8,128)S(1)} collective-permute-done((f32[232,128]{1,0:T(8,128)S(1)}, f32[232,128]{1,0:T(8,128)S(1)}, u32[]{:S(2)}, u32[]{:S(2)}) %collective-permute-start.8) | collective-permute-done | bytes 118816 | tf_op jit(solution)/shard_map/ppermute | solution.py:768
  46.7 0.9 collective-permute-done.7.got_low_ref.low_ref
  47.6 0.1 collective-permute-start.9
  47.7 5.1 %collective-permute-start.10 = (f32[40,128]{1,0:T(8,128)S(1)}, f32[40,128]{1,0:T(8,128)S(1)}, u32[]{:S(2)}, u32[]{:S(2)}) collective-permute-start(f32[40,128]{1,0:T(8,128)S(1)} %get-tuple-element.61), channel_id=1, source_target_pairs={{0,15},{1,0},{2,1},{3,2},{4,3},{5,4},{6,5},{7,6},{8,7},{9,8},{10,9... | collective-permute-start | bytes 61448 | tf_op jit(solution)/shard_map/ppermute | solution.py:768
  52.8 1.1 %collective-permute-done.9.from_down_ref = f32[40,128]{1,0:T(8,128)S(1)} collective-permute-done((f32[40,128]{1,0:T(8,128)S(1)}, f32[40,128]{1,0:T(8,128)S(1)}, u32[]{:S(2)}, u32[]{:S(2)}) %collective-permute-start.9) | collective-permute-done | bytes 20512 | tf_op jit(solution)/shard_map/ppermute | solution.py:768
  53.9 0.0 collective-permute-done.10.from_up_ref
  53.9 2.1 %apply.3 = (f32[3,27,8,128]{3,2,1,0:T(8,128)S(1)}, f32[232,128]{1,0:T(8,128)S(1)}, f32[232,128]{1,0:T(8,128)S(1)}, f32[2,27,8,128]{3,2,1,0:T(8,128)S(1)}, f32[2,16,128]{2,1,0:T(8,128)S(1)}) custom-call(f32[232,128]{1,0:T(8,128)S(1)} %get-tuple-element.56.minus_ref, f32[232,128]{1,0:T(8,128)S(1)} %get-tuple-element.57.plus_ref, ...), custom_call_target="tpu_custom_call" | custom-call | flops 13312000 | bytes 2920448 | tf_op jit(solution)/shard_map/apply/pallas_call | solution.py:741
  56.0 4.5 %collective-permute-start.12 = (f32[232,128]{1,0:T(8,128)S(1)}, f32[232,128]{1,0:T(8,128)S(1)}, u32[]{:S(2)}, u32[]{:S(2)}) collective-permute-start(f32[232,128]{1,0:T(8,128)S(1)} %get-tuple-element.62.minus_ref), channel_id=1, source_target_pairs={{0,112},{1,113},{2,114},{3,115},{4,116},{5,117},{6,118},{7,119},{8... | collective-permute-start | bytes 356360 | tf_op jit(solution)/shard_map/ppermute | solution.py:768
  60.6 0.0 collective-permute-start.11
  60.6 1.3 %collective-permute-done.12.got_high_ref.high_ref = f32[232,128]{1,0:T(8,128)S(1)} collective-permute-done((f32[232,128]{1,0:T(8,128)S(1)}, f32[232,128]{1,0:T(8,128)S(1)}, u32[]{:S(2)}, u32[]{:S(2)}) %collective-permute-start.12) | collective-permute-done | bytes 118816 | tf_op jit(solution)/shard_map/ppermute | solution.py:768
  61.8 0.5 collective-permute-done.11.got_low_ref.low_ref
  62.4 0.1 collective-permute-start.13
  62.5 5.2 %collective-permute-start.14 = (f32[40,128]{1,0:T(8,128)S(1)}, f32[40,128]{1,0:T(8,128)S(1)}, u32[]{:S(2)}, u32[]{:S(2)}) collective-permute-start(f32[40,128]{1,0:T(8,128)S(1)} %get-tuple-element.67), channel_id=1, source_target_pairs={{0,15},{1,0},{2,1},{3,2},{4,3},{5,4},{6,5},{7,6},{8,7},{9,8},{10,9... | collective-permute-start | bytes 61448 | tf_op jit(solution)/shard_map/ppermute | solution.py:768
  67.7 1.1 %collective-permute-done.13.from_down_ref = f32[40,128]{1,0:T(8,128)S(1)} collective-permute-done((f32[40,128]{1,0:T(8,128)S(1)}, f32[40,128]{1,0:T(8,128)S(1)}, u32[]{:S(2)}, u32[]{:S(2)}) %collective-permute-start.13) | collective-permute-done | bytes 20512 | tf_op jit(solution)/shard_map/ppermute | solution.py:768
  68.8 0.0 collective-permute-done.14.from_up_ref
  68.8 1.5 %moments.1 = (f32[3,27,8,128]{3,2,1,0:T(8,128)S(1)}, f32[128,128]{1,0:T(8,128)S(1)}) custom-call(f32[232,128]{1,0:T(8,128)S(1)} %get-tuple-element.62.minus_ref, f32[232,128]{1,0:T(8,128)S(1)} %get-tuple-element.63.plus_ref, f32[2,27,8,128]{3,2,1,0:T(8,128)S(1)} %get-tuple-element.64.inner_ref, f32[2,16,128]{2,1,0:T(8,128)S(1)} %get-tuple-element.65.rim_ref, ...), custom_call_target="tpu_custom_call" | custom-call | flops 8192000 | bytes 3174400 | tf_op jit(solution)/shard_map/moments/pallas_call | solution.py:741
  70.3 20.2 %all_to_all.5 = f32[128,1,128]{2,1,0:T(1,128)S(1)} all-to-all(f32[128,1,128]{2,1,0:T(1,128)S(1)} %bitcast.17), channel_id=1, replica_groups=mesh['gx'=8,'gy'=16] {'gx','gy'}, dimensions={0} | all-to-all | bytes 131072 | tf_op jit(solution)/shard_map/all_to_all | solution.py:840
  90.5 1.4 %final.1 = (f32[3,3,24,384]{3,2,1,0:T(8,128)}, f32[3,3,24,384]{3,2,1,0:T(8,128)}, f32[3,3,24,384]{3,2,1,0:T(8,128)}) custom-call(f32[128,128]{1,0:T(8,128)S(1)} %bitcast.16, f32[3,27,8,128]{3,2,1,0:T(8,128)S(1)} %get-tuple-element.68.r_ref, f32[3,27,8,128]{3,2,1,0:T(8,128)S(1)} %get-tuple-element.69.v_ref, f32[3,27,8,128]{3,2,1,0:T(8,128)S(1)} %get-tuple-element.71.w_ref, ...), custom_call_target="tpu_custom_call" | custom-call | flops 1024000 | bytes 2719744 | tf_op jit(solution)/shard_map/final/pallas_call | solution.py:741
  (3 shorter events, 0.1 us)
Async XLA Ops:
  0.6 12.8 %copy-start.2 = (f32[3,3,24,384]{3,2,1,0:T(8,128)S(1)}, f32[3,3,24,384]{3,2,1,0:T(8,128)}, u32[]{:S(2)}) copy-start(f32[3,3,24,384]{3,2,1,0:T(8,128)} %vel_ref.1) | copy-start | bytes 995332
  0.6 12.8 %copy-start.1 = (f32[3,3,24,384]{3,2,1,0:T(8,128)S(1)}, f32[3,3,24,384]{3,2,1,0:T(8,128)}, u32[]{:S(2)}) copy-start(f32[3,3,24,384]{3,2,1,0:T(8,128)} %d_ref.5) | copy-start | bytes 995332
  0.7 12.8 %copy-start.4 = (f32[27,1,8,128]{3,2,1,0:T(8,128)S(1)}, f32[27,1,8,128]{3,2,1,0:T(8,128)}, u32[]{:S(2)}) copy-start(f32[27,1,8,128]{3,2,1,0:T(8,128)} %param.7) | copy-start | bytes 331780
  0.7 14.0 %copy-start = (f32[216,1,8,128]{3,2,1,0:T(8,128)S(1)}, f32[216,1,8,128]{3,2,1,0:T(8,128)}, u32[]{:S(2)}) copy-start(f32[216,1,8,128]{3,2,1,0:T(8,128)} %param.8) | copy-start | bytes 2654212
  2.8 11.9 %collective-permute-start = (f32[9,24,384]{2,1,0:T(8,128)}, f32[9,24,384]{2,1,0:T(8,128)S(1)}, u32[]{:S(2)}, u32[]{:S(2)}) collective-permute-start(f32[9,24,384]{2,1,0:T(8,128)} %get-tuple-element.41), channel_id=1, source_target_pairs={{0,112},{1,113},{2,114},{3,115},{4,116},{5,117},{6,118},{7,119},{8... | collective-permute-start | bytes 995336 | tf_op jit(solution)/shard_map/ppermute | solution.py:768
  4.2 10.5 %collective-permute-start.1 = (f32[27,384]{1,0:T(8,128)}, f32[27,384]{1,0:T(8,128)S(1)}, u32[]{:S(2)}, u32[]{:S(2)}) collective-permute-start(f32[27,384]{1,0:T(8,128)} %get-tuple-element.42), channel_id=1, source_target_pairs={{0,15},{1,0},{2,1},{3,2},{4,3},{5,4},{6,5},{7,6},{8,7},{9,8},{10,9... | collective-permute-start | bytes 124424 | tf_op jit(solution)/shard_map/ppermute | solution.py:768
  9.2 5.4 %collective-permute-start.2 = (f32[9,384]{1,0:T(8,128)}, f32[9,384]{1,0:T(8,128)S(1)}, u32[]{:S(2)}, u32[]{:S(2)}) collective-permute-start(f32[9,384]{1,0:T(8,128)} %get-tuple-element.43), channel_id=1, source_target_pairs={{0,127},{1,112},{2,113},{3,114},{4,115},{5,116},{6,117},{7,118},{8... | collective-permute-start | bytes 41480 | tf_op jit(solution)/shard_map/ppermute | solution.py:768
  14.7 13.8 %copy-start.3 = (s32[3,3,24,384]{3,2,1,0:T(8,128)S(1)}, s32[3,3,24,384]{3,2,1,0:T(8,128)}, u32[]{:S(2)}) copy-start(s32[3,3,24,384]{3,2,1,0:T(8,128)} %f_ref.3) | copy-start | bytes 995332
  26.6 4.3 %collective-permute-start.4 = (f32[232,128]{1,0:T(8,128)S(1)}, f32[232,128]{1,0:T(8,128)S(1)}, u32[]{:S(2)}, u32[]{:S(2)}) collective-permute-start(f32[232,128]{1,0:T(8,128)S(1)} %get-tuple-element.45.minus_ref), channel_id=1, source_target_pairs={{0,112},{1,113},{2,114},{3,115},{4,116},{5,117},{6,118},{7,119},{8... | collective-permute-start | bytes 356360 | tf_op jit(solution)/shard_map/ppermute | solution.py:768
  28.4 3.3 %collective-permute-start.3 = (f32[232,128]{1,0:T(8,128)S(1)}, f32[232,128]{1,0:T(8,128)S(1)}, u32[]{:S(2)}, u32[]{:S(2)}) collective-permute-start(f32[232,128]{1,0:T(8,128)S(1)} %get-tuple-element.46.plus_ref), channel_id=1, source_target_pairs={{0,16},{1,17},{2,18},{3,19},{4,20},{5,21},{6,22},{7,23},{8,24},{9,... | collective-permute-start | bytes 356360 | tf_op jit(solution)/shard_map/ppermute | solution.py:768
  31.8 6.0 %collective-permute-start.5 = (f32[40,128]{1,0:T(8,128)S(1)}, f32[40,128]{1,0:T(8,128)S(1)}, u32[]{:S(2)}, u32[]{:S(2)}) collective-permute-start(f32[40,128]{1,0:T(8,128)S(1)} %get-tuple-element.51), channel_id=1, source_target_pairs={{0,1},{1,2},{2,3},{3,4},{4,5},{5,6},{6,7},{7,8},{8,9},{9,10},{10,1... | collective-permute-start | bytes 61448 | tf_op jit(solution)/shard_map/ppermute | solution.py:768
  31.9 5.9 %collective-permute-start.6 = (f32[40,128]{1,0:T(8,128)S(1)}, f32[40,128]{1,0:T(8,128)S(1)}, u32[]{:S(2)}, u32[]{:S(2)}) collective-permute-start(f32[40,128]{1,0:T(8,128)S(1)} %get-tuple-element.52), channel_id=1, source_target_pairs={{0,15},{1,0},{2,1},{3,2},{4,3},{5,4},{6,5},{7,6},{8,7},{9,8},{10,9... | collective-permute-start | bytes 61448 | tf_op jit(solution)/shard_map/ppermute | solution.py:768
  39.9 6.8 %collective-permute-start.8 = (f32[232,128]{1,0:T(8,128)S(1)}, f32[232,128]{1,0:T(8,128)S(1)}, u32[]{:S(2)}, u32[]{:S(2)}) collective-permute-start(f32[232,128]{1,0:T(8,128)S(1)} %get-tuple-element.56.minus_ref), channel_id=1, source_target_pairs={{0,112},{1,113},{2,114},{3,115},{4,116},{5,117},{6,118},{7,119},{8... | collective-permute-start | bytes 356360 | tf_op jit(solution)/shard_map/ppermute | solution.py:768
  45.7 1.8 %collective-permute-start.7 = (f32[232,128]{1,0:T(8,128)S(1)}, f32[232,128]{1,0:T(8,128)S(1)}, u32[]{:S(2)}, u32[]{:S(2)}) collective-permute-start(f32[232,128]{1,0:T(8,128)S(1)} %get-tuple-element.57.plus_ref), channel_id=1, source_target_pairs={{0,16},{1,17},{2,18},{3,19},{4,20},{5,21},{6,22},{7,23},{8,24},{9,... | collective-permute-start | bytes 356360 | tf_op jit(solution)/shard_map/ppermute | solution.py:768
  47.6 6.3 %collective-permute-start.9 = (f32[40,128]{1,0:T(8,128)S(1)}, f32[40,128]{1,0:T(8,128)S(1)}, u32[]{:S(2)}, u32[]{:S(2)}) collective-permute-start(f32[40,128]{1,0:T(8,128)S(1)} %get-tuple-element.60), channel_id=1, source_target_pairs={{0,1},{1,2},{2,3},{3,4},{4,5},{5,6},{6,7},{7,8},{8,9},{9,10},{10,1... | collective-permute-start | bytes 61448 | tf_op jit(solution)/shard_map/ppermute | solution.py:768
  47.7 6.2 %collective-permute-start.10 = (f32[40,128]{1,0:T(8,128)S(1)}, f32[40,128]{1,0:T(8,128)S(1)}, u32[]{:S(2)}, u32[]{:S(2)}) collective-permute-start(f32[40,128]{1,0:T(8,128)S(1)} %get-tuple-element.61), channel_id=1, source_target_pairs={{0,15},{1,0},{2,1},{3,2},{4,3},{5,4},{6,5},{7,6},{8,7},{9,8},{10,9... | collective-permute-start | bytes 61448 | tf_op jit(solution)/shard_map/ppermute | solution.py:768
  56.0 5.8 %collective-permute-start.12 = (f32[232,128]{1,0:T(8,128)S(1)}, f32[232,128]{1,0:T(8,128)S(1)}, u32[]{:S(2)}, u32[]{:S(2)}) collective-permute-start(f32[232,128]{1,0:T(8,128)S(1)} %get-tuple-element.62.minus_ref), channel_id=1, source_target_pairs={{0,112},{1,113},{2,114},{3,115},{4,116},{5,117},{6,118},{7,119},{8... | collective-permute-start | bytes 356360 | tf_op jit(solution)/shard_map/ppermute | solution.py:768
  60.6 1.8 %collective-permute-start.11 = (f32[232,128]{1,0:T(8,128)S(1)}, f32[232,128]{1,0:T(8,128)S(1)}, u32[]{:S(2)}, u32[]{:S(2)}) collective-permute-start(f32[232,128]{1,0:T(8,128)S(1)} %get-tuple-element.63.plus_ref), channel_id=1, source_target_pairs={{0,16},{1,17},{2,18},{3,19},{4,20},{5,21},{6,22},{7,23},{8,24},{9,... | collective-permute-start | bytes 356360 | tf_op jit(solution)/shard_map/ppermute | solution.py:768
  62.4 6.4 %collective-permute-start.13 = (f32[40,128]{1,0:T(8,128)S(1)}, f32[40,128]{1,0:T(8,128)S(1)}, u32[]{:S(2)}, u32[]{:S(2)}) collective-permute-start(f32[40,128]{1,0:T(8,128)S(1)} %get-tuple-element.66), channel_id=1, source_target_pairs={{0,1},{1,2},{2,3},{3,4},{4,5},{5,6},{6,7},{7,8},{8,9},{9,10},{10,1... | collective-permute-start | bytes 61448 | tf_op jit(solution)/shard_map/ppermute | solution.py:768
  62.5 6.3 %collective-permute-start.14 = (f32[40,128]{1,0:T(8,128)S(1)}, f32[40,128]{1,0:T(8,128)S(1)}, u32[]{:S(2)}, u32[]{:S(2)}) collective-permute-start(f32[40,128]{1,0:T(8,128)S(1)} %get-tuple-element.67), channel_id=1, source_target_pairs={{0,15},{1,0},{2,1},{3,2},{4,3},{5,4},{6,5},{7,6},{8,7},{9,8},{10,9... | collective-permute-start | bytes 61448 | tf_op jit(solution)/shard_map/ppermute | solution.py:768
